TPU v7x, 32 devices: a whole 2x2x4 slice. The times are simulated.
32 devices in a mesh: parts: 2 (over x), gx: 16 (over z, y, core).
Axes of the slice: x: 2, y: 2, z: 4, core: 2. Of those that a mesh axis runs over, the one named last changes fastest.
Arguments:
- right_side: float32 [512, 32, 128], P(('parts', 'gx')), parts along dimension 0, may hold values from -9 to 9
- wet_quarters: int32 [512, 32, 128], P(('parts', 'gx')), parts along dimension 0, may hold values from 0 to 4, as said below
- trans_x: bfloat16 [512, 32, 128], P(('parts', 'gx')), parts along dimension 0, may hold values from 0.049804688 to 1
- trans_y: bfloat16 [512, 32, 128], P(('parts', 'gx')), parts along dimension 0, may hold values from 0.049804688 to 1
- trans_z: bfloat16 [512, 32, 128], P(('parts', 'gx')), parts along dimension 0, may hold values from 0.049804688 to 1
- storage: bfloat16 [512, 32, 128], P(('parts', 'gx')), parts along dimension 0, may hold values from 0.099609375 to 2
- basis: bfloat16 [8, 512, 32, 128], P(None, ('parts', 'gx')), parts along dimension 1, may hold values from 0 to 0.25
- coupling: float32 [6, 8, 8, 512], P(None, None, None, ('parts', 'gx')), parts along dimension 3, may hold values from -2.4 to 2.4
- coarse_inverse: float32 [8, 8, 512], P(None, None, 'parts'), parts along dimension 2, may hold values from -0.1 to 0.45
- owned_block: int32 [256], replicated, may hold values from 0 to 255, as said below
- block_slot: int32 [256], P('gx'), may hold values from 0 to 255, as said below
- neighbours: int32 [6, 256], P(None, 'gx'), may hold values from -1 to 255, as said below
Outputs:
- pressure: float32 [512, 32, 128], P(('parts', 'gx')), parts along dimension 0
- residual: float32 [512, 32, 128], P(('parts', 'gx')), parts along dimension 0
There are 2 independent parts, one for each index of `parts`. A program takes and returns all parts, laid end to end along the dimension named above; an argument that names none is the same for every part. Nothing has to cross between parts.
Inputs may be any that keep to these rules, and one draw needn't show every extreme that they name: `wet_quarters`: in every column of 128 cells the cells below a water table hold 4, the cell at the table 1 to 3, the cells above it 0. `owned_block`: A permutation of the 256 block numbers. `block_slot`: the inverse permutation of owned_block. `neighbours`: entry [k, s] is the slot of the block sharing the k-th face (order +x, -x, +y, -y, +z, -z) with the block in slot s, or -1 where that block lies outside the grid.
All inputs are finite; a program needn't handle non-finite values.
Results may differ from a plain program's by a relative error of at most 0.0003.
Values may be sent and summed in bfloat16 or wider, within the bound.
No kernel may reach another device: no remote copies, remote signals or barrier semaphores. Data moves between devices by JAX's collectives and lax.ppermute only.
A program may use at most 64 MiB of HBM per device.

v0:
```python
import jax
import jax.numpy as jnp
from jax import lax
from jax.sharding import PartitionSpec as P

BLK = 16
NBF = 8
ITERS = 2
SWEEPS = 3
CSWEEPS = 4
NYB = 2
NZB = 8


relaxation = 2.0 / 3.0


def extended(block, sides, width):
    for axis, dim in sides:
        count = lax.axis_size(axis)
        forward = [(i, i + 1) for i in range(count - 1)]
        backward = [(target, source) for source, target in forward]
        low = lax.ppermute(
            lax.slice_in_dim(block, block.shape[dim] - width, None, axis=dim), axis, forward
        )
        high = lax.ppermute(lax.slice_in_dim(block, 0, width, axis=dim), axis, backward)
        block = jnp.concatenate([low, block, high], axis=dim)
    return block


def passed_along(value, axis, steps):
    count = lax.axis_size(axis)
    leading, last = (max(0, -steps), min(count, count - steps))
    return lax.ppermute(value, axis, [(source, source + steps) for source in range(leading, last)])


def lower_shift(values, axis_number):
    pieces = [(0, 0), (0, 0), (0, 0)]
    pieces[axis_number] = (1, 0)
    padded = jnp.pad(values, pieces)
    return lax.slice_in_dim(padded, 0, values.shape[axis_number], axis=axis_number)


def upper_lower(state_field, axis_number):
    pieces = [(0, 0), (0, 0), (0, 0)]
    pieces[axis_number] = (1, 1)
    padded = jnp.pad(state_field, pieces)
    length = state_field.shape[axis_number]
    upper_side = lax.slice_in_dim(padded, 2, length + 2, axis=axis_number)
    lower_side = lax.slice_in_dim(padded, 0, length, axis=axis_number)
    return (upper_side, lower_side)


def operate(state_field, faces, wet_share, dry_cell, storage_f):
    east_face, west_face, north_face, south_face, upper_face, lower_face = faces
    padded = extended(state_field, (("gx", 0),), 1)
    east_cell = padded[2:]
    west_cell = padded[:-2]
    north_cell, south_cell = upper_lower(state_field, 1)
    top_cell, bottom_cell = upper_lower(state_field, 2)
    face_flux = east_face * (state_field - east_cell) + west_face * (state_field - west_cell)
    face_flux = (
        face_flux
        + north_face * (state_field - north_cell)
        + south_face * (state_field - south_cell)
    )
    face_flux = (
        face_flux + upper_face * (state_field - top_cell) + lower_face * (state_field - bottom_cell)
    )
    return wet_share * (storage_f * state_field + face_flux) + dry_cell * state_field


def restrict(misfit, basis):
    slab_blocks = basis.shape[1] // BLK
    weighted = basis.astype(jnp.float32) * misfit[None]
    summed = weighted.reshape(NBF, slab_blocks, BLK, NYB, BLK, NZB, BLK).sum(axis=(2, 4, 6))
    return summed.reshape(NBF, slab_blocks * NYB * NZB)


def prolong(coarse_slab, basis):
    slab_blocks = basis.shape[1] // BLK
    correction = jnp.zeros(basis.shape[1:], jnp.float32)
    for basis_index in range(NBF):
        block_grid = coarse_slab[basis_index].reshape(slab_blocks, 1, NYB, 1, NZB, 1)
        spread_out = jnp.broadcast_to(block_grid, (slab_blocks, BLK, NYB, BLK, NZB, BLK)).reshape(
            basis.shape[1:]
        )
        correction = correction + basis[basis_index].astype(jnp.float32) * spread_out
    return correction


def spread_values(values):
    return lax.all_gather(values, "gx", axis=1, tiled=True)


def coarse_solve(coarse_local, coupling, coarse_inverse, owned_block, block_slot, neighbours):
    exact_mode = lax.Precision.HIGHEST
    gathered_residual = lax.all_gather(coarse_local, "gx", axis=1, tiled=True)
    present = (neighbours >= 0).astype(jnp.float32)
    safe_index = jnp.maximum(neighbours, 0)
    per_device = coarse_local.shape[1]
    my_slots = lax.axis_index("gx") * per_device + jnp.arange(per_device, dtype=jnp.int32)
    my_blocks = owned_block[my_slots]
    own_residual = gathered_residual[:, my_blocks]
    own_inverse = coarse_inverse[:, :, my_blocks]
    values = jnp.einsum("ijb,jb->ib", own_inverse, own_residual, precision=exact_mode)
    for sweep_index in range(CSWEEPS - 1):
        nearby = spread_values(values)[:, safe_index] * present[None]
        coupled = jnp.einsum("kijb,jkb->ib", coupling, nearby, precision=exact_mode)
        values = jnp.einsum("ijb,jb->ib", own_inverse, own_residual - coupled, precision=exact_mode)
    return spread_values(values)[:, block_slot]


def local(
    right_side,
    wet_quarters,
    trans_x,
    trans_y,
    trans_z,
    storage,
    basis,
    coupling,
    coarse_inverse,
    owned_block,
    block_slot,
    neighbours,
):
    wet_share = wet_quarters.astype(jnp.float32) * 0.25
    dry_cell = 1.0 - jnp.minimum(wet_quarters, 1).astype(jnp.float32)
    east_face = trans_x.astype(jnp.float32)
    before = passed_along(trans_x[-1:], "gx", 1)
    west_face = jnp.concatenate([before, trans_x[:-1]], 0).astype(jnp.float32)
    north_face = trans_y.astype(jnp.float32)
    south_face = lower_shift(north_face, 1)
    upper_face = trans_z.astype(jnp.float32)
    lower_face = lower_shift(upper_face, 2)
    storage_f = storage.astype(jnp.float32)
    faces = (east_face, west_face, north_face, south_face, upper_face, lower_face)
    diagonal_coef = (
        wet_share
        * (storage_f + east_face + west_face + north_face + south_face + upper_face + lower_face)
        + dry_cell
    )
    pressure = jnp.zeros_like(right_side)
    for outer_step in range(ITERS):
        if outer_step == 0:
            misfit = right_side
        else:
            misfit = right_side - operate(pressure, faces, wet_share, dry_cell, storage_f)
        coarse_values = coarse_solve(
            restrict(misfit, basis), coupling, coarse_inverse, owned_block, block_slot, neighbours
        )
        pressure = pressure + prolong(coarse_values, basis)
        for sweep_index in range(SWEEPS):
            pressure = (
                pressure
                + relaxation
                * (right_side - operate(pressure, faces, wet_share, dry_cell, storage_f))
                / diagonal_coef
            )
    residual = right_side - operate(pressure, faces, wet_share, dry_cell, storage_f)
    return (pressure, residual)


def solution(mesh):
    placed = (
        P(("parts", "gx"), None, None),
        P(("parts", "gx"), None, None),
        P(("parts", "gx"), None, None),
        P(("parts", "gx"), None, None),
        P(("parts", "gx"), None, None),
        P(("parts", "gx"), None, None),
        P(None, ("parts", "gx"), None, None),
        P(None, None, None, ("parts", "gx")),
        P(None, None, "parts"),
        P(),
        P("gx"),
        P(None, "gx"),
    )
    return jax.shard_map(
        local,
        mesh=mesh,
        in_specs=placed,
        out_specs=(P(("parts", "gx"), None, None), P(("parts", "gx"), None, None)),
        check_vma=False,
    )
```

profile of v0, /device:TPU:10, one launch (start us, length us, event | category | flops | bytes accessed | tf_op | source)
XLA Modules:
  0.0 300.6 jit_solution(5393286767969416938)
XLA Ops:
  6.8 19.0 %all-gather = f32[16,16,8]{1,2,0:T(8,128)S(1)} all-gather(f32[1,16,8]{1,2,0:T(8,128)S(1)} %bitcast.281), channel_id=1, replica_groups=mesh['parts'=2,'gx'=16] {'gx'}, dimensions={0}, use_global_device_ids=true | all-gather | bytes 8704 | tf_op jit(solution)/shard_map/all_gather | solution.py:98
  27.8 17.6 %all-gather.1 = f32[16,16,8]{1,2,0:T(8,128)S(1)} all-gather(f32[1,16,8]{1,2,0:T(8,128)S(1)} %bitcast.282), channel_id=1, replica_groups=mesh['parts'=2,'gx'=16] {'gx'}, dimensions={0}, use_global_device_ids=true | all-gather | bytes 8704 | tf_op jit(solution)/shard_map/all_gather | solution.py:93
  47.2 18.9 %all-gather.2 = f32[16,16,8]{1,2,0:T(8,128)S(1)} all-gather(f32[1,16,8]{1,2,0:T(8,128)S(1)} %bitcast.283), channel_id=1, replica_groups=mesh['parts'=2,'gx'=16] {'gx'}, dimensions={0}, use_global_device_ids=true | all-gather | bytes 8704 | tf_op jit(solution)/shard_map/all_gather | solution.py:93
  68.0 17.6 %all-gather.3 = f32[16,16,8]{1,2,0:T(8,128)S(1)} all-gather(f32[1,16,8]{1,2,0:T(8,128)S(1)} %bitcast.284), channel_id=1, replica_groups=mesh['parts'=2,'gx'=16] {'gx'}, dimensions={0}, use_global_device_ids=true | all-gather | bytes 8704 | tf_op jit(solution)/shard_map/all_gather | solution.py:93
  87.4 18.9 %all-gather.4 = f32[16,16,8]{1,2,0:T(8,128)S(1)} all-gather(f32[1,16,8]{1,2,0:T(8,128)S(1)} %bitcast.285), channel_id=1, replica_groups=mesh['parts'=2,'gx'=16] {'gx'}, dimensions={0}, use_global_device_ids=true | all-gather | bytes 8704 | tf_op jit(solution)/shard_map/all_gather | solution.py:93
  109.7 4.9 %collective-permute-start = (f32[1,32,128]{2,1,0:T(8,128)S(1)}, f32[1,32,128]{2,1,0:T(8,128)S(1)}, u32[]{:S(2)}, u32[]{:S(2)}) collective-permute-start(f32[1,32,128]{2,1,0:T(8,128)S(1)} %get-tuple-element.32), channel_id=1, source_target_pairs={{1,0},{2,1},{3,2},{4,3},{5,4},{6,5},{7,6},{8,7},{9,8},{10,9},{11,1... | collective-permute-start | bytes 49160 | tf_op jit(solution)/shard_map/ppermute | solution.py:26
  118.6 3.8 %collective-permute-done.1 = bf16[1,32,128]{2,1,0:T(8,128)(2,1)S(1)} collective-permute-done((bf16[1,32,128]{2,1,0:T(8,128)(2,1)S(1)}, bf16[1,32,128]{2,1,0:T(8,128)(2,1)S(1)}, u32[]{:S(2)}, u32[]{:S(2)}) %collective-permute-start.1) | collective-permute-done | bytes 8224 | tf_op jit(solution)/shard_map/ppermute | solution.py:34
  125.0 2.4 collective-permute-start.4
  127.4 3.5 %collective-permute-done.4 = f32[1,32,128]{2,1,0:T(8,128)S(1)} collective-permute-done((f32[1,32,128]{2,1,0:T(8,128)S(1)}, f32[1,32,128]{2,1,0:T(8,128)S(1)}, u32[]{:S(2)}, u32[]{:S(2)}) %collective-permute-start.4) | collective-permute-done | bytes 16416 | tf_op jit(solution)/shard_map/ppermute | solution.py:23
  133.4 2.4 collective-permute-start.6
  135.9 3.5 %collective-permute-done.6 = f32[1,32,128]{2,1,0:T(8,128)S(1)} collective-permute-done((f32[1,32,128]{2,1,0:T(8,128)S(1)}, f32[1,32,128]{2,1,0:T(8,128)S(1)}, u32[]{:S(2)}, u32[]{:S(2)}) %collective-permute-start.6) | collective-permute-done | bytes 16416 | tf_op jit(solution)/shard_map/ppermute | solution.py:23
  144.3 3.5 %collective-permute-done.8 = f32[1,32,128]{2,1,0:T(8,128)S(1)} collective-permute-done((f32[1,32,128]{2,1,0:T(8,128)S(1)}, f32[1,32,128]{2,1,0:T(8,128)S(1)}, u32[]{:S(2)}, u32[]{:S(2)}) %collective-permute-start.8) | collective-permute-done | bytes 16416 | tf_op jit(solution)/shard_map/ppermute | solution.py:23
  152.8 13.7 %all-gather.5 = f32[16,16,8]{1,2,0:T(8,128)S(1)} all-gather(f32[1,16,8]{1,2,0:T(8,128)S(1)} %bitcast.286), channel_id=1, replica_groups=mesh['parts'=2,'gx'=16] {'gx'}, dimensions={0}, use_global_device_ids=true | all-gather | bytes 8704 | tf_op jit(solution)/shard_map/all_gather | solution.py:98
  169.4 18.3 %all-gather.6 = f32[16,16,8]{1,2,0:T(8,128)S(1)} all-gather(f32[1,16,8]{1,2,0:T(8,128)S(1)} %bitcast.287), channel_id=1, replica_groups=mesh['parts'=2,'gx'=16] {'gx'}, dimensions={0}, use_global_device_ids=true | all-gather | bytes 8704 | tf_op jit(solution)/shard_map/all_gather | solution.py:93
  193.3 17.8 %all-gather.7 = f32[16,16,8]{1,2,0:T(8,128)S(1)} all-gather(f32[1,16,8]{1,2,0:T(8,128)S(1)} %bitcast.288), channel_id=1, replica_groups=mesh['parts'=2,'gx'=16] {'gx'}, dimensions={0}, use_global_device_ids=true | all-gather | bytes 8704 | tf_op jit(solution)/shard_map/all_gather | solution.py:93
  216.5 18.9 %all-gather.8 = f32[16,16,8]{1,2,0:T(8,128)S(1)} all-gather(f32[1,16,8]{1,2,0:T(8,128)S(1)} %bitcast.289), channel_id=1, replica_groups=mesh['parts'=2,'gx'=16] {'gx'}, dimensions={0}, use_global_device_ids=true | all-gather | bytes 8704 | tf_op jit(solution)/shard_map/all_gather | solution.py:93
  240.9 17.6 %all-gather.9 = f32[16,16,8]{1,2,0:T(8,128)S(1)} all-gather(f32[1,16,8]{1,2,0:T(8,128)S(1)} %bitcast.290), channel_id=1, replica_groups=mesh['parts'=2,'gx'=16] {'gx'}, dimensions={0}, use_global_device_ids=true | all-gather | bytes 8704 | tf_op jit(solution)/shard_map/all_gather | solution.py:93
  262.0 6.2 %collective-permute-start.9 = (f32[1,32,128]{2,1,0:T(8,128)S(1)}, f32[1,32,128]{2,1,0:T(8,128)S(1)}, u32[]{:S(2)}, u32[]{:S(2)}) collective-permute-start(f32[1,32,128]{2,1,0:T(8,128)S(1)} %get-tuple-element.24), channel_id=1, source_target_pairs={{1,0},{2,1},{3,2},{4,3},{5,4},{6,5},{7,6},{8,7},{9,8},{10,9},{11,1... | collective-permute-start | bytes 49160 | tf_op jit(solution)/shard_map/ppermute | solution.py:26
  270.1 4.0 %collective-permute-done.10 = f32[1,32,128]{2,1,0:T(8,128)S(1)} collective-permute-done((f32[1,32,128]{2,1,0:T(8,128)S(1)}, f32[1,32,128]{2,1,0:T(8,128)S(1)}, u32[]{:S(2)}, u32[]{:S(2)}) %collective-permute-start.10) | collective-permute-done | bytes 16416 | tf_op jit(solution)/shard_map/ppermute | solution.py:23
  279.1 3.5 %collective-permute-done.12 = f32[1,32,128]{2,1,0:T(8,128)S(1)} collective-permute-done((f32[1,32,128]{2,1,0:T(8,128)S(1)}, f32[1,32,128]{2,1,0:T(8,128)S(1)}, u32[]{:S(2)}, u32[]{:S(2)}) %collective-permute-start.12) | collective-permute-done | bytes 16416 | tf_op jit(solution)/shard_map/ppermute | solution.py:23
  285.1 2.4 collective-permute-start.14
  287.5 3.5 %collective-permute-done.14 = f32[1,32,128]{2,1,0:T(8,128)S(1)} collective-permute-done((f32[1,32,128]{2,1,0:T(8,128)S(1)}, f32[1,32,128]{2,1,0:T(8,128)S(1)}, u32[]{:S(2)}, u32[]{:S(2)}) %collective-permute-start.14) | collective-permute-done | bytes 16416 | tf_op jit(solution)/shard_map/ppermute | solution.py:23
  293.6 2.4 collective-permute-start.16
  296.0 3.5 %collective-permute-done.16 = f32[1,32,128]{2,1,0:T(8,128)S(1)} collective-permute-done((f32[1,32,128]{2,1,0:T(8,128)S(1)}, f32[1,32,128]{2,1,0:T(8,128)S(1)}, u32[]{:S(2)}, u32[]{:S(2)}) %collective-permute-start.16) | collective-permute-done | bytes 16416 | tf_op jit(solution)/shard_map/ppermute | solution.py:23
  (194 shorter events, 71.0 us)
Async XLA Ops:
  2.8 103.7 %copy-start.12 = (s32[1024]{0:T(1024)}, s32[1024]{0:T(1024)S(1)}, u32[]{:S(2)}) copy-start(s32[1024]{0:T(1024)S(1)} %pad_clamp_fusion) | copy-start | bytes 12292
  3.5 23.4 %copy-start.11 = (s32[1024]{0:T(1024)}, s32[1024]{0:T(1024)S(1)}, u32[]{:S(2)}) copy-start(s32[1024]{0:T(1024)S(1)} %pad_clamp_fusion.2) | copy-start | bytes 12292
  6.2 19.7 %copy-start.10 = (f32[8,8,256]{2,1,0:T(8,128)S(1)}, f32[8,8,256]{2,1,0:T(8,128)}, u32[]{:S(2)}) copy-start(f32[8,8,256]{2,1,0:T(8,128)} %param.20) | copy-start | bytes 196612
  109.2 9.3 %copy-start.4 = (bf16[16,32,128]{2,1,0:T(8,128)(2,1)S(1)}, bf16[16,32,128]{2,1,0:T(8,128)(2,1)}, u32[]{:S(2)}) copy-start(bf16[16,32,128]{2,1,0:T(8,128)(2,1)} %param.15) | copy-start | bytes 393220
  109.4 9.1 %copy-start.5 = (bf16[16,32,128]{2,1,0:T(8,128)(2,1)S(1)}, bf16[16,32,128]{2,1,0:T(8,128)(2,1)}, u32[]{:S(2)}) copy-start(bf16[16,32,128]{2,1,0:T(8,128)(2,1)} %param.16) | copy-start | bytes 393220
  109.5 13.0 %copy-start.2 = (s32[16,32,128]{2,1,0:T(8,128)S(1)}, s32[16,32,128]{2,1,0:T(8,128)}, u32[]{:S(2)}) copy-start(s32[16,32,128]{2,1,0:T(8,128)} %param.13) | copy-start | bytes 786436
  109.5 13.0 %copy-start.7 = (bf16[16,32,128]{2,1,0:T(8,128)(2,1)S(1)}, bf16[16,32,128]{2,1,0:T(8,128)(2,1)}, u32[]{:S(2)}) copy-start(bf16[16,32,128]{2,1,0:T(8,128)(2,1)} %param.17) | copy-start | bytes 393220
  109.7 12.7 %collective-permute-start = (f32[1,32,128]{2,1,0:T(8,128)S(1)}, f32[1,32,128]{2,1,0:T(8,128)S(1)}, u32[]{:S(2)}, u32[]{:S(2)}) collective-permute-start(f32[1,32,128]{2,1,0:T(8,128)S(1)} %get-tuple-element.32), channel_id=1, source_target_pairs={{1,0},{2,1},{3,2},{4,3},{5,4},{6,5},{7,6},{8,7},{9,8},{10,9},{11,1... | collective-permute-start | bytes 49160 | tf_op jit(solution)/shard_map/ppermute | solution.py:26
  114.6 7.8 %collective-permute-start.2 = (f32[1,32,128]{2,1,0:T(8,128)S(1)}, f32[1,32,128]{2,1,0:T(8,128)S(1)}, u32[]{:S(2)}, u32[]{:S(2)}) collective-permute-start(f32[1,32,128]{2,1,0:T(8,128)S(1)} %get-tuple-element.33), channel_id=1, source_target_pairs={{0,1},{1,2},{2,3},{3,4},{4,5},{5,6},{6,7},{7,8},{8,9},{9,10},{10,1... | collective-permute-start | bytes 49160 | tf_op jit(solution)/shard_map/ppermute | solution.py:23
  116.6 5.9 %collective-permute-start.1 = (bf16[1,32,128]{2,1,0:T(8,128)(2,1)S(1)}, bf16[1,32,128]{2,1,0:T(8,128)(2,1)S(1)}, u32[]{:S(2)}, u32[]{:S(2)}) collective-permute-start(bf16[1,32,128]{2,1,0:T(8,128)(2,1)S(1)} %slice.318), channel_id=1, source_target_pairs={{0,1},{1,2},{2,3},{3,4},{4,5},{5,6},{6,7},{7,8},{8,9},{9,10},{10,1... | collective-permute-start | bytes 24584 | tf_op jit(solution)/shard_map/ppermute | solution.py:34
  123.1 4.3 %collective-permute-start.3 = (f32[1,32,128]{2,1,0:T(8,128)S(1)}, f32[1,32,128]{2,1,0:T(8,128)S(1)}, u32[]{:S(2)}, u32[]{:S(2)}) collective-permute-start(f32[1,32,128]{2,1,0:T(8,128)S(1)} %get-tuple-element.30), channel_id=1, source_target_pairs={{1,0},{2,1},{3,2},{4,3},{5,4},{6,5},{7,6},{8,7},{9,8},{10,9},{11,1... | collective-permute-start | bytes 49160 | tf_op jit(solution)/shard_map/ppermute | solution.py:26
  125.0 6.0 %collective-permute-start.4 = (f32[1,32,128]{2,1,0:T(8,128)S(1)}, f32[1,32,128]{2,1,0:T(8,128)S(1)}, u32[]{:S(2)}, u32[]{:S(2)}) collective-permute-start(f32[1,32,128]{2,1,0:T(8,128)S(1)} %get-tuple-element.31), channel_id=1, source_target_pairs={{0,1},{1,2},{2,3},{3,4},{4,5},{5,6},{6,7},{7,8},{8,9},{9,10},{10,1... | collective-permute-start | bytes 49160 | tf_op jit(solution)/shard_map/ppermute | solution.py:23
  131.5 4.3 %collective-permute-start.5 = (f32[1,32,128]{2,1,0:T(8,128)S(1)}, f32[1,32,128]{2,1,0:T(8,128)S(1)}, u32[]{:S(2)}, u32[]{:S(2)}) collective-permute-start(f32[1,32,128]{2,1,0:T(8,128)S(1)} %get-tuple-element.28), channel_id=1, source_target_pairs={{1,0},{2,1},{3,2},{4,3},{5,4},{6,5},{7,6},{8,7},{9,8},{10,9},{11,1... | collective-permute-start | bytes 49160 | tf_op jit(solution)/shard_map/ppermute | solution.py:26
  133.4 6.0 %collective-permute-start.6 = (f32[1,32,128]{2,1,0:T(8,128)S(1)}, f32[1,32,128]{2,1,0:T(8,128)S(1)}, u32[]{:S(2)}, u32[]{:S(2)}) collective-permute-start(f32[1,32,128]{2,1,0:T(8,128)S(1)} %get-tuple-element.29), channel_id=1, source_target_pairs={{0,1},{1,2},{2,3},{3,4},{4,5},{5,6},{6,7},{7,8},{8,9},{9,10},{10,1... | collective-permute-start | bytes 49160 | tf_op jit(solution)/shard_map/ppermute | solution.py:23
  140.0 4.3 %collective-permute-start.7 = (f32[1,32,128]{2,1,0:T(8,128)S(1)}, f32[1,32,128]{2,1,0:T(8,128)S(1)}, u32[]{:S(2)}, u32[]{:S(2)}) collective-permute-start(f32[1,32,128]{2,1,0:T(8,128)S(1)} %get-tuple-element.26), channel_id=1, source_target_pairs={{1,0},{2,1},{3,2},{4,3},{5,4},{6,5},{7,6},{8,7},{9,8},{10,9},{11,1... | collective-permute-start | bytes 49160 | tf_op jit(solution)/shard_map/ppermute | solution.py:26
  141.9 6.0 %collective-permute-start.8 = (f32[1,32,128]{2,1,0:T(8,128)S(1)}, f32[1,32,128]{2,1,0:T(8,128)S(1)}, u32[]{:S(2)}, u32[]{:S(2)}) collective-permute-start(f32[1,32,128]{2,1,0:T(8,128)S(1)} %get-tuple-element.27), channel_id=1, source_target_pairs={{0,1},{1,2},{2,3},{3,4},{4,5},{5,6},{6,7},{7,8},{8,9},{9,10},{10,1... | collective-permute-start | bytes 49160 | tf_op jit(solution)/shard_map/ppermute | solution.py:23
  262.0 8.2 %collective-permute-start.9 = (f32[1,32,128]{2,1,0:T(8,128)S(1)}, f32[1,32,128]{2,1,0:T(8,128)S(1)}, u32[]{:S(2)}, u32[]{:S(2)}) collective-permute-start(f32[1,32,128]{2,1,0:T(8,128)S(1)} %get-tuple-element.24), channel_id=1, source_target_pairs={{1,0},{2,1},{3,2},{4,3},{5,4},{6,5},{7,6},{8,7},{9,8},{10,9},{11,1... | collective-permute-start | bytes 49160 | tf_op jit(solution)/shard_map/ppermute | solution.py:26
  268.2 6.0 %collective-permute-start.10 = (f32[1,32,128]{2,1,0:T(8,128)S(1)}, f32[1,32,128]{2,1,0:T(8,128)S(1)}, u32[]{:S(2)}, u32[]{:S(2)}) collective-permute-start(f32[1,32,128]{2,1,0:T(8,128)S(1)} %get-tuple-element.25), channel_id=1, source_target_pairs={{0,1},{1,2},{2,3},{3,4},{4,5},{5,6},{6,7},{7,8},{8,9},{9,10},{10,1... | collective-permute-start | bytes 49160 | tf_op jit(solution)/shard_map/ppermute | solution.py:23
  274.7 4.3 %collective-permute-start.11 = (f32[1,32,128]{2,1,0:T(8,128)S(1)}, f32[1,32,128]{2,1,0:T(8,128)S(1)}, u32[]{:S(2)}, u32[]{:S(2)}) collective-permute-start(f32[1,32,128]{2,1,0:T(8,128)S(1)} %get-tuple-element.22), channel_id=1, source_target_pairs={{1,0},{2,1},{3,2},{4,3},{5,4},{6,5},{7,6},{8,7},{9,8},{10,9},{11,1... | collective-permute-start | bytes 49160 | tf_op jit(solution)/shard_map/ppermute | solution.py:26
  276.7 6.0 %collective-permute-start.12 = (f32[1,32,128]{2,1,0:T(8,128)S(1)}, f32[1,32,128]{2,1,0:T(8,128)S(1)}, u32[]{:S(2)}, u32[]{:S(2)}) collective-permute-start(f32[1,32,128]{2,1,0:T(8,128)S(1)} %get-tuple-element.23), channel_id=1, source_target_pairs={{0,1},{1,2},{2,3},{3,4},{4,5},{5,6},{6,7},{7,8},{8,9},{9,10},{10,1... | collective-permute-start | bytes 49160 | tf_op jit(solution)/shard_map/ppermute | solution.py:23
  283.2 4.3 %collective-permute-start.13 = (f32[1,32,128]{2,1,0:T(8,128)S(1)}, f32[1,32,128]{2,1,0:T(8,128)S(1)}, u32[]{:S(2)}, u32[]{:S(2)}) collective-permute-start(f32[1,32,128]{2,1,0:T(8,128)S(1)} %get-tuple-element.20), channel_id=1, source_target_pairs={{1,0},{2,1},{3,2},{4,3},{5,4},{6,5},{7,6},{8,7},{9,8},{10,9},{11,1... | collective-permute-start | bytes 49160 | tf_op jit(solution)/shard_map/ppermute | solution.py:26
  285.1 6.0 %collective-permute-start.14 = (f32[1,32,128]{2,1,0:T(8,128)S(1)}, f32[1,32,128]{2,1,0:T(8,128)S(1)}, u32[]{:S(2)}, u32[]{:S(2)}) collective-permute-start(f32[1,32,128]{2,1,0:T(8,128)S(1)} %get-tuple-element.21), channel_id=1, source_target_pairs={{0,1},{1,2},{2,3},{3,4},{4,5},{5,6},{6,7},{7,8},{8,9},{9,10},{10,1... | collective-permute-start | bytes 49160 | tf_op jit(solution)/shard_map/ppermute | solution.py:23
  291.6 4.3 %collective-permute-start.15 = (f32[1,32,128]{2,1,0:T(8,128)S(1)}, f32[1,32,128]{2,1,0:T(8,128)S(1)}, u32[]{:S(2)}, u32[]{:S(2)}) collective-permute-start(f32[1,32,128]{2,1,0:T(8,128)S(1)} %get-tuple-element.18), channel_id=1, source_target_pairs={{1,0},{2,1},{3,2},{4,3},{5,4},{6,5},{7,6},{8,7},{9,8},{10,9},{11,1... | collective-permute-start | bytes 49160 | tf_op jit(solution)/shard_map/ppermute | solution.py:26
  293.6 6.0 %collective-permute-start.16 = (f32[1,32,128]{2,1,0:T(8,128)S(1)}, f32[1,32,128]{2,1,0:T(8,128)S(1)}, u32[]{:S(2)}, u32[]{:S(2)}) collective-permute-start(f32[1,32,128]{2,1,0:T(8,128)S(1)} %get-tuple-element.19), channel_id=1, source_target_pairs={{0,1},{1,2},{2,3},{3,4},{4,5},{5,6},{6,7},{7,8},{8,9},{9,10},{10,1... | collective-permute-start | bytes 49160 | tf_op jit(solution)/shard_map/ppermute | solution.py:23
  (6 other events, 24.8 us)
where the time goes:
time: 302 us; the launch traced here: 301 us
  blocking collectives  178 us (59%)
  starting transfers between devices  42.9 us (14%)
  waiting for transfers between devices  29.1 us (10%)
  local copies, waits for them, and re-layouts  26.3 us (9%)
  other arithmetic  16.3 us (5%)
  matrix products  6.26 us (2%)
    all_gather x8, blocking collectives, spread_values(): return lax.all_gather(values, 'gx', axis=1, tiled=True)  146 us
    all_gather x2, blocking collectives, coarse_solve(): gathered_residual = lax.all_gather(coarse_local, 'gx', axis=1, tiled=True)  32.7 us
    ppermute x8, waiting for transfers between devices, extended(): lax.ppermute(lax.slice_in_dim(block, block.shape[dim] - width, None, axis...  25.2 us
    ppermute x8, starting transfers between devices, extended(): lax.ppermute(lax.slice_in_dim(block, 0, width, axis=dim), axis, backward)  22.7 us
    ppermute x8, starting transfers between devices, extended(): lax.ppermute(lax.slice_in_dim(block, block.shape[dim] - width, None, axis...  18.3 us
    gather x6, local copies, waits for them, and re-layouts, coarse_solve(): nearby = spread_values(values)[:, safe_index] * present[None]  8.23 us
  transfers between devices with their start and end apart: 17, of which 8 were waited for; matrix products, arithmetic and copies ran while one was open for 0% of the time, Pallas kernels for 0%

commit v1 on v0

v1 whole, which is shorter than its diff:
```python
import functools

import jax
import jax.numpy as jnp
from jax import lax
from jax.experimental import pallas as pl
from jax.experimental.pallas import tpu as pltpu
from jax.sharding import PartitionSpec as P

BLK = 16
NBF = 8
NNB = 6
SWEEPS = 3
CSWEEPS = 4
NYB = 2
NZB = 8
PER = NYB * NZB
WIN = 16 * PER
LEAD = 4
HALO = 4
OMEGA = 2.0 / 3.0
KROWS = NNB * NBF * NBF
F32 = jnp.float32
BF16 = jnp.bfloat16

THIN = HALO - 1
H_TX = NBF * HALO
H_REST = H_TX + HALO
H_ALL = H_REST + 6 * THIN


def three_parts(x):
    high = x.astype(BF16)
    rest = x - high.astype(F32)
    middle = rest.astype(BF16)
    low = (rest - middle.astype(F32)).astype(BF16)
    return high, middle, low


def restrict_to(basis_at, field_at, planes):
    def step(x, totals):
        field = field_at(x)
        out = []
        for i in range(NBF):
            for yb in range(NYB):
                rows = slice(yb * BLK, (yb + 1) * BLK)
                product = basis_at(i, x)[rows].astype(F32) * field[rows]
                out.append(totals[i * NYB + yb] + product[:8] + product[8:])
        return tuple(out)

    zero = jnp.zeros((8, 128), F32)
    totals = lax.fori_loop(0, planes, step, (zero,) * (NBF * NYB))
    groups = lax.broadcasted_iota(jnp.int32, (NZB, 3 * 128), 1)
    owner = lax.broadcasted_iota(jnp.int32, (NZB, 3 * 128), 0)
    spread = ((groups % 128) // BLK == owner).astype(F32).astype(BF16)
    halves = []
    for yb in range(NYB):
        rows = [jnp.sum(totals[i * NYB + yb], axis=0, keepdims=True) for i in range(NBF)]
        stacked = jnp.concatenate(three_parts(jnp.concatenate(rows, 0)), axis=1)
        halves.append(
            lax.dot_general(
                spread, stacked, (((1,), (1,)), ((), ())), preferred_element_type=F32
            )
        )
    return jnp.concatenate(halves, 0)


def first_kernel(count, owned_ref, basis_ref, field_ref, coupling_ref, out_ref):
    me = lax.axis_index("gx")
    coarse = restrict_to(lambda i, x: basis_ref[i, x], lambda x: field_ref[x], basis_ref.shape[1])
    slot = lax.broadcasted_iota(jnp.int32, (PER, 1), 0)
    block = jnp.zeros((PER, 1), jnp.int32)
    for s in range(PER):
        block = jnp.where(slot == s, owned_ref[me * PER + s], block)
    tail = jnp.concatenate(
        [coarse, block.astype(F32), jnp.zeros((PER, 128 - NBF - 1), F32)], axis=1
    )
    wide = jnp.concatenate(
        [coupling_ref[...], jnp.zeros((KROWS, 128 - PER), F32)], axis=1
    )
    rows = jnp.concatenate([wide.T[:PER], tail], axis=1)

    def put(e, carry):
        out_ref[e] = rows
        return carry

    lax.fori_loop(0, count, put, 0)


def coarse_solve(coupling_at, inverse_at, residual):
    lane = lax.broadcasted_iota(jnp.int32, (NBF, WIN), 1)
    in_z, in_y = lane % NZB, (lane // NZB) % NYB

    def rows_of(parts):
        return jnp.concatenate([jnp.sum(p, axis=0, keepdims=True) for p in parts], 0)

    def inverted(v):
        return rows_of([inverse_at(i) * v for i in range(NBF)])

    values = inverted(residual)
    for _ in range(CSWEEPS - 1):
        near = (
            pltpu.roll(values, WIN - PER, 1),
            pltpu.roll(values, PER, 1),
            jnp.where(in_y < NYB - 1, pltpu.roll(values, WIN - NZB, 1), 0.0),
            jnp.where(in_y > 0, pltpu.roll(values, NZB, 1), 0.0),
            jnp.where(in_z < NZB - 1, pltpu.roll(values, WIN - 1, 1), 0.0),
            jnp.where(in_z > 0, pltpu.roll(values, 1, 1), 0.0),
        )
        parts = []
        for i in range(NBF):
            total = coupling_at(0, i) * near[0]
            for k in range(1, NNB):
                total = total + coupling_at(k, i) * near[k]
            parts.append(total)
        values = inverted(residual - rows_of(parts))
    return values


def spread_blocks(values):
    width = 3 * NYB * 128
    block = lax.broadcasted_iota(jnp.int32, (128, width), 0)
    column = lax.broadcasted_iota(jnp.int32, (128, width), 1)
    wanted = (LEAD - 1) * PER + column // BLK
    chosen = (block == wanted).astype(F32).astype(BF16)
    stacked = jnp.concatenate(three_parts(values[:, :128]), axis=0)
    spread = jnp.dot(stacked, chosen, preferred_element_type=F32)
    return spread[:NBF] + spread[NBF : 2 * NBF] + spread[2 * NBF :]


def iteration_kernel(last, count, *refs):
    (
        gathered_ref, inverse_ref, coupling_ref, basis_hbm, right_hbm, wet_hbm, tx_hbm, ty_hbm, tz_hbm, st_hbm,
        near_hbm, far_hbm,
    ) = refs[:12]
    refs = refs[12:]
    if last:
        (pressure_hbm, near_p_hbm, far_p_hbm, out_ref, residual_ref) = refs[:5]
        refs = refs[5:]
    else:
        (out_ref, send_near_ref, send_far_ref, packed_ref, coupling_out_ref) = refs[:5]
        refs = refs[5:]
    (
        basis_s, right_s, wet_s, tx_s, ty_s, tz_s, st_s, wet_h, high_h, low_h,
        coef_s, scaled_s, diag_s, one_s, two_s, window_s, coupling_s, sems,
    ) = refs
    planes = right_s.shape[0]
    me = lax.axis_index("gx")
    even = lax.rem(me, 2) == 0
    top = planes + HALO
    near_at, far_at = jnp.where(even, top, 0), jnp.where(even, 0, top)
    near_thin, far_thin = jnp.where(even, top, 1), jnp.where(even, 1, top)

    jobs = [
        (tx_hbm, tx_s.at[pl.ds(HALO, planes)]),
        (ty_hbm, ty_s.at[pl.ds(HALO, planes)]),
        (tz_hbm, tz_s.at[pl.ds(HALO, planes)]),
        (st_hbm, st_s.at[pl.ds(HALO, planes)]),
        (wet_hbm, wet_s),
        (right_hbm, right_s),
    ]
    for halo, wide_at, thin_at in ((near_hbm, near_at, near_thin), (far_hbm, far_at, far_thin)):
        jobs.append((halo.at[pl.ds(H_TX, HALO)], tx_s.at[pl.ds(wide_at, HALO)]))
        for k, into in enumerate((wet_h, ty_s, tz_s, st_s, high_h, low_h)):
            jobs.append((halo.at[pl.ds(H_REST + k * THIN, THIN)], into.at[pl.ds(thin_at, THIN)]))
    statics = len(jobs)
    jobs.append((basis_hbm, basis_s.at[:, pl.ds(HALO, planes)]))
    for halo, wide_at in ((near_hbm, near_at), (far_hbm, far_at)):
        for i in range(NBF):
            jobs.append((halo.at[pl.ds(i * HALO, HALO)], basis_s.at[i, pl.ds(wide_at, HALO)]))
    if last:
        jobs.append((pressure_hbm, one_s.at[pl.ds(HALO, planes)]))
        jobs.append((near_p_hbm, one_s.at[pl.ds(near_at, HALO)]))
        jobs.append((far_p_hbm, one_s.at[pl.ds(far_at, HALO)]))
    copies = [pltpu.make_async_copy(a, b, sems.at[k]) for k, (a, b) in enumerate(jobs)]
    for copy in copies:
        copy.start()

    tall = gathered_ref.shape[0] * PER
    window_s[...] = jnp.zeros_like(window_s)
    first = 0 if last else KROWS
    for e in range(count):
        window_s[pl.ds(LEAD * PER + e * PER, PER)] = gathered_ref[e, :, pl.ds(first, 128)]
    residual = window_s[pl.ds(pl.multiple_of(me * PER, PER), WIN)].T[:NBF]
    if not last:
        lane = lax.broadcasted_iota(jnp.int32, (WIN, WIN), 1) + (me - LEAD) * PER
        for part in range(tall // WIN):
            span = pl.ds(part * (WIN // PER), WIN // PER)
            rows = gathered_ref[span].reshape(WIN, KROWS + 128)
            block = rows[:, KROWS + NBF : KROWS + NBF + 1].astype(jnp.int32)
            chosen = (block == lane).astype(F32).astype(BF16)
            stacked = jnp.concatenate(three_parts(rows[:, :KROWS].T), axis=0)
            found = jnp.dot(stacked, chosen, preferred_element_type=F32)
            found = found[:KROWS] + found[KROWS : 2 * KROWS] + found[2 * KROWS :]
            coupling_s[...] = found if part == 0 else coupling_s[...] + found
        coupling_out_ref[...] = coupling_s[...]
        coupling_from = coupling_s
    else:
        coupling_from = coupling_ref
    values = coarse_solve(
        lambda k, i: coupling_from[pl.ds((k * NBF + i) * NBF, NBF)],
        lambda i: inverse_ref[pl.ds(i * NBF, NBF)],
        residual,
    )
    spread = spread_blocks(values)

    for copy in copies[:statics]:
        copy.wait()
    in_y = lax.broadcasted_iota(jnp.int32, (32, 128), 0)
    in_z = lax.broadcasted_iota(jnp.int32, (32, 128), 1)

    def coefficients(x, quarters, right, own):
        wet = quarters * 0.25
        dry = 1.0 - jnp.minimum(quarters, 1.0)
        east, west = tx_s[x].astype(F32), tx_s[x - 1].astype(F32)
        north, upper = ty_s[x].astype(F32), tz_s[x].astype(F32)
        south = jnp.where(in_y > 0, pltpu.roll(north, 1, 0), 0.0)
        lower = jnp.where(in_z > 0, pltpu.roll(upper, 1, 1), 0.0)
        total = st_s[x].astype(F32) + east + west + north + south + upper + lower
        diag = wet * total + dry
        share = OMEGA / diag
        scale = wet * share
        coef_s[x, 0] = scale * east
        coef_s[x, 1] = scale * west
        coef_s[x, 2] = jnp.where(in_y < 31, scale * north, 0.0)
        coef_s[x, 3] = scale * south
        coef_s[x, 4] = jnp.where(in_z < 127, scale * upper, 0.0)
        coef_s[x, 5] = scale * lower
        scaled_s[x] = right * share
        if own:
            diag_s[x - HALO] = diag * (1.0 / OMEGA)

    def own_plane(k, carry):
        coefficients(k + HALO, wet_s[k].astype(F32), right_s[k], True)
        return carry

    def halo_plane(k, carry):
        x = jnp.where(k < THIN, k + 1, k - THIN + top)
        coefficients(x, wet_h[x].astype(F32), high_h[x].astype(F32) + low_h[x].astype(F32), False)
        return carry

    lax.fori_loop(0, planes, own_plane, 0)
    lax.fori_loop(0, 2 * THIN, halo_plane, 0)

    for copy in copies[statics:]:
        copy.wait()

    def corrected(slab):
        start = slab * NYB * 128
        gains = [
            [jnp.broadcast_to(spread[i : i + 1, start + yb * 128 : start + (yb + 1) * 128], (BLK, 128)) for i in range(NBF)]
            for yb in range(NYB)
        ]

        def step(x, carry):
            for yb in range(NYB):
                rows = slice(yb * BLK, (yb + 1) * BLK)
                total = basis_s[0, x, rows].astype(F32) * gains[yb][0]
                for i in range(1, NBF):
                    total = total + basis_s[i, x, rows].astype(F32) * gains[yb][i]
                one_s[x, rows] = one_s[x, rows] + total if last else total
            return carry

        return step

    lax.fori_loop(0, HALO, corrected(0), 0)
    lax.fori_loop(HALO, top, corrected(1), 0)
    lax.fori_loop(top, top + HALO, corrected(2), 0)

    def pulled(state, x):
        here = state[x]
        total = scaled_s[x] + coef_s[x, 0] * state[x + 1] + coef_s[x, 1] * state[x - 1]
        total = total + coef_s[x, 2] * pltpu.roll(here, 31, 0) + coef_s[x, 3] * pltpu.roll(here, 1, 0)
        total = total + coef_s[x, 4] * pltpu.roll(here, 127, 1) + coef_s[x, 5] * pltpu.roll(here, 1, 1)
        return here, total

    def sweep(source, target):
        def step(x, carry):
            here, total = pulled(source, x)
            target[x] = (1.0 - OMEGA) * here + total
            return carry

        return step

    source, target = one_s, two_s
    for k in range(SWEEPS):
        lax.fori_loop(k + 1, top + HALO - 1 - k, sweep(source, target), 0)
        source, target = target, source

    def misfit(x, carry):
        here, total = pulled(source, x)
        value = (total - OMEGA * here) * diag_s[x - HALO]
        out_ref[x - HALO] = here
        if last:
            residual_ref[x - HALO] = value
        else:
            target[x] = value
        return carry

    lax.fori_loop(HALO, top, misfit, 0)
    if not last:
        send_near_ref[...] = source[pl.ds(jnp.where(even, planes, HALO), HALO)]
        send_far_ref[...] = source[pl.ds(jnp.where(even, HALO, planes), HALO)]
        coarse = restrict_to(
            lambda i, x: basis_s[i, x + HALO], lambda x: target[x + HALO], planes
        )
        tail = jnp.concatenate([coarse, jnp.zeros((PER, 128 - NBF), F32)], axis=1)

        def put(e, carry):
            packed_ref[e] = tail
            return carry

        lax.fori_loop(0, count, put, 0)


VMEM = pl.BlockSpec(memory_space=pltpu.VMEM)
SMEM = pl.BlockSpec(memory_space=pltpu.SMEM)
HBM = pl.BlockSpec(memory_space=pl.ANY)
PARAMS = pltpu.CompilerParams(vmem_limit_bytes=40 * 1024 * 1024)


def local(
    right_side, wet_quarters, trans_x, trans_y, trans_z, storage, basis, coupling, coarse_inverse,
    owned_block, block_slot, neighbours,
):
    count = lax.axis_size("gx")
    me = lax.axis_index("gx")
    planes, ny, nz = right_side.shape
    even = lax.rem(me, 2) == 0
    near_pairs = [(i, i ^ 1) for i in range(count)]
    far_pairs = [(i, i + 1) for i in range(1, count - 1, 2)]
    far_pairs = far_pairs + [(b, a) for a, b in far_pairs]

    def packed_halo(upper):
        wide = jnp.where(upper, planes - HALO, 0)
        thin = jnp.where(upper, planes - THIN, 0)
        pieces = [lax.dynamic_slice_in_dim(basis, wide, HALO, 1).reshape(NBF * HALO, ny, nz)]
        pieces.append(lax.dynamic_slice_in_dim(trans_x, wide, HALO, 0))
        right = lax.dynamic_slice_in_dim(right_side, thin, THIN, 0)
        high = right.astype(BF16)
        for field in (wet_quarters, trans_y, trans_z, storage):
            pieces.append(lax.dynamic_slice_in_dim(field, thin, THIN, 0).astype(BF16))
        pieces.append(high)
        pieces.append((right - high.astype(F32)).astype(BF16))
        return jnp.concatenate(pieces, 0)

    far = lax.ppermute(packed_halo(~even), "gx", far_pairs)
    near = lax.ppermute(packed_halo(even), "gx", near_pairs)

    packed = pl.pallas_call(
        functools.partial(first_kernel, count),
        out_shape=jax.ShapeDtypeStruct((count, PER, KROWS + 128), F32),
        in_specs=[SMEM, VMEM, VMEM, VMEM],
        out_specs=VMEM,
        compiler_params=PARAMS,
        name="restrict_first",
    )(owned_block, basis, right_side, coupling.reshape(KROWS, PER))
    gathered = lax.all_to_all(packed, "gx", 0, 0, tiled=True)

    padded = jnp.pad(coarse_inverse, ((0, 0), (0, 0), (LEAD * PER, WIN - LEAD * PER)))
    inverse = lax.dynamic_slice_in_dim(padded, me * PER, WIN, 2).reshape(NBF * NBF, WIN)

    full = planes + 2 * HALO
    field = (ny, nz)
    scratch = [
        pltpu.VMEM((NBF, full) + field, BF16),
        pltpu.VMEM((planes,) + field, F32),
        pltpu.VMEM((planes,) + field, jnp.int32),
        pltpu.VMEM((full,) + field, BF16),
        pltpu.VMEM((full,) + field, BF16),
        pltpu.VMEM((full,) + field, BF16),
        pltpu.VMEM((full,) + field, BF16),
        pltpu.VMEM((full,) + field, BF16),
        pltpu.VMEM((full,) + field, BF16),
        pltpu.VMEM((full,) + field, BF16),
        pltpu.VMEM((full, 6) + field, F32),
        pltpu.VMEM((full,) + field, F32),
        pltpu.VMEM((planes,) + field, F32),
        pltpu.VMEM((full,) + field, F32),
        pltpu.VMEM((full,) + field, F32),
        pltpu.VMEM((count * PER + WIN, 128), F32),
        pltpu.VMEM((KROWS, WIN), F32),
        pltpu.SemaphoreType.DMA((48,)),
    ]
    statics = (basis, right_side, wet_quarters, trans_x, trans_y, trans_z, storage, near, far)
    whole = jax.ShapeDtypeStruct((planes,) + field, F32)
    halo = jax.ShapeDtypeStruct((HALO,) + field, F32)
    blank = jnp.zeros((8, 128), F32)
    pressure, send_near, send_far, packed, coupled = pl.pallas_call(
        functools.partial(iteration_kernel, False, count),
        out_shape=(
            whole, halo, halo,
            jax.ShapeDtypeStruct((count, PER, 128), F32),
            jax.ShapeDtypeStruct((KROWS, WIN), F32),
        ),
        in_specs=[VMEM] * 3 + [HBM] * 9,
        out_specs=(VMEM,) * 5,
        scratch_shapes=scratch,
        compiler_params=PARAMS,
        name="iteration_first",
    )(gathered, inverse, blank, *statics)

    far_p = lax.ppermute(send_far, "gx", far_pairs)
    near_p = lax.ppermute(send_near, "gx", near_pairs)
    gathered = lax.all_to_all(packed, "gx", 0, 0, tiled=True)
    return pl.pallas_call(
        functools.partial(iteration_kernel, True, count),
        out_shape=(whole, whole),
        in_specs=[VMEM] * 3 + [HBM] * 12,
        out_specs=(VMEM,) * 2,
        scratch_shapes=scratch,
        compiler_params=PARAMS,
        name="iteration_last",
    )(gathered, inverse, coupled, *statics, pressure, near_p, far_p)


def solution(mesh):
    slabs = P(("parts", "gx"), None, None)
    placed = (
        slabs, slabs, slabs, slabs, slabs, slabs,
        P(None, ("parts", "gx"), None, None),
        P(None, None, None, ("parts", "gx")),
        P(None, None, "parts"),
        P(),
        P("gx"),
        P(None, "gx"),
    )
    return jax.shard_map(local, mesh=mesh, in_specs=placed, out_specs=(slabs, slabs), check_vma=False)
```

time: 302 us -> 81.6 us (0.27)
  the two profiles are of different devices: /device:TPU:10 before, /device:TPU:0 now
where the time goes in v1:
time: 81.6 us; the launch traced here: 80.8 us
  Pallas kernels  26.9 us (33%)
  starting transfers between devices  24.4 us (30%)
  local copies, waits for them, and re-layouts  18.4 us (23%)
  waiting for transfers between devices  9.13 us (11%)
  other arithmetic  1.26 us (2%)
    all_to_all x2, starting transfers between devices, local(): gathered = lax.all_to_all(packed, 'gx', 0, 0, tiled=True)  19.3 us
    unnamed x58, local copies, waits for them, and re-layouts  16.8 us
    pallas_call x1, Pallas kernels, local(): pl.pallas_call(functools.partial(iteration_kernel, True, count), out_shap...  12.6 us
    pallas_call x1, Pallas kernels, local(): pl.pallas_call(functools.partial(iteration_kernel, False, count), out_sha...  12.4 us
    all_to_all x2, waiting for transfers between devices, local(): gathered = lax.all_to_all(packed, 'gx', 0, 0, tiled=True)  8.81 us
    ppermute x1, starting transfers between devices, local(): near = lax.ppermute(packed_halo(even), 'gx', near_pairs)  3.3 us
    pallas_call x1, Pallas kernels, local(): pl.pallas_call(functools.partial(first_kernel, count), out_shape=jax.Shap...  1.87 us
  transfers between devices with their start and end apart: 6, of which 4 were waited for; matrix products, arithmetic and copies ran while one was open for 8% of the time, Pallas kernels for 0%

profile of v1, /device:TPU:0, one launch (start us, length us, event | category | flops | bytes accessed | tf_op | source)
XLA Modules:
  0.0 80.8 jit_solution(4983637165542121027)
XLA Ops:
  0.6 0.7 copy-done.21
  1.3 1.2 %copy-done = bf16[8,16,32,128]{3,2,1,0:T(8,128)(2,1)S(1)} copy-done((bf16[8,16,32,128]{3,2,1,0:T(8,128)(2,1)S(1)}, bf16[8,16,32,128]{3,2,1,0:T(8,128)(2,1)}, u32[]{:S(2)}) %copy-start) | copy-done | bytes 1048600
  2.5 0.9 %copy-done.2 = f32[16,32,128]{2,1,0:T(8,128)S(1)} copy-done((f32[16,32,128]{2,1,0:T(8,128)S(1)}, f32[16,32,128]{2,1,0:T(8,128)}, u32[]{:S(2)}) %copy-start.2) | copy-done | bytes 262168
  3.5 0.9 %copy-done.15 = f32[6,8,8,16]{3,2,1,0:T(8,128)S(1)} copy-done((f32[6,8,8,16]{3,2,1,0:T(8,128)S(1)}, f32[6,8,8,16]{3,2,1,0:T(8,128)}, u32[]{:S(2)}) %copy-start.15) | copy-done | bytes 24600
  4.4 1.9 %restrict_first.1 = f32[16,16,512]{2,1,0:T(8,128)} custom-call(s32[256]{0:T(256)S(1)} %copy-done.21, bf16[8,16,32,128]{3,2,1,0:T(8,128)(2,1)S(1)} %copy-done, f32[16,32,128]{2,1,0:T(8,128)S(1)} %copy-done.2, f32[384,16]{1,0:T(8,128)S(1)} %bitcast.5), custom_call_target="tpu_custom_call" | custom-call | tf_op jit(solution)/shard_map/restrict_first/pallas_call | solution.py:350
  6.3 7.4 %all-to-all-start = ((f32[16,16,512]{2,1,0:T(8,128)}), f32[16,16,512]{2,1,0:T(8,128)S(1)}, u32[]{:S(2)}, u32[]{:S(2)}) async-start(f32[16,16,512]{2,1,0:T(8,128)} %restrict_first.1), calls=%async_computation | async-start | bytes 1048576 | tf_op jit(solution)/shard_map/all_to_all | solution.py:358
  13.8 0.8 %constant_dynamic-update-slice_fusion.7 = (bf16[54,32,128]{2,1,0:T(8,128)(2,1)}, bf16[54,32,128]{2,1,0:T(8,128)(2,1)}) fusion(bf16[32,32,128]{2,1,0:T(8,128)(2,1)S(1)} %bitcast.7, bf16[32,32,128]{2,1,0:T(8,128)(2,1)S(1)} %bitcast.6), kind=kLoop, calls=%fused_computation.15 | loop fusion | bytes 1048576
  19.1 0.7 collective-permute-start.1
  19.8 3.3 %collective-permute-start = (bf16[54,32,128]{2,1,0:T(8,128)(2,1)}, bf16[54,32,128]{2,1,0:T(8,128)(2,1)S(1)}, u32[]{:S(2)}, u32[]{:S(2)}) collective-permute-start(bf16[54,32,128]{2,1,0:T(8,128)(2,1)} %get-tuple-element.15), channel_id=1, source_target_pairs={{0,1},{1,0},{2,3},{3,2},{4,5},{5,4},{6,7},{7,6},{8,9},{9,8},{10,11... | collective-permute-start | bytes 1327112 | tf_op jit(solution)/shard_map/ppermute | solution.py:348
  23.1 1.6 %fusion.refs_1_ = f32[64,256]{1,0:T(8,128)} fusion(s32[]{:T(128)S(6)} %select_n.15, f32[8,8,256]{2,1,0:T(8,128)} %param.20), kind=kLoop, calls=%fused_computation.1 | loop fusion | bytes 131076 | tf_op jit(solution)/shard_map/reshape | solution.py:361
  24.7 3.5 %all-to-all-done.refs_0_ = f32[16,16,512]{2,1,0:T(8,128)S(1)} async-done(((f32[16,16,512]{2,1,0:T(8,128)}), f32[16,16,512]{2,1,0:T(8,128)S(1)}, u32[]{:S(2)}, u32[]{:S(2)}) %all-to-all-start) | async-done | bytes 524320 | tf_op jit(solution)/shard_map/all_to_all | solution.py:358
  28.2 0.8 %copy-done.9 = f32[64,256]{1,0:T(8,128)S(1)} copy-done((f32[64,256]{1,0:T(8,128)S(1)}, f32[64,256]{1,0:T(8,128)}, u32[]{:S(2)}) %copy-start.9) | copy-done | bytes 65560
  29.0 12.4 %iteration_first.1 = (f32[16,32,128]{2,1,0:T(8,128)S(1)}, f32[4,32,128]{2,1,0:T(8,128)S(1)}, f32[4,32,128]{2,1,0:T(8,128)S(1)}, f32[16,16,128]{2,1,0:T(8,128)S(1)}, f32[384,256]{1,0:T(8,128)S(1)}) custom-call(f32[16,16,512]{2,1,0:T(8,128)S(1)} %all-to-all-done.refs_0_, f32[64,256]{1,0:T(8,128)S(1)} %copy-done.9, f32[8,128]{1,0:T(8,128)S(1)} %broadcast_in_dim.3.refs_2_, ...), custom_call_target="tpu_custom_call" | custom-call | tf_op jit(solution)/shard_map/iteration_first/pallas_call | solution.py:389
  41.4 0.7 copy-done.11
  42.2 0.7 copy-done.13
  42.9 0.7 copy-done.16
  44.8 11.9 %all-to-all-start.1 = ((f32[16,16,128]{2,1,0:T(8,128)}), f32[16,16,128]{2,1,0:T(8,128)S(1)}, u32[]{:S(2)}, u32[]{:S(2)}) async-start(f32[16,16,128]{2,1,0:T(8,128)} %copy-done.16), calls=%async_computation.1 | async-start | bytes 262144 | tf_op jit(solution)/shard_map/all_to_all | solution.py:405
  57.1 0.7 collective-permute-start.3
  59.3 5.3 %all-to-all-done.1.refs_0_ = f32[16,16,128]{2,1,0:T(8,128)S(1)} async-done(((f32[16,16,128]{2,1,0:T(8,128)}), f32[16,16,128]{2,1,0:T(8,128)S(1)}, u32[]{:S(2)}, u32[]{:S(2)}) %all-to-all-start.1) | async-done | bytes 131104 | tf_op jit(solution)/shard_map/all_to_all | solution.py:405
  64.6 1.0 %copy-done.12 = f32[384,256]{1,0:T(8,128)S(1)} copy-done((f32[384,256]{1,0:T(8,128)S(1)}, f32[384,256]{1,0:T(8,128)}, u32[]{:S(2)}) %copy-start.12) | copy-done | bytes 393240
  65.6 0.9 %copy-done.14 = f32[16,32,128]{2,1,0:T(8,128)S(1)} copy-done((f32[16,32,128]{2,1,0:T(8,128)S(1)}, f32[16,32,128]{2,1,0:T(8,128)}, u32[]{:S(2)}) %copy-start.14) | copy-done | bytes 262168
  66.5 0.8 %copy-done.18 = f32[4,32,128]{2,1,0:T(8,128)S(1)} copy-done((f32[4,32,128]{2,1,0:T(8,128)S(1)}, f32[4,32,128]{2,1,0:T(8,128)}, u32[]{:S(2)}) %copy-start.18) | copy-done | bytes 65560
  67.4 0.8 %copy-done.20 = f32[4,32,128]{2,1,0:T(8,128)S(1)} copy-done((f32[4,32,128]{2,1,0:T(8,128)S(1)}, f32[4,32,128]{2,1,0:T(8,128)}, u32[]{:S(2)}) %copy-start.20) | copy-done | bytes 65560
  68.2 12.6 %iteration_last.1 = (f32[16,32,128]{2,1,0:T(8,128)}, f32[16,32,128]{2,1,0:T(8,128)}) custom-call(f32[16,16,128]{2,1,0:T(8,128)S(1)} %all-to-all-done.1.refs_0_, f32[64,256]{1,0:T(8,128)S(1)} %copy-done.10, f32[384,256]{1,0:T(8,128)S(1)} %copy-done.12, bf16[8,16,32,128]{3,2,1,0:T(8,128)(2,1)S(1)} %copy-done.1, f32[16,32,128]{2,1,0:T(8,128)S(1)} %copy-done.3, ...), custom_call_target="tpu_custom_call" | custom-call | tf_op jit(solution)/shard_map/iteration_last/pallas_call | solution.py:406
  (54 shorter events, 7.8 us)
Async XLA Ops:
  1.3 1.2 %copy-start = (bf16[8,16,32,128]{3,2,1,0:T(8,128)(2,1)S(1)}, bf16[8,16,32,128]{3,2,1,0:T(8,128)(2,1)}, u32[]{:S(2)}) copy-start(bf16[8,16,32,128]{3,2,1,0:T(8,128)(2,1)} %refs_3_.3) | copy-start | bytes 3145732
  2.5 0.9 %copy-start.2 = (f32[16,32,128]{2,1,0:T(8,128)S(1)}, f32[16,32,128]{2,1,0:T(8,128)}, u32[]{:S(2)}) copy-start(f32[16,32,128]{2,1,0:T(8,128)} %refs_4_.3) | copy-start | bytes 786436
  3.5 0.9 %copy-start.15 = (f32[6,8,8,16]{3,2,1,0:T(8,128)S(1)}, f32[6,8,8,16]{3,2,1,0:T(8,128)}, u32[]{:S(2)}) copy-start(f32[6,8,8,16]{3,2,1,0:T(8,128)} %param.19) | copy-start | bytes 73732
  4.4 9.3 %copy-start.1 = (bf16[8,16,32,128]{3,2,1,0:T(8,128)(2,1)S(1)}, bf16[8,16,32,128]{3,2,1,0:T(8,128)(2,1)}, u32[]{:S(2)}) copy-start(bf16[8,16,32,128]{3,2,1,0:T(8,128)(2,1)} %refs_3_.3) | copy-start | bytes 3145732
  6.3 21.9 %all-to-all-start = ((f32[16,16,512]{2,1,0:T(8,128)}), f32[16,16,512]{2,1,0:T(8,128)S(1)}, u32[]{:S(2)}, u32[]{:S(2)}) async-start(f32[16,16,512]{2,1,0:T(8,128)} %restrict_first.1), calls=%async_computation | async-start | bytes 1048576 | tf_op jit(solution)/shard_map/all_to_all | solution.py:358
  13.8 0.9 %copy-start.5 = (bf16[16,32,128]{2,1,0:T(8,128)(2,1)S(1)}, bf16[16,32,128]{2,1,0:T(8,128)(2,1)}, u32[]{:S(2)}) copy-start(bf16[16,32,128]{2,1,0:T(8,128)(2,1)} %refs_6_.3) | copy-start | bytes 393220
  13.8 1.5 %copy-start.4 = (s32[16,32,128]{2,1,0:T(8,128)S(1)}, s32[16,32,128]{2,1,0:T(8,128)}, u32[]{:S(2)}) copy-start(s32[16,32,128]{2,1,0:T(8,128)} %refs_5_.3) | copy-start | bytes 786436
  13.8 3.4 %copy-start.8 = (bf16[16,32,128]{2,1,0:T(8,128)(2,1)S(1)}, bf16[16,32,128]{2,1,0:T(8,128)(2,1)}, u32[]{:S(2)}) copy-start(bf16[16,32,128]{2,1,0:T(8,128)(2,1)} %refs_9_.3) | copy-start | bytes 393220
  14.7 1.3 %copy-start.6 = (bf16[16,32,128]{2,1,0:T(8,128)(2,1)S(1)}, bf16[16,32,128]{2,1,0:T(8,128)(2,1)}, u32[]{:S(2)}) copy-start(bf16[16,32,128]{2,1,0:T(8,128)(2,1)} %refs_7_.3) | copy-start | bytes 393220
  14.7 1.9 %copy-start.7 = (bf16[16,32,128]{2,1,0:T(8,128)(2,1)S(1)}, bf16[16,32,128]{2,1,0:T(8,128)(2,1)}, u32[]{:S(2)}) copy-start(bf16[16,32,128]{2,1,0:T(8,128)(2,1)} %refs_8_.3) | copy-start | bytes 393220
  15.3 2.5 %copy-start.3 = (f32[16,32,128]{2,1,0:T(8,128)S(1)}, f32[16,32,128]{2,1,0:T(8,128)}, u32[]{:S(2)}) copy-start(f32[16,32,128]{2,1,0:T(8,128)} %refs_4_.3) | copy-start | bytes 786436
  19.1 5.5 %collective-permute-start.1 = (bf16[54,32,128]{2,1,0:T(8,128)(2,1)}, bf16[54,32,128]{2,1,0:T(8,128)(2,1)S(1)}, u32[]{:S(2)}, u32[]{:S(2)}) collective-permute-start(bf16[54,32,128]{2,1,0:T(8,128)(2,1)} %get-tuple-element.14), channel_id=1, source_target_pairs={{1,2},{3,4},{5,6},{7,8},{9,10},{11,12},{13,14},{2,1},{4,3},{6,5},{... | collective-permute-start | bytes 1327112 | tf_op jit(solution)/shard_map/ppermute | solution.py:347
  19.8 4.9 %collective-permute-start = (bf16[54,32,128]{2,1,0:T(8,128)(2,1)}, bf16[54,32,128]{2,1,0:T(8,128)(2,1)S(1)}, u32[]{:S(2)}, u32[]{:S(2)}) collective-permute-start(bf16[54,32,128]{2,1,0:T(8,128)(2,1)} %get-tuple-element.15), channel_id=1, source_target_pairs={{0,1},{1,0},{2,3},{3,2},{4,5},{5,4},{6,7},{7,6},{8,9},{9,8},{10,11... | collective-permute-start | bytes 1327112 | tf_op jit(solution)/shard_map/ppermute | solution.py:348
  28.2 0.8 %copy-start.9 = (f32[64,256]{1,0:T(8,128)S(1)}, f32[64,256]{1,0:T(8,128)}, u32[]{:S(2)}) copy-start(f32[64,256]{1,0:T(8,128)} %fusion.refs_1_) | copy-start | bytes 196612
  44.8 11.9 %copy-start.25 = (f32[4,32,128]{2,1,0:T(8,128)S(1)}, f32[4,32,128]{2,1,0:T(8,128)}, u32[]{:S(2)}) copy-start(f32[4,32,128]{2,1,0:T(8,128)} %copy-done.24) | copy-start | bytes 196612
  44.8 12.4 %copy-start.23 = (f32[4,32,128]{2,1,0:T(8,128)S(1)}, f32[4,32,128]{2,1,0:T(8,128)}, u32[]{:S(2)}) copy-start(f32[4,32,128]{2,1,0:T(8,128)} %copy-done.22) | copy-start | bytes 196612
  44.8 19.8 %copy-start.10 = (f32[64,256]{1,0:T(8,128)S(1)}, f32[64,256]{1,0:T(8,128)}, u32[]{:S(2)}) copy-start(f32[64,256]{1,0:T(8,128)} %fusion.refs_1_) | copy-start | bytes 196612
  44.8 19.8 %all-to-all-start.1 = ((f32[16,16,128]{2,1,0:T(8,128)}), f32[16,16,128]{2,1,0:T(8,128)S(1)}, u32[]{:S(2)}, u32[]{:S(2)}) async-start(f32[16,16,128]{2,1,0:T(8,128)} %copy-done.16), calls=%async_computation.1 | async-start | bytes 262144 | tf_op jit(solution)/shard_map/all_to_all | solution.py:405
  56.7 1.4 %collective-permute-start.2 = (f32[4,32,128]{2,1,0:T(8,128)S(1)}, f32[4,32,128]{2,1,0:T(8,128)S(1)}, u32[]{:S(2)}, u32[]{:S(2)}) collective-permute-start(f32[4,32,128]{2,1,0:T(8,128)S(1)} %copy-done.25), channel_id=1, source_target_pairs={{0,1},{1,0},{2,3},{3,2},{4,5},{5,4},{6,7},{7,6},{8,9},{9,8},{10,11... | collective-permute-start | bytes 196616 | tf_op jit(solution)/shard_map/ppermute | solution.py:404
  57.1 1.5 %collective-permute-start.3 = (f32[4,32,128]{2,1,0:T(8,128)S(1)}, f32[4,32,128]{2,1,0:T(8,128)S(1)}, u32[]{:S(2)}, u32[]{:S(2)}) collective-permute-start(f32[4,32,128]{2,1,0:T(8,128)S(1)} %copy-done.23), channel_id=1, source_target_pairs={{1,2},{3,4},{5,6},{7,8},{9,10},{11,12},{13,14},{2,1},{4,3},{6,5},{... | collective-permute-start | bytes 196616 | tf_op jit(solution)/shard_map/ppermute | solution.py:403
  64.6 1.0 %copy-start.12 = (f32[384,256]{1,0:T(8,128)S(1)}, f32[384,256]{1,0:T(8,128)}, u32[]{:S(2)}) copy-start(f32[384,256]{1,0:T(8,128)} %copy-done.11) | copy-start | bytes 1179652
  65.6 0.9 %copy-start.14 = (f32[16,32,128]{2,1,0:T(8,128)S(1)}, f32[16,32,128]{2,1,0:T(8,128)}, u32[]{:S(2)}) copy-start(f32[16,32,128]{2,1,0:T(8,128)} %copy-done.13) | copy-start | bytes 786436
  66.5 0.8 %copy-start.18 = (f32[4,32,128]{2,1,0:T(8,128)S(1)}, f32[4,32,128]{2,1,0:T(8,128)}, u32[]{:S(2)}) copy-start(f32[4,32,128]{2,1,0:T(8,128)} %copy-done.17) | copy-start | bytes 196612
  67.4 0.8 %copy-start.20 = (f32[4,32,128]{2,1,0:T(8,128)S(1)}, f32[4,32,128]{2,1,0:T(8,128)}, u32[]{:S(2)}) copy-start(f32[4,32,128]{2,1,0:T(8,128)} %copy-done.19) | copy-start | bytes 196612
  (8 other events, 5.2 us)

commit v2 on v1

v2 whole, which is shorter than its diff:
```python
import functools

import jax
import jax.numpy as jnp
from jax import lax
from jax.experimental import pallas as pl
from jax.experimental.pallas import tpu as pltpu
from jax.sharding import PartitionSpec as P

BLK = 16
NBF = 8
NNB = 6
SWEEPS = 3
CSWEEPS = 4
NYB = 2
NZB = 8
PER = NYB * NZB
WIN = 16 * PER
LEAD = 4
HALO = 4
OMEGA = 2.0 / 3.0
KROWS = NNB * NBF * NBF
F32 = jnp.float32
BF16 = jnp.bfloat16

THIN = HALO - 1
H_TX = NBF * HALO
H_REST = H_TX + HALO
H_WET = H_REST + 3 * THIN
H_ALL = H_REST + 6 * THIN


def planes_in_groups(low, high, group, step):
    count = (high - low) // group

    def body(k, carry):
        for j in range(group):
            step(low + k * group + j)
        return carry

    lax.fori_loop(0, count, body, 0)
    for x in range(low + count * group, high):
        step(x)


def three_parts(x):
    high = x.astype(BF16)
    rest = x - high.astype(F32)
    middle = rest.astype(BF16)
    low = (rest - middle.astype(F32)).astype(BF16)
    return high, middle, low


def restrict_to(basis_at, field_at, planes):
    def step(x, totals):
        field = field_at(x)
        out = []
        for i in range(NBF):
            for yb in range(NYB):
                rows = slice(yb * BLK, (yb + 1) * BLK)
                product = basis_at(i, x)[rows].astype(F32) * field[rows]
                out.append(totals[i * NYB + yb] + product[:8] + product[8:])
        return tuple(out)

    zero = jnp.zeros((8, 128), F32)
    totals = lax.fori_loop(0, planes, step, (zero,) * (NBF * NYB))
    groups = lax.broadcasted_iota(jnp.int32, (NZB, 3 * 128), 1)
    owner = lax.broadcasted_iota(jnp.int32, (NZB, 3 * 128), 0)
    spread = ((groups % 128) // BLK == owner).astype(F32).astype(BF16)
    halves = []
    for yb in range(NYB):
        rows = [jnp.sum(totals[i * NYB + yb], axis=0, keepdims=True) for i in range(NBF)]
        stacked = jnp.concatenate(three_parts(jnp.concatenate(rows, 0)), axis=1)
        halves.append(
            lax.dot_general(
                spread, stacked, (((1,), (1,)), ((), ())), preferred_element_type=F32
            )
        )
    return jnp.concatenate(halves, 0)


def started(pairs, sems, first=0):
    copies = [pltpu.make_async_copy(a, b, sems.at[first + k]) for k, (a, b) in enumerate(pairs)]
    for copy in copies:
        copy.start()
    return copies


def first_kernel(
    count, owned_hbm, basis_hbm, right_hbm, wet_hbm, tx_hbm, ty_hbm, tz_hbm, st_hbm, coupling_hbm,
    near_hbm, far_hbm, packed_hbm, owned_s, basis_s, right_s, thin_wet, coupling_s, rows_s, halo_s, sems,
):
    me = lax.axis_index("gx")
    even = lax.rem(me, 2) == 0
    planes = right_s.shape[0]
    sides = (jnp.logical_not(even), even)
    wides = [jnp.where(upper, planes - HALO, 0) for upper in sides]
    thins = [jnp.where(upper, planes - THIN, 0) for upper in sides]
    quarter = planes // 4
    pairs = [(right_hbm, right_s)]
    for side in range(2):
        thin = pl.ds(thins[side], THIN)
        pairs.append((wet_hbm.at[thin], thin_wet.at[side]))
        pairs.append((tx_hbm.at[pl.ds(wides[side], HALO)], halo_s.at[side, pl.ds(H_TX, HALO)]))
        for k, field in enumerate((ty_hbm, tz_hbm, st_hbm)):
            pairs.append((field.at[thin], halo_s.at[side, pl.ds(H_REST + k * THIN, THIN)]))
    edge = len(pairs)
    for k in (0, 3, 1, 2):
        span = pl.ds(k * quarter, quarter)
        pairs.append((basis_hbm.at[:, span], basis_s.at[:, span]))
    pairs += [(owned_hbm, owned_s), (coupling_hbm, coupling_s)]
    loads = started(pairs, sems)

    for copy in loads[: edge + 2]:
        copy.wait()
    stores = []
    for side in range(2):
        for i in range(NBF):
            halo_s[side, pl.ds(i * HALO, HALO)] = basis_s[i, pl.ds(wides[side], HALO)]
        for k in range(THIN):
            field = right_s[thins[side] + k]
            high = field.astype(BF16)
            halo_s[side, H_WET + k] = thin_wet[side, k].astype(F32).astype(BF16)
            halo_s[side, H_WET + THIN + k] = high
            halo_s[side, H_WET + 2 * THIN + k] = (field - high.astype(F32)).astype(BF16)
        stores += started(
            ((halo_s.at[side], (far_hbm, near_hbm)[side]),), sems, len(loads) + side
        )
    for copy in loads[edge + 2 :]:
        copy.wait()
    coarse = restrict_to(lambda i, x: basis_s[i, x], lambda x: right_s[x], planes)
    slot = lax.broadcasted_iota(jnp.int32, (PER, 1), 0)
    block = jnp.zeros((PER, 1), jnp.int32)
    for s in range(PER):
        block = jnp.where(slot == s, owned_s[me * PER + s], block)
    tail = jnp.concatenate(
        [coarse, block.astype(F32), jnp.zeros((PER, 128 - NBF - 1), F32)], axis=1
    )
    wide = jnp.concatenate([coupling_s[...], jnp.zeros((KROWS, 128 - PER), F32)], axis=1)
    rows_s[...] = jnp.concatenate([wide.T[:PER], tail], axis=1)
    stores += started(
        [(rows_s, packed_hbm.at[e]) for e in range(count)], sems, len(loads) + 2
    )
    for copy in stores:
        copy.wait()


def coarse_solve(coupling_at, inverse_at, residual):
    lane = lax.broadcasted_iota(jnp.int32, (NBF, WIN), 1)
    in_z, in_y = lane % NZB, (lane // NZB) % NYB

    def rows_of(parts):
        return jnp.concatenate([jnp.sum(p, axis=0, keepdims=True) for p in parts], 0)

    def inverted(v):
        return rows_of([inverse_at(i) * v for i in range(NBF)])

    values = inverted(residual)
    for _ in range(CSWEEPS - 1):
        near = (
            pltpu.roll(values, WIN - PER, 1),
            pltpu.roll(values, PER, 1),
            jnp.where(in_y < NYB - 1, pltpu.roll(values, WIN - NZB, 1), 0.0),
            jnp.where(in_y > 0, pltpu.roll(values, NZB, 1), 0.0),
            jnp.where(in_z < NZB - 1, pltpu.roll(values, WIN - 1, 1), 0.0),
            jnp.where(in_z > 0, pltpu.roll(values, 1, 1), 0.0),
        )
        parts = []
        for i in range(NBF):
            total = coupling_at(0, i) * near[0]
            for k in range(1, NNB):
                total = total + coupling_at(k, i) * near[k]
            parts.append(total)
        values = inverted(residual - rows_of(parts))
    return values


def spread_blocks(values):
    width = 3 * NYB * 128
    block = lax.broadcasted_iota(jnp.int32, (128, width), 0)
    column = lax.broadcasted_iota(jnp.int32, (128, width), 1)
    wanted = (LEAD - 1) * PER + column // BLK
    chosen = (block == wanted).astype(F32).astype(BF16)
    stacked = jnp.concatenate(three_parts(values[:, :128]), axis=0)
    spread = jnp.dot(stacked, chosen, preferred_element_type=F32)
    return spread[:NBF] + spread[NBF : 2 * NBF] + spread[2 * NBF :]


def coefficients(coef_ref, x, quarters, right, east, west, north, upper, storage):
    in_y = lax.broadcasted_iota(jnp.int32, north.shape, 0)
    in_z = lax.broadcasted_iota(jnp.int32, north.shape, 1)
    last_y, last_z = north.shape[0] - 1, north.shape[1] - 1
    east, west, north, upper = (a.astype(F32) for a in (east, west, north, upper))
    wet = quarters * 0.25
    dry = 1.0 - jnp.minimum(quarters, 1.0)
    south = jnp.where(in_y > 0, pltpu.roll(north, 1, 0), 0.0)
    lower = jnp.where(in_z > 0, pltpu.roll(upper, 1, 1), 0.0)
    diag = wet * (storage.astype(F32) + east + west + north + south + upper + lower) + dry
    share = OMEGA / diag
    scale = wet * share
    coef_ref[x, 0] = scale * east
    coef_ref[x, 1] = scale * west
    coef_ref[x, 2] = jnp.where(in_y < last_y, scale * north, 0.0)
    coef_ref[x, 3] = scale * south
    coef_ref[x, 4] = jnp.where(in_z < last_z, scale * upper, 0.0)
    coef_ref[x, 5] = scale * lower
    coef_ref[x, 6] = right * share
    coef_ref[x, 7] = diag * (1.0 / OMEGA)


def prepare_kernel(
    right_hbm, wet_hbm, tx_hbm, ty_hbm, tz_hbm, st_hbm, all_inverse_hbm,
    right_ref, wet_ref, tx_ref, ty_ref, tz_ref, st_ref, inverse_ref, _room_ref, _more_room_ref,
    quarters, all_inverse, sems,
):
    me = lax.axis_index("gx")
    pairs = (
        (right_hbm, right_ref), (wet_hbm, quarters), (tx_hbm, tx_ref), (ty_hbm, ty_ref), (tz_hbm, tz_ref),
        (st_hbm, st_ref), (all_inverse_hbm, all_inverse),
    )
    for copy in started(pairs, sems):
        copy.wait()
    wet_ref[...] = quarters[...].astype(F32).astype(BF16)
    blocks = all_inverse.shape[1]
    start = (me - LEAD) * PER
    turned = pltpu.roll(all_inverse[...], lax.rem(blocks - start, blocks), 1)[:, :WIN]
    block = lax.broadcasted_iota(jnp.int32, turned.shape, 1) + start
    inverse_ref[...] = jnp.where((block >= 0) & (block < blocks), turned, 0.0)


def all_coefficients(coef_ref, near_ref, far_ref, statics, tx_s, even):
    right_ref, wet_ref, tx_ref, ty_ref, tz_ref, st_ref = statics
    planes = right_ref.shape[0]
    top = planes + HALO
    tx_s[HALO] = tx_ref[0]
    tx_s[top - 1] = tx_ref[planes - 1]
    for halo, wide in ((near_ref, jnp.where(even, top, 0)), (far_ref, jnp.where(even, 0, top))):
        tx_s[pl.ds(wide, HALO)] = halo[pl.ds(H_TX, HALO)]

    def own(x, before):
        coefficients(
            coef_ref, x + HALO, wet_ref[x].astype(F32), right_ref[x], tx_ref[x], before, ty_ref[x], tz_ref[x],
            st_ref[x],
        )

    planes_in_groups(1, planes, 5, lambda x: own(x, tx_ref[x - 1]))
    own(0, tx_s[HALO - 1])
    for halo, thin in ((near_ref, jnp.where(even, top, 1)), (far_ref, jnp.where(even, 1, top))):
        for k in range(THIN):
            right = halo[H_WET + THIN + k].astype(F32) + halo[H_WET + 2 * THIN + k].astype(F32)
            coefficients(
                coef_ref, thin + k, halo[H_WET + k].astype(F32), right, tx_s[thin + k],
                tx_s[thin + k - 1], halo[H_REST + k], halo[H_REST + THIN + k],
                halo[H_REST + 2 * THIN + k],
            )


def window_of(gathered_ref, window_s, me, count, first):
    window_s[...] = jnp.zeros_like(window_s)
    for e in range(count):
        window_s[pl.ds(LEAD * PER + e * PER, PER)] = gathered_ref[e, :, pl.ds(first, 128)]
    return window_s[pl.ds(pl.multiple_of(me * PER, PER), WIN)].T[:NBF]


def blocks_in_order(gathered_ref, coupling_ref, me, count):
    lane = lax.broadcasted_iota(jnp.int32, (WIN, WIN), 1) + (me - LEAD) * PER
    for part in range(count * PER // WIN):
        span = pl.ds(part * (WIN // PER), WIN // PER)
        rows = gathered_ref[span].reshape(WIN, KROWS + 128)
        block = rows[:, KROWS + NBF : KROWS + NBF + 1].astype(jnp.int32)
        chosen = (block == lane).astype(F32).astype(BF16)
        stacked = jnp.concatenate(three_parts(rows[:, :KROWS].T), axis=0)
        found = jnp.dot(stacked, chosen, preferred_element_type=F32)
        found = found[:KROWS] + found[KROWS : 2 * KROWS] + found[2 * KROWS :]
        coupling_ref[...] = found if part == 0 else coupling_ref[...] + found


def corrected_values(coupling_ref, inverse_ref, residual):
    values = coarse_solve(
        lambda k, i: coupling_ref[pl.ds((k * NBF + i) * NBF, NBF)],
        lambda i: inverse_ref[pl.ds(i * NBF, NBF)],
        residual,
    )
    return spread_blocks(values)


def prolong(state, spread, basis_ref, near_ref, far_ref, even, planes, before):
    top = planes + HALO

    def gains_of(values):
        return [
            [
                jnp.broadcast_to(values[i : i + 1, yb * 128 : (yb + 1) * 128], (BLK, 128))
                for i in range(NBF)
            ]
            for yb in range(NYB)
        ]

    def plane(x, at, gains, base):
        for yb in range(NYB):
            rows = slice(yb * BLK, (yb + 1) * BLK)
            total = at(0, rows).astype(F32) * gains[yb][0]
            for i in range(1, NBF):
                total = total + at(i, rows).astype(F32) * gains[yb][i]
            state[x, rows] = total if base is None else base[rows] + total

    width = NYB * 128
    below, own, above = (spread[:, s * width : (s + 1) * width] for s in range(3))
    for near, halo, wide in (
        (True, near_ref, jnp.where(even, top, 0)), (False, far_ref, jnp.where(even, 0, top))
    ):
        upper = even if near else jnp.logical_not(even)
        gains = gains_of(jnp.where(upper, above, below))
        for k in range(HALO):
            base = before(k, near)
            plane(wide + k, lambda i, rows: halo[i * HALO + k, rows], gains, base)
    gains = gains_of(own)

    def step(x):
        plane(x + HALO, lambda i, rows: basis_ref[i, x, rows], gains, before(x, None))

    planes_in_groups(0, planes, 4, step)


def pulled(coef_ref, state, x):
    here = state[x]
    ny, nz = here.shape
    total = coef_ref[x, 6] + coef_ref[x, 0] * state[x + 1] + coef_ref[x, 1] * state[x - 1]
    total = total + coef_ref[x, 2] * pltpu.roll(here, ny - 1, 0) + coef_ref[x, 3] * pltpu.roll(here, 1, 0)
    total = total + coef_ref[x, 4] * pltpu.roll(here, nz - 1, 1) + coef_ref[x, 5] * pltpu.roll(here, 1, 1)
    return here, total


def smooth(coef_ref, one, two, planes):
    source, target = one, two
    for k in range(SWEEPS):

        def step(x):
            here, total = pulled(coef_ref, source, x)
            target[x] = (1.0 - OMEGA) * here + total

        low, high = k + 1, planes + 2 * HALO - 1 - k
        planes_in_groups(low, high, (high - low) // 2, step)
        source, target = target, source
    return source, target


def misfit(coef_ref, source, x):
    here, total = pulled(coef_ref, source, x)
    return (total - OMEGA * here) * coef_ref[x, 7]


def second_kernel(
    count, basis_hbm, gathered_ref, inverse_ref, near_ref, far_ref, *refs
):
    statics, refs = refs[:6], refs[8:]
    pressure_ref, coupling_ref, send_near_hbm, send_far_hbm, packed_hbm = refs[:5]
    coef_ref, one_s, two_s, tx_s, window_s, tail_s, basis_ref, sems = refs[5:]
    load = started(((basis_hbm, basis_ref),), sems, 2 + count)
    planes = pressure_ref.shape[0]
    me = lax.axis_index("gx")
    even = lax.rem(me, 2) == 0
    blocks_in_order(gathered_ref, coupling_ref, me, count)
    spread = corrected_values(
        coupling_ref, inverse_ref, window_of(gathered_ref, window_s, me, count, KROWS)
    )
    all_coefficients(coef_ref, near_ref, far_ref, statics, tx_s, even)
    load[0].wait()
    prolong(one_s, spread, basis_ref, near_ref, far_ref, even, planes, lambda k, near: None)
    source, target = smooth(coef_ref, one_s, two_s, planes)
    near_from, far_from = jnp.where(even, planes, HALO), jnp.where(even, HALO, planes)
    stores = started(
        (
            (source.at[pl.ds(far_from, HALO)], send_far_hbm),
            (source.at[pl.ds(near_from, HALO)], send_near_hbm),
        ),
        sems,
    )
    pressure_ref[...] = source[pl.ds(HALO, planes)]

    def step(x):
        target[x] = misfit(coef_ref, source, x)

    planes_in_groups(HALO, planes + HALO, 8, step)
    coarse = restrict_to(lambda i, x: basis_ref[i, x], lambda x: target[x + HALO], planes)
    tail_s[...] = jnp.concatenate([coarse, jnp.zeros((PER, 128 - NBF), F32)], axis=1)
    stores += started([(tail_s, packed_hbm.at[e]) for e in range(count)], sems, 2)
    for copy in stores:
        copy.wait()


def last_kernel(
    count, basis_hbm, gathered_ref, inverse_ref, near_ref, far_ref, coupling_ref, pressure_ref, near_p_ref,
    far_p_ref, *refs
):
    statics, refs = refs[:6], refs[6:]
    pressure_out, residual_out, coef_ref, one_s, two_s, tx_s, residual_s, window_s, basis_ref, sems = refs
    load = started(((basis_hbm, basis_ref),), sems, 3)
    planes = pressure_ref.shape[0]
    me = lax.axis_index("gx")
    even = lax.rem(me, 2) == 0
    spread = corrected_values(
        coupling_ref, inverse_ref, window_of(gathered_ref, window_s, me, count, 0)
    )

    def before(k, near):
        if near is None:
            return pressure_ref[k]
        return near_p_ref[k] if near else far_p_ref[k]

    all_coefficients(coef_ref, near_ref, far_ref, statics, tx_s, even)
    load[0].wait()
    prolong(one_s, spread, basis_ref, near_ref, far_ref, even, planes, before)
    source, _ = smooth(coef_ref, one_s, two_s, planes)
    stores = started(((source.at[pl.ds(HALO, planes)], pressure_out),), sems)
    half = planes // 2

    def step(x):
        residual_s[x - HALO] = misfit(coef_ref, source, x)

    for k in range(2):
        planes_in_groups(HALO + k * half, HALO + (k + 1) * half, half, step)
        span = pl.ds(k * half, half)
        stores += started(((residual_s.at[span], residual_out.at[span]),), sems, 1 + k)
    for copy in stores:
        copy.wait()


VMEM = pl.BlockSpec(memory_space=pltpu.VMEM)
ANY = pl.BlockSpec(memory_space=pl.ANY)


def kernel_call(name, body, arguments, outputs, scratch, aliases=None):
    spec = {pltpu.HBM: ANY, pltpu.VMEM: VMEM}
    call = pl.pallas_call(
        body,
        out_shape=[space(shape, dtype) for space, shape, dtype in outputs],
        in_specs=[spec[space] for space, _ in arguments],
        out_specs=[spec[space] for space, _, _ in outputs],
        scratch_shapes=scratch,
        input_output_aliases=aliases or {},
        compiler_params=pltpu.CompilerParams(vmem_limit_bytes=16 * 1024 * 1024),
        name=name,
    )
    return call(*[pltpu.with_memory_space_constraint(value, space) for space, value in arguments])


def local(
    right_side, wet_quarters, trans_x, trans_y, trans_z, storage, basis, coupling, coarse_inverse,
    owned_block, block_slot, neighbours,
):
    count = lax.axis_size("gx")
    planes, ny, nz = right_side.shape
    field = (ny, nz)
    full = planes + 2 * HALO
    near_pairs = [(i, i ^ 1) for i in range(count)]
    far_pairs = [(i, i + 1) for i in range(1, count - 1, 2)]
    far_pairs = far_pairs + [(b, a) for a, b in far_pairs]
    H, V = pltpu.HBM, pltpu.VMEM
    statics = [(H, a) for a in (right_side, wet_quarters, trans_x, trans_y, trans_z, storage)]
    halo = (H_ALL,) + field

    near, far, packed = kernel_call(
        "restrict_first",
        functools.partial(first_kernel, count),
        [(H, owned_block), (H, basis), *statics, (H, coupling.reshape(KROWS, PER))],
        [(H, halo, BF16), (H, halo, BF16), (H, (count, PER, KROWS + 128), F32)],
        [
            pltpu.SMEM(owned_block.shape, jnp.int32),
            pltpu.VMEM(basis.shape, BF16),
            pltpu.VMEM(right_side.shape, F32),
            pltpu.VMEM((2, THIN) + field, jnp.int32),
            pltpu.VMEM((KROWS, PER), F32),
            pltpu.VMEM((PER, KROWS + 128), F32),
            pltpu.VMEM((2,) + halo, BF16),
            pltpu.SemaphoreType.DMA((20 + count,)),
        ],
    )
    far = lax.ppermute(far, "gx", far_pairs)
    near = lax.ppermute(near, "gx", near_pairs)
    gathered = lax.all_to_all(packed, "gx", 0, 0, tiled=True)

    blocks = coarse_inverse.shape[2]
    *fields, inverse, room, more_room = kernel_call(
        "prepare",
        prepare_kernel,
        [*statics, (H, coarse_inverse.reshape(NBF * NBF, blocks))],
        [(V, right_side.shape, F32)]
        + [(V, right_side.shape, BF16)] * 5
        + [(V, (NBF * NBF, WIN), F32), (V, right_side.shape, F32), (V, (KROWS, WIN), F32)],
        [
            pltpu.VMEM(right_side.shape, jnp.int32),
            pltpu.VMEM((NBF * NBF, blocks), F32),
            pltpu.SemaphoreType.DMA((7,)),
        ],
    )

    factors = pltpu.VMEM((full, 8) + field, F32)
    state = pltpu.VMEM((full,) + field, F32)
    window = pltpu.VMEM((count * PER + WIN, 128), F32)
    around = pltpu.VMEM((full,) + field, BF16)
    pressure, coupled, send_near, send_far, packed = kernel_call(
        "iteration_first",
        functools.partial(second_kernel, count),
        [(H, basis)] + [(V, a) for a in (gathered, inverse, near, far, *fields, room, more_room)],
        [
            (V, (planes,) + field, F32),
            (V, (KROWS, WIN), F32),
            (H, (HALO,) + field, F32),
            (H, (HALO,) + field, F32),
            (H, (count, PER, 128), F32),
        ],
        [
            factors, state, state, around, window,
            pltpu.VMEM((PER, 128), F32), pltpu.VMEM(basis.shape, BF16), pltpu.SemaphoreType.DMA((3 + count,)),
        ],
        {11: 0, 12: 1},
    )

    far_p = lax.ppermute(send_far, "gx", far_pairs)
    near_p = lax.ppermute(send_near, "gx", near_pairs)
    gathered = lax.all_to_all(packed, "gx", 0, 0, tiled=True)
    whole = (H, (planes,) + field, F32)
    return kernel_call(
        "iteration_last",
        functools.partial(last_kernel, count),
        [(H, basis)]
        + [(V, a) for a in (gathered, inverse, near, far, coupled, pressure, near_p, far_p, *fields)],
        [whole, whole],
        [
            factors, state, state, around,
            pltpu.VMEM((planes,) + field, F32), window, pltpu.VMEM(basis.shape, BF16),
            pltpu.SemaphoreType.DMA((4,)),
        ],
    )


def solution(mesh):
    slabs = P(("parts", "gx"), None, None)
    placed = (
        slabs, slabs, slabs, slabs, slabs, slabs,
        P(None, ("parts", "gx"), None, None),
        P(None, None, None, ("parts", "gx")),
        P(None, None, "parts"),
        P(),
        P("gx"),
        P(None, "gx"),
    )
    return jax.shard_map(local, mesh=mesh, in_specs=placed, out_specs=(slabs, slabs), check_vma=False)
```

time: 81.6 us -> 51.3 us (0.63)
  local copies, waits for them, and re-layouts: 18.4 us -> 0.01 us
  Pallas kernels: 26.9 us -> 13.1 us
  waiting for transfers between devices: 9.13 us -> 18.8 us
  starting transfers between devices: 24.4 us -> 18.3 us
  other arithmetic: 1.26 us -> 0 us
    unnamed x58 -> x6, local copies, waits for them, and re-layouts: 16.8 us -> 0.01 us
    pallas_call x3 -> x4, Pallas kernels: 26.9 us -> 13.1 us  [kernel_call(): call(*[pltpu.with_memory_space_constraint(value, space) for space, value...]
    all_to_all x2, waiting for transfers between devices: 8.81 us -> 18.5 us  [local(): gathered = lax.all_to_all(packed, 'gx', 0, 0, tiled=True)]
    all_to_all x2, starting transfers between devices: 19.3 us -> 16.1 us  [local(): gathered = lax.all_to_all(packed, 'gx', 0, 0, tiled=True)]
    ppermute x2, starting transfers between devices: 3.98 us -> 1.09 us  [the longest x1 0.68 us: local(): far = lax.ppermute(far, 'gx', far_pairs)]
    reshape x1 -> x0, local copies, waits for them, and re-layouts: 1.55 us -> none  [local(): lax.dynamic_slice_in_dim(padded, me * PER, WIN, 2).reshape(NBF * NBF, WIN)]
  transfers between devices with their start and end apart: 6 -> 6, of which waited for: 4 -> 3; matrix products, arithmetic and copies ran while one was open for 8% -> 0% of each run, Pallas kernels for 0% -> 3%
where the time goes in v2:
time: 51.3 us; the launch traced here: 50.9 us
  waiting for transfers between devices  18.8 us (37%)
  starting transfers between devices  18.3 us (36%)
  Pallas kernels  13.1 us (26%)
  between operations  0.74 us (1%)
    all_to_all x2, waiting for transfers between devices, local(): gathered = lax.all_to_all(packed, 'gx', 0, 0, tiled=True)  18.5 us
    all_to_all x2, starting transfers between devices, local(): gathered = lax.all_to_all(packed, 'gx', 0, 0, tiled=True)  16.1 us
    pallas_call x4, Pallas kernels, kernel_call(): call(*[pltpu.with_memory_space_constraint(value, space) for space, value...  13.1 us
  transfers between devices with their start and end apart: 6, of which 3 were waited for; matrix products, arithmetic and copies ran while one was open for 0% of the time, Pallas kernels for 3%

profile of v2, /device:TPU:0, one launch (start us, length us, event | category | flops | bytes accessed | tf_op | source)
XLA Modules:
  0.0 50.9 jit_solution(2148141340081929351)
XLA Ops:
  0.6 3.1 %restrict_first.1 = (bf16[54,32,128]{2,1,0:T(8,128)(2,1)}, bf16[54,32,128]{2,1,0:T(8,128)(2,1)}, f32[16,16,512]{2,1,0:T(8,128)}) custom-call(s32[256]{0:T(256)} %owned_hbm.1, bf16[8,16,32,128]{3,2,1,0:T(8,128)(2,1)} %basis_hbm.5, f32[16,32,128]{2,1,0:T(8,128)} %right_hbm.3, s32[16,32,128]{2,1,0:T(8,128)} %wet_hbm.3, bf16[16,32,128]{2,1,0:T(8,128)(2,1)} %tx_hbm.3, ...), custom_call_target="tpu_custom_call" | custom-call | tf_op jit(solution)/shard_map/restrict_first/pallas_call | solution.py:445
  3.7 0.0 copy-start
  3.7 7.5 %all-to-all-start = ((f32[16,16,512]{2,1,0:T(8,128)}), f32[16,16,512]{2,1,0:T(8,128)S(1)}, u32[]{:S(2)}, u32[]{:S(2)}) async-start(f32[16,16,512]{2,1,0:T(8,128)} %get-tuple-element.19), calls=%async_computation | async-start | bytes 1048576 | tf_op jit(solution)/shard_map/all_to_all | solution.py:481
  11.3 0.4 collective-permute-start
  11.7 0.0 copy-done
  11.7 0.7 %collective-permute-start.1 = (bf16[54,32,128]{2,1,0:T(8,128)(2,1)S(1)}, bf16[54,32,128]{2,1,0:T(8,128)(2,1)S(1)}, u32[]{:S(2)}, u32[]{:S(2)}) collective-permute-start(bf16[54,32,128]{2,1,0:T(8,128)(2,1)S(1)} %copy-done), channel_id=1, source_target_pairs={{1,2},{3,4},{5,6},{7,8},{9,10},{11,12},{13,14},{2,1},{4,3},{6,5},{... | collective-permute-start | bytes 1327112 | tf_op jit(solution)/shard_map/ppermute | solution.py:479
  12.4 1.3 %prepare.1 = (f32[16,32,128]{2,1,0:T(8,128)S(1)}, bf16[16,32,128]{2,1,0:T(8,128)(2,1)S(1)}, bf16[16,32,128]{2,1,0:T(8,128)(2,1)S(1)}, bf16[16,32,128]{2,1,0:T(8,...) custom-call(f32[16,32,128]{2,1,0:T(8,128)} %right_hbm.3, ...), custom_call_target="tpu_custom_call" | custom-call | tf_op jit(solution)/shard_map/prepare/pallas_call | solution.py:445
  13.7 0.0 collective-permute-done.near_ref
  13.7 0.0 collective-permute-done.1.far_ref
  13.7 12.0 %all-to-all-done.gathered_ref = f32[16,16,512]{2,1,0:T(8,128)S(1)} async-done(((f32[16,16,512]{2,1,0:T(8,128)}), f32[16,16,512]{2,1,0:T(8,128)S(1)}, u32[]{:S(2)}, u32[]{:S(2)}) %all-to-all-start) | async-done | bytes 524320 | tf_op jit(solution)/shard_map/all_to_all | solution.py:481
  25.7 4.8 %iteration_first.1 = (f32[16,32,128]{2,1,0:T(8,128)S(1)}, f32[384,256]{1,0:T(8,128)S(1)}, f32[4,32,128]{2,1,0:T(8,128)}, f32[4,32,128]{2,1,0:T(8,128)}, f32[16,16,128]{2,1,0:T(8,128)}) custom-call(bf16[8,16,32,128]{3,2,1,0:T(8,128)(2,1)} %basis_hbm.5, f32[16,16,512]{2,1,0:T(8,128)S(1)} %all-to-all-done.gathered_ref, ...), custom_call_target="tpu_custom_call", output_to_operand_aliasing={{0}: (11, {}), {1}: (12, {})} | custom-call | tf_op jit(solution)/shard_map/iteration_first/pallas_call | solution.py:445
  30.5 0.0 copy-start.2
  30.5 0.0 copy-start.1
  30.5 8.5 %all-to-all-start.1 = ((f32[16,16,128]{2,1,0:T(8,128)}), f32[16,16,128]{2,1,0:T(8,128)S(1)}, u32[]{:S(2)}, u32[]{:S(2)}) async-start(f32[16,16,128]{2,1,0:T(8,128)} %get-tuple-element.31), calls=%async_computation.1 | async-start | bytes 262144 | tf_op jit(solution)/shard_map/all_to_all | solution.py:522
  39.1 0.0 copy-done.2
  39.1 0.5 collective-permute-start.2
  39.5 0.0 copy-done.1
  39.5 0.7 %collective-permute-start.3 = (f32[4,32,128]{2,1,0:T(8,128)S(1)}, f32[4,32,128]{2,1,0:T(8,128)S(1)}, u32[]{:S(2)}, u32[]{:S(2)}) collective-permute-start(f32[4,32,128]{2,1,0:T(8,128)S(1)} %copy-done.1), channel_id=1, source_target_pairs={{1,2},{3,4},{5,6},{7,8},{9,10},{11,12},{13,14},{2,1},{4,3},{6,5},{... | collective-permute-start | bytes 196616 | tf_op jit(solution)/shard_map/ppermute | solution.py:520
  40.2 0.2 collective-permute-done.2.near_p_ref
  40.4 0.0 collective-permute-done.3.far_p_ref
  40.4 6.5 %all-to-all-done.1.gathered_ref = f32[16,16,128]{2,1,0:T(8,128)S(1)} async-done(((f32[16,16,128]{2,1,0:T(8,128)}), f32[16,16,128]{2,1,0:T(8,128)S(1)}, u32[]{:S(2)}, u32[]{:S(2)}) %all-to-all-start.1) | async-done | bytes 131104 | tf_op jit(solution)/shard_map/all_to_all | solution.py:522
  47.0 3.9 %iteration_last.1 = (f32[16,32,128]{2,1,0:T(8,128)}, f32[16,32,128]{2,1,0:T(8,128)}) custom-call(bf16[8,16,32,128]{3,2,1,0:T(8,128)(2,1)} %basis_hbm.5, f32[16,16,128]{2,1,0:T(8,128)S(1)} %all-to-all-done.1.gathered_ref, f32[64,256]{1,0:T(8,128)S(1)} %get-tuple-element.20.inverse_ref, bf16[54,32,128]{2,1,0:T(8,128)(2,1)S(1)} %collective-permute-done.near_ref, ...), custom_call_target="tpu_custom_call" | custom-call | tf_op jit(solution)/shard_map/iteration_last/pallas_call | solution.py:445
Async XLA Ops:
  3.7 8.0 %copy-start = (bf16[54,32,128]{2,1,0:T(8,128)(2,1)S(1)}, bf16[54,32,128]{2,1,0:T(8,128)(2,1)}, u32[]{:S(2)}) copy-start(bf16[54,32,128]{2,1,0:T(8,128)(2,1)} %get-tuple-element.22) | copy-start | bytes 1327108
  3.7 22.0 %all-to-all-start = ((f32[16,16,512]{2,1,0:T(8,128)}), f32[16,16,512]{2,1,0:T(8,128)S(1)}, u32[]{:S(2)}, u32[]{:S(2)}) async-start(f32[16,16,512]{2,1,0:T(8,128)} %get-tuple-element.19), calls=%async_computation | async-start | bytes 1048576 | tf_op jit(solution)/shard_map/all_to_all | solution.py:481
  11.3 2.5 %collective-permute-start = (bf16[54,32,128]{2,1,0:T(8,128)(2,1)}, bf16[54,32,128]{2,1,0:T(8,128)(2,1)S(1)}, u32[]{:S(2)}, u32[]{:S(2)}) collective-permute-start(bf16[54,32,128]{2,1,0:T(8,128)(2,1)} %get-tuple-element.21), channel_id=1, source_target_pairs={{0,1},{1,0},{2,3},{3,2},{4,5},{5,4},{6,7},{7,6},{8,9},{9,8},{10,11... | collective-permute-start | bytes 1327112 | tf_op jit(solution)/shard_map/ppermute | solution.py:480
  11.7 2.1 %collective-permute-start.1 = (bf16[54,32,128]{2,1,0:T(8,128)(2,1)S(1)}, bf16[54,32,128]{2,1,0:T(8,128)(2,1)S(1)}, u32[]{:S(2)}, u32[]{:S(2)}) collective-permute-start(bf16[54,32,128]{2,1,0:T(8,128)(2,1)S(1)} %copy-done), channel_id=1, source_target_pairs={{1,2},{3,4},{5,6},{7,8},{9,10},{11,12},{13,14},{2,1},{4,3},{6,5},{... | collective-permute-start | bytes 1327112 | tf_op jit(solution)/shard_map/ppermute | solution.py:479
  30.5 8.6 %copy-start.2 = (f32[4,32,128]{2,1,0:T(8,128)S(1)}, f32[4,32,128]{2,1,0:T(8,128)}, u32[]{:S(2)}) copy-start(f32[4,32,128]{2,1,0:T(8,128)} %get-tuple-element.34) | copy-start | bytes 196612
  30.5 9.0 %copy-start.1 = (f32[4,32,128]{2,1,0:T(8,128)S(1)}, f32[4,32,128]{2,1,0:T(8,128)}, u32[]{:S(2)}) copy-start(f32[4,32,128]{2,1,0:T(8,128)} %get-tuple-element.35) | copy-start | bytes 196612
  30.5 16.5 %all-to-all-start.1 = ((f32[16,16,128]{2,1,0:T(8,128)}), f32[16,16,128]{2,1,0:T(8,128)S(1)}, u32[]{:S(2)}, u32[]{:S(2)}) async-start(f32[16,16,128]{2,1,0:T(8,128)} %get-tuple-element.31), calls=%async_computation.1 | async-start | bytes 262144 | tf_op jit(solution)/shard_map/all_to_all | solution.py:522
  39.1 1.4 %collective-permute-start.2 = (f32[4,32,128]{2,1,0:T(8,128)S(1)}, f32[4,32,128]{2,1,0:T(8,128)S(1)}, u32[]{:S(2)}, u32[]{:S(2)}) collective-permute-start(f32[4,32,128]{2,1,0:T(8,128)S(1)} %copy-done.2), channel_id=1, source_target_pairs={{0,1},{1,0},{2,3},{3,2},{4,5},{5,4},{6,7},{7,6},{8,9},{9,8},{10,11... | collective-permute-start | bytes 196616 | tf_op jit(solution)/shard_map/ppermute | solution.py:521
  39.5 0.9 %collective-permute-start.3 = (f32[4,32,128]{2,1,0:T(8,128)S(1)}, f32[4,32,128]{2,1,0:T(8,128)S(1)}, u32[]{:S(2)}, u32[]{:S(2)}) collective-permute-start(f32[4,32,128]{2,1,0:T(8,128)S(1)} %copy-done.1), channel_id=1, source_target_pairs={{1,2},{3,4},{5,6},{7,8},{9,10},{11,12},{13,14},{2,1},{4,3},{6,5},{... | collective-permute-start | bytes 196616 | tf_op jit(solution)/shard_map/ppermute | solution.py:520

commit v3 on v2

--- a/solution.py
+++ b/solution.py
@@ -87,7 +87,7 @@
 
 
 def first_kernel(
-    count, owned_hbm, basis_hbm, right_hbm, wet_hbm, tx_hbm, ty_hbm, tz_hbm, st_hbm, coupling_hbm,
+    owned_hbm, basis_hbm, right_hbm, wet_hbm, tx_hbm, ty_hbm, tz_hbm, st_hbm, coupling_hbm,
     near_hbm, far_hbm, packed_hbm, owned_s, basis_s, right_s, thin_wet, coupling_s, rows_s, halo_s, sems,
 ):
     me = lax.axis_index("gx")
@@ -139,7 +139,7 @@
     wide = jnp.concatenate([coupling_s[...], jnp.zeros((KROWS, 128 - PER), F32)], axis=1)
     rows_s[...] = jnp.concatenate([wide.T[:PER], tail], axis=1)
     stores += started(
-        [(rows_s, packed_hbm.at[e]) for e in range(count)], sems, len(loads) + 2
+        [(rows_s, packed_hbm.at[chip]) for chip in range(packed_hbm.shape[0])], sems, len(loads) + 3
     )
     for copy in stores:
         copy.wait()
@@ -255,24 +255,27 @@
             )
 
 
-def window_of(gathered_ref, window_s, me, count, first):
+def window_of(pieces, window_s, me):
     window_s[...] = jnp.zeros_like(window_s)
-    for e in range(count):
-        window_s[pl.ds(LEAD * PER + e * PER, PER)] = gathered_ref[e, :, pl.ds(first, 128)]
+    for device, piece in pieces:
+        window_s[pl.ds(pl.multiple_of((LEAD + device) * PER, PER), PER)] = piece
     return window_s[pl.ds(pl.multiple_of(me * PER, PER), WIN)].T[:NBF]
 
 
-def blocks_in_order(gathered_ref, coupling_ref, me, count):
+def blocks_in_order(halves, coupling_ref, me):
     lane = lax.broadcasted_iota(jnp.int32, (WIN, WIN), 1) + (me - LEAD) * PER
-    for part in range(count * PER // WIN):
-        span = pl.ds(part * (WIN // PER), WIN // PER)
-        rows = gathered_ref[span].reshape(WIN, KROWS + 128)
+    tall = halves[0].shape[0]
+    for start in range(0, 2 * tall, WIN):
+        if tall >= WIN:
+            rows = halves[start // tall][pl.ds(start % tall, WIN)]
+        else:
+            rows = jnp.concatenate([half[...] for half in halves], axis=0)
         block = rows[:, KROWS + NBF : KROWS + NBF + 1].astype(jnp.int32)
         chosen = (block == lane).astype(F32).astype(BF16)
         stacked = jnp.concatenate(three_parts(rows[:, :KROWS].T), axis=0)
         found = jnp.dot(stacked, chosen, preferred_element_type=F32)
         found = found[:KROWS] + found[KROWS : 2 * KROWS] + found[2 * KROWS :]
-        coupling_ref[...] = found if part == 0 else coupling_ref[...] + found
+        coupling_ref[...] = found if start == 0 else coupling_ref[...] + found
 
 
 def corrected_values(coupling_ref, inverse_ref, residual):
@@ -284,42 +287,46 @@
     return spread_blocks(values)
 
 
-def prolong(state, spread, basis_ref, near_ref, far_ref, even, planes, before):
+def gains_of(values):
+    return [
+        [
+            jnp.broadcast_to(values[i : i + 1, yb * 128 : (yb + 1) * 128], (BLK, 128))
+            for i in range(NBF)
+        ]
+        for yb in range(NYB)
+    ]
+
+
+def prolong_plane(state, x, basis_at, gains, base):
+    for yb in range(NYB):
+        rows = slice(yb * BLK, (yb + 1) * BLK)
+        total = basis_at(0, rows).astype(F32) * gains[yb][0]
+        for i in range(1, NBF):
+            total = total + basis_at(i, rows).astype(F32) * gains[yb][i]
+        state[x, rows] = total if base is None else base[rows] + total
+
+
+def prolong_own(state, first, spread, basis_ref, pressure_ref=None):
+    width = NYB * 128
+    gains = gains_of(spread[:, width : 2 * width])
+
+    def step(x):
+        base = None if pressure_ref is None else pressure_ref[x]
+        prolong_plane(state, x + first, lambda i, rows: basis_ref[i, x, rows], gains, base)
+
+    planes_in_groups(0, basis_ref.shape[1], 4, step)
+
+
+def prolong_halo(state, spread, near_ref, far_ref, even, planes, near_p=None, far_p=None):
     top = planes + HALO
-
-    def gains_of(values):
-        return [
-            [
-                jnp.broadcast_to(values[i : i + 1, yb * 128 : (yb + 1) * 128], (BLK, 128))
-                for i in range(NBF)
-            ]
-            for yb in range(NYB)
-        ]
-
-    def plane(x, at, gains, base):
-        for yb in range(NYB):
-            rows = slice(yb * BLK, (yb + 1) * BLK)
-            total = at(0, rows).astype(F32) * gains[yb][0]
-            for i in range(1, NBF):
-                total = total + at(i, rows).astype(F32) * gains[yb][i]
-            state[x, rows] = total if base is None else base[rows] + total
-
     width = NYB * 128
-    below, own, above = (spread[:, s * width : (s + 1) * width] for s in range(3))
-    for near, halo, wide in (
-        (True, near_ref, jnp.where(even, top, 0)), (False, far_ref, jnp.where(even, 0, top))
-    ):
-        upper = even if near else jnp.logical_not(even)
+    below, above = spread[:, :width], spread[:, 2 * width :]
+    for halo, before, upper in ((near_ref, near_p, even), (far_ref, far_p, jnp.logical_not(even))):
         gains = gains_of(jnp.where(upper, above, below))
+        wide = jnp.where(upper, top, 0)
         for k in range(HALO):
-            base = before(k, near)
-            plane(wide + k, lambda i, rows: halo[i * HALO + k, rows], gains, base)
-    gains = gains_of(own)
-
-    def step(x):
-        plane(x + HALO, lambda i, rows: basis_ref[i, x, rows], gains, before(x, None))
-
-    planes_in_groups(0, planes, 4, step)
+            base = None if before is None else before[k]
+            prolong_plane(state, wide + k, lambda i, rows: halo[i * HALO + k, rows], gains, base)
 
 
 def pulled(coef_ref, state, x):
@@ -350,23 +357,37 @@
     return (total - OMEGA * here) * coef_ref[x, 7]
 
 
-def second_kernel(
-    count, basis_hbm, gathered_ref, inverse_ref, near_ref, far_ref, *refs
+def coarse_kernel(
+    count, basis_hbm, half_ref, other_ref, inverse_ref, _room, _more_room,
+    corrected_ref, coupling_ref, spread_ref, window_s, basis_ref, sems,
 ):
-    statics, refs = refs[:6], refs[8:]
-    pressure_ref, coupling_ref, send_near_hbm, send_far_hbm, packed_hbm = refs[:5]
-    coef_ref, one_s, two_s, tx_s, window_s, tail_s, basis_ref, sems = refs[5:]
+    me = lax.axis_index("gx")
+    load = started(((basis_hbm, basis_ref),), sems)
+    blocks_in_order((half_ref, other_ref), coupling_ref, me)
+    core = lax.rem(me, 2)
+    pieces = []
+    for chip in range(count // 2):
+        rows = pl.ds(chip * PER, PER), pl.ds(KROWS, 128)
+        pieces.append((2 * chip + core, half_ref[rows]))
+        pieces.append((2 * chip + 1 - core, other_ref[rows]))
+    spread = corrected_values(coupling_ref, inverse_ref, window_of(pieces, window_s, me))
+    spread_ref[...] = spread
+    load[0].wait()
+    prolong_own(corrected_ref, 0, spread, basis_ref)
+
+
+def second_kernel(count, basis_hbm, spread_ref, near_ref, far_ref, corrected_ref, *refs):
+    statics, refs = refs[:6], refs[6:]
+    pressure_ref, send_near_hbm, send_far_hbm, packed_hbm = refs[:4]
+    coef_ref, one_s, two_s, tx_s, tail_s, basis_ref, sems = refs[4:]
     load = started(((basis_hbm, basis_ref),), sems, 2 + count)
     planes = pressure_ref.shape[0]
     me = lax.axis_index("gx")
     even = lax.rem(me, 2) == 0
-    blocks_in_order(gathered_ref, coupling_ref, me, count)
-    spread = corrected_values(
-        coupling_ref, inverse_ref, window_of(gathered_ref, window_s, me, count, KROWS)
-    )
+    for x in range(planes):
+        one_s[x + HALO] = corrected_ref[x]
+    prolong_halo(one_s, spread_ref[...], near_ref, far_ref, even, planes)
     all_coefficients(coef_ref, near_ref, far_ref, statics, tx_s, even)
-    load[0].wait()
-    prolong(one_s, spread, basis_ref, near_ref, far_ref, even, planes, lambda k, near: None)
     source, target = smooth(coef_ref, one_s, two_s, planes)
     near_from, far_from = jnp.where(even, planes, HALO), jnp.where(even, HALO, planes)
     stores = started(
@@ -382,6 +403,7 @@
         target[x] = misfit(coef_ref, source, x)
 
     planes_in_groups(HALO, planes + HALO, 8, step)
+    load[0].wait()
     coarse = restrict_to(lambda i, x: basis_ref[i, x], lambda x: target[x + HALO], planes)
     tail_s[...] = jnp.concatenate([coarse, jnp.zeros((PER, 128 - NBF), F32)], axis=1)
     stores += started([(tail_s, packed_hbm.at[e]) for e in range(count)], sems, 2)
@@ -399,18 +421,13 @@
     planes = pressure_ref.shape[0]
     me = lax.axis_index("gx")
     even = lax.rem(me, 2) == 0
-    spread = corrected_values(
-        coupling_ref, inverse_ref, window_of(gathered_ref, window_s, me, count, 0)
-    )
-
-    def before(k, near):
-        if near is None:
-            return pressure_ref[k]
-        return near_p_ref[k] if near else far_p_ref[k]
+    pieces = [(device, gathered_ref[device]) for device in range(count)]
+    spread = corrected_values(coupling_ref, inverse_ref, window_of(pieces, window_s, me))
 
     all_coefficients(coef_ref, near_ref, far_ref, statics, tx_s, even)
     load[0].wait()
-    prolong(one_s, spread, basis_ref, near_ref, far_ref, even, planes, before)
+    prolong_own(one_s, HALO, spread, basis_ref, pressure_ref)
+    prolong_halo(one_s, spread, near_ref, far_ref, even, planes, near_p_ref, far_p_ref)
     source, _ = smooth(coef_ref, one_s, two_s, planes)
     stores = started(((source.at[pl.ds(HALO, planes)], pressure_out),), sems)
     half = planes // 2
@@ -462,9 +479,9 @@
 
     near, far, packed = kernel_call(
         "restrict_first",
-        functools.partial(first_kernel, count),
+        first_kernel,
         [(H, owned_block), (H, basis), *statics, (H, coupling.reshape(KROWS, PER))],
-        [(H, halo, BF16), (H, halo, BF16), (H, (count, PER, KROWS + 128), F32)],
+        [(H, halo, BF16), (H, halo, BF16), (H, (count // 2, PER, KROWS + 128), F32)],
         [
             pltpu.SMEM(owned_block.shape, jnp.int32),
             pltpu.VMEM(basis.shape, BF16),
@@ -473,13 +490,11 @@
             pltpu.VMEM((KROWS, PER), F32),
             pltpu.VMEM((PER, KROWS + 128), F32),
             pltpu.VMEM((2,) + halo, BF16),
-            pltpu.SemaphoreType.DMA((20 + count,)),
+            pltpu.SemaphoreType.DMA((24 + count // 2,)),
         ],
     )
     far = lax.ppermute(far, "gx", far_pairs)
     near = lax.ppermute(near, "gx", near_pairs)
-    gathered = lax.all_to_all(packed, "gx", 0, 0, tiled=True)
-
     blocks = coarse_inverse.shape[2]
     *fields, inverse, room, more_room = kernel_call(
         "prepare",
@@ -495,26 +510,43 @@
         ],
     )
 
+    chips = [[core + 2 * chip for chip in range(count // 2)] for core in range(2)]
+    half = lax.all_to_all(packed, "gx", 0, 0, axis_index_groups=chips, tiled=True)
+    half = half.reshape(count // 2 * PER, KROWS + 128)
+    half, near, fields = lax.optimization_barrier((half, near, fields))
+    parts = [half, lax.ppermute(half, "gx", near_pairs)]
+
     factors = pltpu.VMEM((full, 8) + field, F32)
     state = pltpu.VMEM((full,) + field, F32)
     window = pltpu.VMEM((count * PER + WIN, 128), F32)
     around = pltpu.VMEM((full,) + field, BF16)
-    pressure, coupled, send_near, send_far, packed = kernel_call(
+    corrected, coupled, spread = kernel_call(
+        "coarse_first",
+        functools.partial(coarse_kernel, count),
+        [(H, basis)] + [(V, a) for a in (*parts, inverse, room, more_room)],
+        [
+            (V, (planes,) + field, F32),
+            (V, (KROWS, WIN), F32),
+            (V, (NBF, 3 * NYB * nz), F32),
+        ],
+        [window, pltpu.VMEM(basis.shape, BF16), pltpu.SemaphoreType.DMA((1,))],
+        {4: 0, 5: 1},
+    )
+    pressure, send_near, send_far, packed = kernel_call(
         "iteration_first",
         functools.partial(second_kernel, count),
-        [(H, basis)] + [(V, a) for a in (gathered, inverse, near, far, *fields, room, more_room)],
+        [(H, basis)] + [(V, a) for a in (spread, near, far, corrected, *fields)],
         [
             (V, (planes,) + field, F32),
-            (V, (KROWS, WIN), F32),
             (H, (HALO,) + field, F32),
             (H, (HALO,) + field, F32),
             (H, (count, PER, 128), F32),
         ],
         [
-            factors, state, state, around, window,
+            factors, state, state, around,
             pltpu.VMEM((PER, 128), F32), pltpu.VMEM(basis.shape, BF16), pltpu.SemaphoreType.DMA((3 + count,)),
         ],
-        {11: 0, 12: 1},
+        {4: 0},
     )
 
     far_p = lax.ppermute(send_far, "gx", far_pairs)

time: 51.3 us -> 46.3 us (0.903)
  waiting for transfers between devices: 18.8 us -> 15.3 us
  starting transfers between devices: 18.3 us -> 16.3 us
    all_to_all x2 -> x1, waiting for transfers between devices: 18.5 us -> 6.55 us  [local(): gathered = lax.all_to_all(packed, 'gx', 0, 0, tiled=True)]
    all_to_all x2 -> x1, starting transfers between devices: 16.1 us -> 7.07 us  [local(): gathered = lax.all_to_all(packed, 'gx', 0, 0, tiled=True)]
    all_to_all x0 -> x1, starting transfers between devices: none -> 7.42 us  [local(): lax.all_to_all(packed, 'gx', 0, 0, axis_index_groups=chips, tiled=True)]
    all_to_all x0 -> x1, waiting for transfers between devices: none -> 6.95 us  [local(): lax.all_to_all(packed, 'gx', 0, 0, axis_index_groups=chips, tiled=True)]
    ppermute x0 -> x1, waiting for transfers between devices: none -> 1.53 us  [local(): parts = [half, lax.ppermute(half, 'gx', near_pairs)]]
    pallas_call x4 -> x5, Pallas kernels: 13.1 us -> 13.5 us  [kernel_call(): call(*[pltpu.with_memory_space_constraint(value, space) for space, value...]
  transfers between devices with their start and end apart: 6 -> 7, of which waited for: 3 -> 4; matrix products, arithmetic and copies ran while one was open for 0% -> 0% of each run, Pallas kernels for 3% -> 8%
where the time goes in v3:
time: 46.3 us; the launch traced here: 45.8 us
  starting transfers between devices  16.3 us (35%)
  waiting for transfers between devices  15.3 us (33%)
  Pallas kernels  13.5 us (29%)
  between operations  0.75 us (2%)
    pallas_call x5, Pallas kernels, kernel_call(): call(*[pltpu.with_memory_space_constraint(value, space) for space, value...  13.5 us
    all_to_all x1, starting transfers between devices, local(): lax.all_to_all(packed, 'gx', 0, 0, axis_index_groups=chips, tiled=True)  7.42 us
    all_to_all x1, starting transfers between devices, local(): gathered = lax.all_to_all(packed, 'gx', 0, 0, tiled=True)  7.07 us
    all_to_all x1, waiting for transfers between devices, local(): lax.all_to_all(packed, 'gx', 0, 0, axis_index_groups=chips, tiled=True)  6.95 us
    all_to_all x1, waiting for transfers between devices, local(): gathered = lax.all_to_all(packed, 'gx', 0, 0, tiled=True)  6.55 us
    ppermute x1, waiting for transfers between devices, local(): parts = [half, lax.ppermute(half, 'gx', near_pairs)]  1.53 us
  transfers between devices with their start and end apart: 7, of which 4 were waited for; matrix products, arithmetic and copies ran while one was open for 0% of the time, Pallas kernels for 8%

profile of v3, /device:TPU:0, one launch (start us, length us, event | category | flops | bytes accessed | tf_op | source)
XLA Modules:
  0.0 45.8 jit_solution(9113517855180207307)
XLA Ops:
  0.6 2.9 %restrict_first.1 = (bf16[54,32,128]{2,1,0:T(8,128)(2,1)}, bf16[54,32,128]{2,1,0:T(8,128)(2,1)}, f32[8,16,512]{2,1,0:T(8,128)}) custom-call(s32[256]{0:T(256)} %owned_hbm.1, bf16[8,16,32,128]{3,2,1,0:T(8,128)(2,1)} %basis_hbm.7, f32[16,32,128]{2,1,0:T(8,128)} %right_hbm.3, s32[16,32,128]{2,1,0:T(8,128)} %wet_hbm.3, bf16[16,32,128]{2,1,0:T(8,128)(2,1)} %tx_hbm.3, ...), custom_call_target="tpu_custom_call" | custom-call | tf_op jit(solution)/shard_map/restrict_first/pallas_call | solution.py:462
  3.6 0.0 copy-start
  3.6 7.4 %all-to-all-start = ((f32[8,16,512]{2,1,0:T(8,128)}), f32[8,16,512]{2,1,0:T(8,128)S(1)}, u32[]{:S(2)}, u32[]{:S(2)}) async-start(f32[8,16,512]{2,1,0:T(8,128)} %get-tuple-element.29), calls=%async_computation | async-start | bytes 524288 | tf_op jit(solution)/shard_map/all_to_all | solution.py:514
  11.0 0.0 collective-permute-start
  11.0 0.0 copy-done
  11.0 0.7 %collective-permute-start.2 = (bf16[54,32,128]{2,1,0:T(8,128)(2,1)S(1)}, bf16[54,32,128]{2,1,0:T(8,128)(2,1)S(1)}, u32[]{:S(2)}, u32[]{:S(2)}) collective-permute-start(bf16[54,32,128]{2,1,0:T(8,128)(2,1)S(1)} %copy-done), channel_id=1, source_target_pairs={{1,2},{3,4},{5,6},{7,8},{9,10},{11,12},{13,14},{2,1},{4,3},{6,5},{... | collective-permute-start | bytes 1327112 | tf_op jit(solution)/shard_map/ppermute | solution.py:496
  11.7 1.3 %prepare.1 = (f32[16,32,128]{2,1,0:T(8,128)S(1)}, bf16[16,32,128]{2,1,0:T(8,128)(2,1)S(1)}, bf16[16,32,128]{2,1,0:T(8,128)(2,1)S(1)}, bf16[16,32,128]{2,1,0:T(8,...) custom-call(f32[16,32,128]{2,1,0:T(8,128)} %right_hbm.3, ...), custom_call_target="tpu_custom_call" | custom-call | tf_op jit(solution)/shard_map/prepare/pallas_call | solution.py:462
  13.1 0.0 collective-permute-done.near_ref
  13.1 6.9 %all-to-all-done = f32[8,16,512]{2,1,0:T(8,128)S(1)} async-done(((f32[8,16,512]{2,1,0:T(8,128)}), f32[8,16,512]{2,1,0:T(8,128)S(1)}, u32[]{:S(2)}, u32[]{:S(2)}) %all-to-all-start) | async-done | bytes 262176 | tf_op jit(solution)/shard_map/all_to_all | solution.py:514
  20.0 0.0 collective-permute-start.1
  20.0 1.5 %collective-permute-done.1.other_ref = f32[128,512]{1,0:T(8,128)S(1)} collective-permute-done((f32[128,512]{1,0:T(8,128)S(1)}, f32[128,512]{1,0:T(8,128)S(1)}, u32[]{:S(2)}, u32[]{:S(2)}) %collective-permute-start.1) | collective-permute-done | bytes 262176 | tf_op jit(solution)/shard_map/ppermute | solution.py:517
  21.6 2.2 %coarse_first.1 = (f32[16,32,128]{2,1,0:T(8,128)S(1)}, f32[384,256]{1,0:T(8,128)S(1)}, f32[8,768]{1,0:T(8,128)S(1)}) custom-call(bf16[8,16,32,128]{3,2,1,0:T(8,128)(2,1)} %basis_hbm.7, f32[128,512]{1,0:T(8,128)S(1)} %bitcast.4, f32[128,512]{1,0:T(8,128)S(1)} %collective-permute-done.1.other_ref, ...), custom_call_target="tpu_custom_call", output_to_operand_aliasing={{0}: (4, {}), {1}: (5, {})} | custom-call | tf_op jit(solution)/shard_map/coarse_first/pallas_call | solution.py:462
  23.7 0.0 collective-permute-done.2.far_ref
  23.7 3.2 %iteration_first.1 = (f32[16,32,128]{2,1,0:T(8,128)S(1)}, f32[4,32,128]{2,1,0:T(8,128)}, f32[4,32,128]{2,1,0:T(8,128)}, f32[16,16,128]{2,1,0:T(8,128)}) custom-call(bf16[8,16,32,128]{3,2,1,0:T(8,128)(2,1)} %basis_hbm.7, f32[8,768]{1,0:T(8,128)S(1)} %get-tuple-element.41.spread_ref, ...), custom_call_target="tpu_custom_call", output_to_operand_aliasing={{0}: (4, {})} | custom-call | tf_op jit(solution)/shard_map/iteration_first/pallas_call | solution.py:462
  26.9 0.0 copy-start.2
  26.9 0.0 copy-start.1
  26.9 7.1 %all-to-all-start.1 = ((f32[16,16,128]{2,1,0:T(8,128)}), f32[16,16,128]{2,1,0:T(8,128)S(1)}, u32[]{:S(2)}, u32[]{:S(2)}) async-start(f32[16,16,128]{2,1,0:T(8,128)} %get-tuple-element.51), calls=%async_computation.1 | async-start | bytes 262144 | tf_op jit(solution)/shard_map/all_to_all | solution.py:554
  34.0 0.0 copy-done.2
  34.0 0.5 %collective-permute-start.3 = (f32[4,32,128]{2,1,0:T(8,128)S(1)}, f32[4,32,128]{2,1,0:T(8,128)S(1)}, u32[]{:S(2)}, u32[]{:S(2)}) collective-permute-start(f32[4,32,128]{2,1,0:T(8,128)S(1)} %copy-done.2), channel_id=1, source_target_pairs={{0,1},{1,0},{2,3},{3,2},{4,5},{5,4},{6,7},{7,6},{8,9},{9,8},{10,11... | collective-permute-start | bytes 196616 | tf_op jit(solution)/shard_map/ppermute | solution.py:553
  34.5 0.7 %collective-permute-start.4 = (f32[4,32,128]{2,1,0:T(8,128)S(1)}, f32[4,32,128]{2,1,0:T(8,128)S(1)}, u32[]{:S(2)}, u32[]{:S(2)}) collective-permute-start(f32[4,32,128]{2,1,0:T(8,128)S(1)} %copy-done.1), channel_id=1, source_target_pairs={{1,2},{3,4},{5,6},{7,8},{9,10},{11,12},{13,14},{2,1},{4,3},{6,5},{... | collective-permute-start | bytes 196616 | tf_op jit(solution)/shard_map/ppermute | solution.py:552
  35.2 0.2 collective-permute-done.3.near_p_ref
  35.4 0.0 collective-permute-done.4.far_p_ref
  35.4 6.5 %all-to-all-done.1.gathered_ref = f32[16,16,128]{2,1,0:T(8,128)S(1)} async-done(((f32[16,16,128]{2,1,0:T(8,128)}), f32[16,16,128]{2,1,0:T(8,128)S(1)}, u32[]{:S(2)}, u32[]{:S(2)}) %all-to-all-start.1) | async-done | bytes 131104 | tf_op jit(solution)/shard_map/all_to_all | solution.py:554
  42.0 3.9 %iteration_last.1 = (f32[16,32,128]{2,1,0:T(8,128)}, f32[16,32,128]{2,1,0:T(8,128)}) custom-call(bf16[8,16,32,128]{3,2,1,0:T(8,128)(2,1)} %basis_hbm.7, f32[16,16,128]{2,1,0:T(8,128)S(1)} %all-to-all-done.1.gathered_ref, f32[64,256]{1,0:T(8,128)S(1)} %get-tuple-element.38.inverse_ref, bf16[54,32,128]{2,1,0:T(8,128)(2,1)S(1)} %collective-permute-done.near_ref, ...), custom_call_target="tpu_custom_call" | custom-call | tf_op jit(solution)/shard_map/iteration_last/pallas_call | solution.py:462
  (1 shorter events, 0.0 us)
Async XLA Ops:
  3.6 7.4 %copy-start = (bf16[54,32,128]{2,1,0:T(8,128)(2,1)S(1)}, bf16[54,32,128]{2,1,0:T(8,128)(2,1)}, u32[]{:S(2)}) copy-start(bf16[54,32,128]{2,1,0:T(8,128)(2,1)} %get-tuple-element.43) | copy-start | bytes 1327108
  3.6 16.5 %all-to-all-start = ((f32[8,16,512]{2,1,0:T(8,128)}), f32[8,16,512]{2,1,0:T(8,128)S(1)}, u32[]{:S(2)}, u32[]{:S(2)}) async-start(f32[8,16,512]{2,1,0:T(8,128)} %get-tuple-element.29), calls=%async_computation | async-start | bytes 524288 | tf_op jit(solution)/shard_map/all_to_all | solution.py:514
  11.0 2.1 %collective-permute-start = (bf16[54,32,128]{2,1,0:T(8,128)(2,1)}, bf16[54,32,128]{2,1,0:T(8,128)(2,1)S(1)}, u32[]{:S(2)}, u32[]{:S(2)}) collective-permute-start(bf16[54,32,128]{2,1,0:T(8,128)(2,1)} %get-tuple-element.30), channel_id=1, source_target_pairs={{0,1},{1,0},{2,3},{3,2},{4,5},{5,4},{6,7},{7,6},{8,9},{9,8},{10,11... | collective-permute-start | bytes 1327112 | tf_op jit(solution)/shard_map/ppermute | solution.py:497
  11.0 12.7 %collective-permute-start.2 = (bf16[54,32,128]{2,1,0:T(8,128)(2,1)S(1)}, bf16[54,32,128]{2,1,0:T(8,128)(2,1)S(1)}, u32[]{:S(2)}, u32[]{:S(2)}) collective-permute-start(bf16[54,32,128]{2,1,0:T(8,128)(2,1)S(1)} %copy-done), channel_id=1, source_target_pairs={{1,2},{3,4},{5,6},{7,8},{9,10},{11,12},{13,14},{2,1},{4,3},{6,5},{... | collective-permute-start | bytes 1327112 | tf_op jit(solution)/shard_map/ppermute | solution.py:496
  20.0 1.5 %collective-permute-start.1 = (f32[128,512]{1,0:T(8,128)S(1)}, f32[128,512]{1,0:T(8,128)S(1)}, u32[]{:S(2)}, u32[]{:S(2)}) collective-permute-start(f32[128,512]{1,0:T(8,128)S(1)} %bitcast.3), channel_id=1, source_target_pairs={{0,1},{1,0},{2,3},{3,2},{4,5},{5,4},{6,7},{7,6},{8,9},{9,8},{10,11... | collective-permute-start | bytes 786440 | tf_op jit(solution)/shard_map/ppermute | solution.py:517
  26.9 7.1 %copy-start.2 = (f32[4,32,128]{2,1,0:T(8,128)S(1)}, f32[4,32,128]{2,1,0:T(8,128)}, u32[]{:S(2)}) copy-start(f32[4,32,128]{2,1,0:T(8,128)} %get-tuple-element.54) | copy-start | bytes 196612
  26.9 7.6 %copy-start.1 = (f32[4,32,128]{2,1,0:T(8,128)S(1)}, f32[4,32,128]{2,1,0:T(8,128)}, u32[]{:S(2)}) copy-start(f32[4,32,128]{2,1,0:T(8,128)} %get-tuple-element.55) | copy-start | bytes 196612
  26.9 15.0 %all-to-all-start.1 = ((f32[16,16,128]{2,1,0:T(8,128)}), f32[16,16,128]{2,1,0:T(8,128)S(1)}, u32[]{:S(2)}, u32[]{:S(2)}) async-start(f32[16,16,128]{2,1,0:T(8,128)} %get-tuple-element.51), calls=%async_computation.1 | async-start | bytes 262144 | tf_op jit(solution)/shard_map/all_to_all | solution.py:554
  34.0 1.4 %collective-permute-start.3 = (f32[4,32,128]{2,1,0:T(8,128)S(1)}, f32[4,32,128]{2,1,0:T(8,128)S(1)}, u32[]{:S(2)}, u32[]{:S(2)}) collective-permute-start(f32[4,32,128]{2,1,0:T(8,128)S(1)} %copy-done.2), channel_id=1, source_target_pairs={{0,1},{1,0},{2,3},{3,2},{4,5},{5,4},{6,7},{7,6},{8,9},{9,8},{10,11... | collective-permute-start | bytes 196616 | tf_op jit(solution)/shard_map/ppermute | solution.py:553
  34.5 0.9 %collective-permute-start.4 = (f32[4,32,128]{2,1,0:T(8,128)S(1)}, f32[4,32,128]{2,1,0:T(8,128)S(1)}, u32[]{:S(2)}, u32[]{:S(2)}) collective-permute-start(f32[4,32,128]{2,1,0:T(8,128)S(1)} %copy-done.1), channel_id=1, source_target_pairs={{1,2},{3,4},{5,6},{7,8},{9,10},{11,12},{13,14},{2,1},{4,3},{6,5},{... | collective-permute-start | bytes 196616 | tf_op jit(solution)/shard_map/ppermute | solution.py:552

commit v4 on v3

v4 whole, which is shorter than its diff:
```python
import functools

import jax
import jax.numpy as jnp
from jax import lax
from jax.experimental import pallas as pl
from jax.experimental.pallas import tpu as pltpu
from jax.sharding import PartitionSpec as P

BLK = 16
NBF = 8
NNB = 6
SWEEPS = 3
CSWEEPS = 4
NYB = 2
NZB = 8
PER = NYB * NZB
WIN = 16 * PER
LEAD = 4
HALO = 4
OMEGA = 2.0 / 3.0
KROWS = NNB * NBF * NBF
ROWS = (KROWS // 128 * 2 + 1) * 8
F32 = jnp.float32
BF16 = jnp.bfloat16


THIN = HALO - 1
H_TX = NBF * HALO
H_REST = H_TX + HALO
H_WET = H_REST + 3 * THIN
H_ALL = H_REST + 6 * THIN


def planes_in_groups(low, high, group, step):
    count = (high - low) // group

    def body(k, carry):
        for j in range(group):
            step(low + k * group + j)
        return carry

    if count > 1:
        lax.fori_loop(0, count, body, 0)
    elif count:
        body(0, 0)
    for x in range(low + count * group, high):
        step(x)


def three_parts(x):
    high = x.astype(BF16)
    rest = x - high.astype(F32)
    middle = rest.astype(BF16)
    low = (rest - middle.astype(F32)).astype(BF16)
    return high, middle, low


def restrict_totals(basis_at, field_at, low, high, totals=None):
    def step(x, totals):
        field = field_at(x)
        out = []
        for i in range(NBF):
            for yb in range(NYB):
                rows = slice(yb * BLK, (yb + 1) * BLK)
                product = basis_at(i, x)[rows].astype(F32) * field[rows]
                out.append(totals[i * NYB + yb] + product[:8] + product[8:])
        return tuple(out)

    if totals is None:
        totals = (jnp.zeros((8, 128), F32),) * (NBF * NYB)
    return lax.fori_loop(low, high, step, tuple(totals))


def restricted(totals):
    groups = lax.broadcasted_iota(jnp.int32, (NZB, 3 * 128), 1)
    owner = lax.broadcasted_iota(jnp.int32, (NZB, 3 * 128), 0)
    spread = ((groups % 128) // BLK == owner).astype(F32).astype(BF16)
    halves = []
    for yb in range(NYB):
        rows = [jnp.sum(totals[i * NYB + yb], axis=0, keepdims=True) for i in range(NBF)]
        stacked = jnp.concatenate(three_parts(jnp.concatenate(rows, 0)), axis=1)
        halves.append(
            lax.dot_general(
                spread, stacked, (((1,), (1,)), ((), ())), preferred_element_type=F32
            )
        )
    return halves


def restricted_tile(totals, first):
    block = lax.broadcasted_iota(jnp.int32, (128, 128), 0) // BLK + first
    lane = lax.broadcasted_iota(jnp.int32, (128, 128), 1)
    tile = 0.0
    for yb in range(NYB):
        rows = [jnp.sum(totals[i * NYB + yb], axis=0, keepdims=True) for i in range(NBF)]
        stacked = jnp.concatenate(three_parts(jnp.concatenate(rows, 0)), axis=0)
        chosen = (lane == block + yb * NZB).astype(F32).astype(BF16)
        tile = tile + jnp.dot(stacked, chosen, preferred_element_type=F32)
    return tile[:NBF] + tile[NBF : 2 * NBF] + tile[2 * NBF :]


def lane_of(device):
    return lax.rem(device, 128 // PER) * PER


def window_of_tiles(gathered_ref, me):
    count = gathered_ref.shape[0]
    halves = []
    for half in range(WIN // 128):
        total = 0.0
        for w in range(128 // PER):
            device = me - LEAD + half * (128 // PER) + w
            inside = (device >= 0) & (device < count)
            total = total + jnp.where(inside, gathered_ref[jnp.clip(device, 0, count - 1)], 0.0)
        halves.append(pltpu.roll(total, lax.rem(128 - lane_of(me + 128 // PER - LEAD), 128), 1))
    return jnp.concatenate(halves, axis=1)


def started(pairs, sems, first=0):
    copies = [pltpu.make_async_copy(a, b, sems.at[first + k]) for k, (a, b) in enumerate(pairs)]
    for copy in copies:
        copy.start()
    return copies


def is_even():
    return lax.rem(lax.axis_index("gx"), 2) == 0


def plane_at(place, planes):
    return jnp.where(is_even(), place, planes - 1 - place)


def first_kernel(
    owned_hbm, basis_hbm, right_hbm, wet_hbm, tx_hbm, ty_hbm, tz_hbm, st_hbm, coupling_hbm, all_inverse_hbm,
    near_hbm, far_hbm, packed_hbm, *rest
):
    field_refs, inverse_ref, rest = rest[:6], rest[6], rest[9:]
    (
        owned_s, basis_s, right_s, wet_s, tx_s, ty_s, tz_s, st_s, coupling_s, all_inverse, rows_s, halo_s, sems
    ) = rest
    me = lax.axis_index("gx")
    planes = right_s.shape[0]
    wides = [[plane_at(HALO - 1 - k, planes) for k in range(HALO)], [plane_at(planes - 1 - k, planes) for k in range(HALO)]]
    thins = [wides[0][1:], wides[1][:THIN]]
    quarter = planes // 4
    spans = [pl.ds(k * quarter, quarter) for k in (0, 3, 1, 2)]
    pairs = [(right_hbm, right_s)] + [(basis_hbm.at[:, span], basis_s.at[:, span]) for span in spans[:2]]
    pairs += list(zip((wet_hbm, tx_hbm, ty_hbm, tz_hbm, st_hbm), (wet_s, tx_s, ty_s, tz_s, st_s)))
    edge = len(pairs)
    pairs += [(basis_hbm.at[:, span], basis_s.at[:, span]) for span in spans[2:]]
    pairs += [(owned_hbm, owned_s), (coupling_hbm, coupling_s), (all_inverse_hbm, all_inverse)]
    loads = started(pairs, sems)

    def basis_at(i, x):
        return basis_s[i, x]

    def right_at(x):
        return right_s[x]

    loads[0].wait()
    totals = None
    for k in (0, 3):
        loads[1 + k // 3].wait()
        totals = restrict_totals(basis_at, right_at, k * quarter, (k + 1) * quarter, totals)
    for copy in loads[3:edge]:
        copy.wait()
    stores = []
    for side in range(2):
        for k in range(HALO):
            for i in range(NBF):
                halo_s[side, i * HALO + k] = basis_s[i, wides[side][k]]
            halo_s[side, H_TX + k] = tx_s[wides[side][k]]
        for k, x in enumerate(thins[side]):
            for j, field in enumerate((ty_s, tz_s, st_s)):
                halo_s[side, H_REST + j * THIN + k] = field[x]
            right = right_s[x]
            high = right.astype(BF16)
            halo_s[side, H_WET + k] = wet_s[x].astype(F32).astype(BF16)
            halo_s[side, H_WET + THIN + k] = high
            halo_s[side, H_WET + 2 * THIN + k] = (right - high.astype(F32)).astype(BF16)
        stores += started(
            ((halo_s.at[side], (far_hbm, near_hbm)[side]),), sems, len(loads) + side
        )
    for k in (1, 2):
        loads[edge + k - 1].wait()
        totals = restrict_totals(basis_at, right_at, k * quarter, (k + 1) * quarter, totals)
    for copy in loads[edge + 2 :]:
        copy.wait()
    slot = lax.broadcasted_iota(jnp.int32, (8, 1), 0)
    parts = []
    for half, coarse in enumerate(restricted(totals)):
        block = jnp.zeros((8, 1), jnp.int32)
        for s in range(8):
            block = jnp.where(slot == s, owned_s[me * PER + half * 8 + s], block)
        parts += [coarse, block.astype(F32), jnp.zeros((8, 64 - NBF - 1), F32)]
    wide = jnp.concatenate([coupling_s[...], jnp.zeros((KROWS, 128 - PER), F32)], axis=1).T
    for r in range(2):
        for l in range(KROWS // 128):
            rows_s[pl.ds((r * (KROWS // 128) + l) * 8, 8)] = wide[r * 8 : r * 8 + 8, l * 128 : l * 128 + 128]
    rows_s[pl.ds(ROWS - 8, 8)] = jnp.concatenate(parts, axis=1)
    stores += started(
        [(rows_s, packed_hbm.at[chip]) for chip in range(packed_hbm.shape[0])], sems, len(loads) + 2
    )

    def place_fields(place):
        x = plane_at(place, planes)
        for source, target in zip((right_s, wet_s, tx_s, ty_s, tz_s, st_s), field_refs):
            plane = source[x]
            target[place] = plane.astype(F32).astype(BF16) if source is wet_s else plane

    planes_in_groups(0, planes, 4, place_fields)
    blocks = all_inverse.shape[1]
    start = (me - LEAD) * PER
    turned = pltpu.roll(all_inverse[...], lax.rem(blocks - start, blocks), 1)[:, :WIN]
    block = lax.broadcasted_iota(jnp.int32, turned.shape, 1) + start
    inverse_ref[...] = jnp.where((block >= 0) & (block < blocks), turned, 0.0)
    for copy in stores:
        copy.wait()


def coarse_solve(coupling_at, inverse_at, residual):
    lane = lax.broadcasted_iota(jnp.int32, (NBF, WIN), 1)
    in_z, in_y = lane % NZB, (lane // NZB) % NYB

    def rows_of(parts):
        return jnp.concatenate([jnp.sum(p, axis=0, keepdims=True) for p in parts], 0)

    def inverted(v):
        return rows_of([inverse_at(i) * v for i in range(NBF)])

    values = inverted(residual)
    for _ in range(CSWEEPS - 1):
        near = (
            pltpu.roll(values, WIN - PER, 1),
            pltpu.roll(values, PER, 1),
            jnp.where(in_y < NYB - 1, pltpu.roll(values, WIN - NZB, 1), 0.0),
            jnp.where(in_y > 0, pltpu.roll(values, NZB, 1), 0.0),
            jnp.where(in_z < NZB - 1, pltpu.roll(values, WIN - 1, 1), 0.0),
            jnp.where(in_z > 0, pltpu.roll(values, 1, 1), 0.0),
        )
        parts = []
        for i in range(NBF):
            total = coupling_at(0, i) * near[0]
            for k in range(1, NNB):
                total = total + coupling_at(k, i) * near[k]
            parts.append(total)
        values = inverted(residual - rows_of(parts))
    return values


def spread_blocks(values):
    width = 3 * NYB * 128
    block = lax.broadcasted_iota(jnp.int32, (128, width), 0)
    column = lax.broadcasted_iota(jnp.int32, (128, width), 1)
    wanted = (LEAD - 1) * PER + column // BLK
    chosen = (block == wanted).astype(F32).astype(BF16)
    stacked = jnp.concatenate(three_parts(values[:, :128]), axis=0)
    spread = jnp.dot(stacked, chosen, preferred_element_type=F32)
    return spread[:NBF] + spread[NBF : 2 * NBF] + spread[2 * NBF :]


def coefficients(coef_ref, x, quarters, right, east, west, north, upper, storage):
    in_y = lax.broadcasted_iota(jnp.int32, north.shape, 0)
    in_z = lax.broadcasted_iota(jnp.int32, north.shape, 1)
    last_y, last_z = north.shape[0] - 1, north.shape[1] - 1
    east, west, north, upper = (a.astype(F32) for a in (east, west, north, upper))
    wet = quarters * 0.25
    dry = 1.0 - jnp.minimum(quarters, 1.0)
    south = jnp.where(in_y > 0, pltpu.roll(north, 1, 0), 0.0)
    lower = jnp.where(in_z > 0, pltpu.roll(upper, 1, 1), 0.0)
    diag = wet * (storage.astype(F32) + east + west + north + south + upper + lower) + dry
    share = OMEGA / diag
    scale = wet * share
    coef_ref[x, 0] = scale * east
    coef_ref[x, 1] = scale * west
    coef_ref[x, 2] = jnp.where(in_y < last_y, scale * north, 0.0)
    coef_ref[x, 3] = scale * south
    coef_ref[x, 4] = jnp.where(in_z < last_z, scale * upper, 0.0)
    coef_ref[x, 5] = scale * lower
    coef_ref[x, 6] = right * share
    coef_ref[x, 7] = diag * (1.0 / OMEGA)


def all_coefficients(coef_ref, near_ref, far_ref, statics, tx_s, low, high):
    right_ref, wet_ref, tx_ref, ty_ref, tz_ref, st_ref = statics
    top = right_ref.shape[0] + HALO
    tx_s[pl.ds(HALO, top - HALO)] = tx_ref[...]
    if near_ref is not None:
        tx_s[pl.ds(top, HALO)] = near_ref[pl.ds(H_TX, HALO)]
    if far_ref is not None:
        tx_s[pl.ds(0, HALO)] = far_ref[pl.ds(H_TX, HALO)]
    turn = jnp.where(is_even(), 0, 1)

    def plane(u, quarters, right, north, upper, storage):
        coefficients(
            coef_ref, u, quarters.astype(F32), right, tx_s[u + turn], tx_s[u - 1 + turn], north, upper, storage
        )

    def own(u):
        x = u - HALO
        plane(u, wet_ref[x], right_ref[x], ty_ref[x], tz_ref[x], st_ref[x])

    def outside(u, halo, k):
        right = halo[H_WET + THIN + k].astype(F32) + halo[H_WET + 2 * THIN + k].astype(F32)
        plane(u, halo[H_WET + k], right, halo[H_REST + k], halo[H_REST + THIN + k], halo[H_REST + 2 * THIN + k])

    for u in range(low, HALO):
        outside(u, far_ref, u - 1)
    planes_in_groups(max(low, HALO), min(high, top), 8, own)
    for u in range(top, high):
        outside(u, near_ref, u - top)


def window_of(pieces, window_s, me):
    window_s[...] = jnp.zeros_like(window_s)
    for device, piece in pieces:
        window_s[pl.ds(pl.multiple_of((LEAD + device) * PER, PER), PER)] = piece
    return window_s[pl.ds(pl.multiple_of(me * PER, PER), WIN)].T[:NBF]


def blocks_in_order(rows_s, coupling_ref, me):
    lane = lax.broadcasted_iota(jnp.int32, (WIN, WIN), 1) + (me - LEAD) * PER
    for start in range(0, rows_s.shape[0], WIN):
        rows = rows_s[pl.ds(start, WIN)]
        block = rows[:, KROWS + NBF : KROWS + NBF + 1].astype(jnp.int32)
        chosen = (block == lane).astype(F32).astype(BF16)
        stacked = jnp.concatenate(three_parts(rows[:, :KROWS].T), axis=0)
        found = jnp.dot(stacked, chosen, preferred_element_type=F32)
        found = found[:KROWS] + found[KROWS : 2 * KROWS] + found[2 * KROWS :]
        coupling_ref[...] = found if start == 0 else coupling_ref[...] + found


def corrected_values(coupling_ref, inverse_ref, residual):
    values = coarse_solve(
        lambda k, i: coupling_ref[pl.ds((k * NBF + i) * NBF, NBF)],
        lambda i: inverse_ref[pl.ds(i * NBF, NBF)],
        residual,
    )
    return spread_blocks(values)


def prolong(state, places, gains, basis_at, base_at=None):
    wide = [
        [
            jnp.broadcast_to(gains[i : i + 1, yb * 128 : (yb + 1) * 128], (BLK, 128))
            for i in range(NBF)
        ]
        for yb in range(NYB)
    ]

    def step(u):
        for yb in range(NYB):
            rows = slice(yb * BLK, (yb + 1) * BLK)
            total = basis_at(0, u, rows).astype(F32) * wide[yb][0]
            for i in range(1, NBF):
                total = total + basis_at(i, u, rows).astype(F32) * wide[yb][i]
            state[u, rows] = total if base_at is None else base_at(u)[rows] + total

    planes_in_groups(places[0], places[1], 4, step)


def gains_of(spread, side):
    width = NYB * 128
    below, own, above = (spread[:, s * width : (s + 1) * width] for s in range(3))
    if side == 0:
        return own
    return jnp.where(is_even(), below if side < 0 else above, above if side < 0 else below)


def pulled(coef_ref, state, x):
    here = state[x]
    ny, nz = here.shape
    total = coef_ref[x, 6] + coef_ref[x, 0] * state[x + 1] + coef_ref[x, 1] * state[x - 1]
    total = total + coef_ref[x, 2] * pltpu.roll(here, ny - 1, 0) + coef_ref[x, 3] * pltpu.roll(here, 1, 0)
    total = total + coef_ref[x, 4] * pltpu.roll(here, nz - 1, 1) + coef_ref[x, 5] * pltpu.roll(here, 1, 1)
    return here, total


def sweep(coef_ref, source, target, low, high):
    def step(u):
        here, total = pulled(coef_ref, source, u)
        target[u] = (1.0 - OMEGA) * here + total

    planes_in_groups(low, high, high - low, step)


def misfit(coef_ref, source, x):
    here, total = pulled(coef_ref, source, x)
    return (total - OMEGA * here) * coef_ref[x, 7]


def body_kernel(
    basis_hbm, half_ref, other_ref, inverse_ref, near_ref, *refs
):
    statics, refs = refs[:6], refs[8:]
    pressure_ref, coupling_ref, spread_ref, one_out, two_out, totals_ref, edge_basis, send_near_hbm = refs[:8]
    rows_s, window_s, basis_ref, coef_ref, one_s, two_s, tx_s, sems = refs[8:]
    planes = pressure_ref.shape[0]
    top = planes + HALO
    me = lax.axis_index("gx")
    load = started(((basis_hbm, basis_ref),), sems)[0]
    core = lax.rem(me, 2)
    chips = half_ref.shape[0]

    def unpack(chip, carry):
        for ref, device in ((half_ref, 2 * chip + core), (other_ref, 2 * chip + 1 - core)):
            at = device * PER
            for r in range(2):
                rows = pl.ds(pl.multiple_of(at + r * 8, 8), 8)
                for l in range(KROWS // 128):
                    piece = ref[chip, pl.ds((r * (KROWS // 128) + l) * 8, 8)]
                    rows_s[rows, pl.ds(l * 128, 128)] = piece
                piece = ref[chip, pl.ds(ROWS - 8, 8)]
                rows_s[rows, pl.ds(KROWS, 128)] = pltpu.roll(piece, 64, 1) if r else piece
        return carry

    lax.fori_loop(0, chips, unpack, 0)
    blocks_in_order(rows_s, coupling_ref, me)
    pieces = [(e, rows_s[pl.ds(e * PER, PER), pl.ds(KROWS, 128)]) for e in range(2 * chips)]
    spread = corrected_values(coupling_ref, inverse_ref, window_of(pieces, window_s, me))
    spread_ref[...] = spread
    near_thin = near_ref.at[pl.ds(0, H_ALL)]
    all_coefficients(coef_ref, near_thin, None, statics, tx_s, HALO + 1, top + THIN)
    load.wait()
    prolong(one_s, (HALO, top), gains_of(spread, 0), lambda i, u, rows: basis_ref[i, plane_at(u - HALO, planes), rows])
    prolong(
        one_s, (top, top + HALO), gains_of(spread, 1), lambda i, u, rows: near_ref[i * HALO + u - top, rows]
    )
    sweep(coef_ref, one_s, two_s, HALO + 1, top + HALO - 1)
    sweep(coef_ref, two_s, one_s, HALO + 2, top + HALO - 2)
    sweep(coef_ref, one_s, two_s, HALO + 3, top + HALO - 3)
    for k in range(HALO):
        for i in range(NBF):
            edge_basis[i, k] = basis_ref[i, plane_at(k, planes)]
    one_out[...] = one_s[pl.ds(HALO, HALO)]
    two_out[...] = two_s[pl.ds(HALO + 1, HALO)]
    stores = started(
        [(two_s.at[pl.ds(top - 1 - k, 1)], send_near_hbm.at[pl.ds(k, 1)]) for k in range(HALO)], sems, 1
    )
    done = planes - THIN
    pressure_ref[pl.ds(THIN, done)] = two_s[pl.ds(HALO + THIN, done)]

    def step(u):
        one_s[u] = misfit(coef_ref, two_s, u)

    planes_in_groups(HALO + THIN + 1, top, planes - THIN - 1, step)
    totals = restrict_totals(
        lambda i, u: basis_ref[i, plane_at(u - HALO, planes)], lambda u: one_s[u], HALO + THIN + 1, top
    )
    for k, total in enumerate(totals):
        totals_ref[k] = total
    for copy in stores:
        copy.wait()


def edge_kernel(
    count, spread_ref, one_in, two_in, totals_in, basis_ref, pressure_in, far_ref, *refs
):
    statics, refs = refs[:6], refs[6:]
    pressure_ref, send_far_hbm, packed_hbm = refs[:3]
    coef_ref, one_s, two_s, tx_s, tail_s, sems = refs[3:]
    me = lax.axis_index("gx")
    planes = pressure_ref.shape[0]
    pressure_ref[pl.ds(THIN, planes - THIN)] = pressure_in[pl.ds(THIN, planes - THIN)]
    one_s[pl.ds(HALO, HALO)] = one_in[...]
    two_s[pl.ds(HALO + 1, HALO)] = two_in[...]
    all_coefficients(coef_ref, None, far_ref, statics, tx_s, 1, 2 * HALO)
    prolong(
        one_s, (0, HALO), gains_of(spread_ref[...], -1), lambda i, u, rows: far_ref[i * HALO + u, rows]
    )
    sweep(coef_ref, one_s, two_s, 1, HALO + 1)
    sweep(coef_ref, two_s, one_s, 2, HALO + 2)
    sweep(coef_ref, one_s, two_s, 3, HALO + 3)
    stores = started(
        [(two_s.at[pl.ds(2 * HALO - 1 - k, 1)], send_far_hbm.at[pl.ds(k, 1)]) for k in range(HALO)], sems
    )
    pressure_ref[pl.ds(0, THIN)] = two_s[pl.ds(HALO, THIN)]
    for u in range(HALO, 2 * HALO):
        one_s[u] = misfit(coef_ref, two_s, u)
    totals = restrict_totals(
        lambda i, u: basis_ref[i, u - HALO],
        lambda u: one_s[u],
        HALO,
        2 * HALO,
        [totals_in[k] for k in range(NBF * NYB)],
    )
    tail_s[...] = restricted_tile(totals, lane_of(me))
    stores += started(
        [(tail_s, packed_hbm.at[e]) for e in range(count)], sems, HALO
    )
    for copy in stores:
        copy.wait()


def last_kernel(
    basis_hbm, gathered_ref, inverse_ref, near_ref, far_ref, coupling_ref, pressure_ref, near_p_ref, far_p_ref,
    *refs
):
    statics, refs = refs[:6], refs[6:]
    pressure_out, residual_out, basis_ref, coef_ref, one_s, two_s, tx_s, pressure_s, residual_s, sems = refs
    planes = pressure_ref.shape[0]
    top = planes + HALO
    me = lax.axis_index("gx")
    load = started(((basis_hbm, basis_ref),), sems)[0]
    spread = corrected_values(coupling_ref, inverse_ref, window_of_tiles(gathered_ref, me))
    all_coefficients(coef_ref, near_ref, far_ref, statics, tx_s, 1, top + THIN)
    prolong(
        one_s, (0, HALO), gains_of(spread, -1), lambda i, u, rows: far_ref[i * HALO + u, rows],
        lambda u: far_p_ref[u],
    )
    prolong(
        one_s, (top, top + HALO), gains_of(spread, 1), lambda i, u, rows: near_ref[i * HALO + u - top, rows],
        lambda u: near_p_ref[u - top],
    )
    load.wait()
    prolong(
        one_s, (HALO, top), gains_of(spread, 0), lambda i, u, rows: basis_ref[i, plane_at(u - HALO, planes), rows],
        lambda u: pressure_ref[u - HALO],
    )
    sweep(coef_ref, one_s, two_s, 1, top + HALO - 1)
    sweep(coef_ref, two_s, one_s, 2, top + HALO - 2)
    sweep(coef_ref, one_s, two_s, 3, top + HALO - 3)
    for place in range(planes):
        pressure_s[plane_at(place, planes)] = two_s[place + HALO]
    stores = started(((pressure_s, pressure_out),), sems, 1)

    def step(u):
        residual_s[plane_at(u - HALO, planes)] = misfit(coef_ref, two_s, u)

    planes_in_groups(HALO, top, planes, step)
    stores += started(((residual_s, residual_out),), sems, 2)
    for copy in stores:
        copy.wait()


VMEM = pl.BlockSpec(memory_space=pltpu.VMEM)
ANY = pl.BlockSpec(memory_space=pl.ANY)


def kernel_call(name, body, arguments, outputs, scratch, aliases=None):
    spec = {pltpu.HBM: ANY, pltpu.VMEM: VMEM}
    call = pl.pallas_call(
        body,
        out_shape=[space(shape, dtype) for space, shape, dtype in outputs],
        in_specs=[spec[space] for space, _ in arguments],
        out_specs=[spec[space] for space, _, _ in outputs],
        scratch_shapes=scratch,
        input_output_aliases=aliases or {},
        compiler_params=pltpu.CompilerParams(vmem_limit_bytes=16 * 1024 * 1024),
        name=name,
    )
    return call(*[pltpu.with_memory_space_constraint(value, space) for space, value in arguments])


def local(
    right_side, wet_quarters, trans_x, trans_y, trans_z, storage, basis, coupling, coarse_inverse,
    owned_block, block_slot, neighbours,
):
    count = lax.axis_size("gx")
    planes, ny, nz = right_side.shape
    field = (ny, nz)
    full = planes + 2 * HALO
    near_pairs = [(i, i ^ 1) for i in range(count)]
    far_pairs = [(i, i + 1) for i in range(1, count - 1, 2)]
    far_pairs = far_pairs + [(b, a) for a, b in far_pairs]
    H, V = pltpu.HBM, pltpu.VMEM
    statics = [(H, a) for a in (right_side, wet_quarters, trans_x, trans_y, trans_z, storage)]
    halo = (H_ALL,) + field
    factors = pltpu.VMEM((full, 8) + field, F32)
    state = pltpu.VMEM((full,) + field, F32)
    own = pltpu.VMEM((planes,) + field, F32)
    window = pltpu.VMEM((count * PER + WIN, 128), F32)
    around = pltpu.VMEM((full,) + field, BF16)
    whole_basis = pltpu.VMEM(basis.shape, BF16)

    blocks = coarse_inverse.shape[2]
    near, far, packed, *fields, inverse, room, more_room = kernel_call(
        "restrict_first",
        first_kernel,
        [
            (H, owned_block), (H, basis), *statics, (H, coupling.reshape(KROWS, PER)),
            (H, coarse_inverse.reshape(NBF * NBF, blocks)),
        ],
        [(H, halo, BF16), (H, halo, BF16), (H, (count // 2, ROWS, 128), F32), (V, right_side.shape, F32)]
        + [(V, right_side.shape, BF16)] * 5
        + [(V, (NBF * NBF, WIN), F32), (V, right_side.shape, F32), (V, (KROWS, WIN), F32)],
        [
            pltpu.SMEM(owned_block.shape, jnp.int32),
            whole_basis,
            *[pltpu.VMEM(a.shape, a.dtype) for _, a in statics],
            pltpu.VMEM((KROWS, PER), F32),
            pltpu.VMEM((NBF * NBF, blocks), F32),
            pltpu.VMEM((ROWS, 128), F32),
            pltpu.VMEM((2,) + halo, BF16),
            pltpu.SemaphoreType.DMA((16 + count // 2,)),
        ],
    )
    far = lax.ppermute(far, "gx", far_pairs)
    chips = [[core + 2 * chip for chip in range(count // 2)] for core in range(2)]
    half = lax.all_to_all(packed, "gx", 0, 0, axis_index_groups=chips, tiled=True)
    near = lax.ppermute(near, "gx", near_pairs)
    other = lax.ppermute(half, "gx", near_pairs)

    pressure, coupled, spread, one, two, totals, edge_basis, send_near = kernel_call(
        "iteration_first",
        body_kernel,
        [(H, basis)] + [(V, a) for a in (half, other, inverse, near, *fields, room, more_room)],
        [
            (V, (planes,) + field, F32),
            (V, (KROWS, WIN), F32),
            (V, (NBF, 3 * NYB * nz), F32),
            (V, (HALO,) + field, F32),
            (V, (HALO,) + field, F32),
            (V, (NBF * NYB, 8, nz), F32),
            (V, (NBF, HALO) + field, BF16),
            (H, (HALO,) + field, F32),
        ],
        [
            pltpu.VMEM((count * PER, KROWS + 128), F32),
            window, whole_basis, factors, state, state, around, pltpu.SemaphoreType.DMA((1 + HALO,)),
        ],
        {11: 0, 12: 1},
    )
    near_p = lax.ppermute(send_near, "gx", near_pairs)
    far, near_p = lax.optimization_barrier((far, near_p))
    pressure, send_far, packed = kernel_call(
        "edge_first",
        functools.partial(edge_kernel, count),
        [(V, a) for a in (spread, one, two, totals, edge_basis, pressure, far, *fields)],
        [
            (V, (planes,) + field, F32),
            (H, (HALO,) + field, F32),
            (H, (count, NBF, 128), F32),
        ],
        [
            factors, state, state, around,
            pltpu.VMEM((NBF, 128), F32), pltpu.SemaphoreType.DMA((HALO + count,)),
        ],
        {5: 0},
    )

    far_p = lax.ppermute(send_far, "gx", far_pairs)
    gathered = lax.all_to_all(packed, "gx", 0, 0, tiled=True)
    whole = (H, (planes,) + field, F32)
    return kernel_call(
        "iteration_last",
        last_kernel,
        [(H, basis)]
        + [(V, a) for a in (gathered, inverse, near, far, coupled, pressure, near_p, far_p, *fields)],
        [whole, whole],
        [
            whole_basis, factors, state, state, around, own, own,
            pltpu.SemaphoreType.DMA((3,)),
        ],
    )


def solution(mesh):
    slabs = P(("parts", "gx"), None, None)
    placed = (
        slabs, slabs, slabs, slabs, slabs, slabs,
        P(None, ("parts", "gx"), None, None),
        P(None, None, None, ("parts", "gx")),
        P(None, None, "parts"),
        P(),
        P("gx"),
        P(None, "gx"),
    )
    return jax.shard_map(local, mesh=mesh, in_specs=placed, out_specs=(slabs, slabs), check_vma=False)
```

time: 46.3 us -> 42.5 us (0.918)
  Pallas kernels: 13.5 us -> 10.4 us
  starting transfers between devices: 16.3 us -> 14.1 us
  waiting for transfers between devices: 15.3 us -> 16.8 us
    pallas_call x5 -> x4, Pallas kernels: 13.5 us -> 10.4 us  [kernel_call(): call(*[pltpu.with_memory_space_constraint(value, space) for space, value...]
    all_to_all x1, starting transfers between devices: 7.07 us -> 5.11 us  [local(): gathered = lax.all_to_all(packed, 'gx', 0, 0, tiled=True)]
    ppermute x1, waiting for transfers between devices: 0.24 us -> 1.32 us  [local(): near_p = lax.ppermute(send_near, 'gx', near_pairs)]
    all_to_all x1, waiting for transfers between devices: 6.95 us -> 7.83 us  [local(): lax.all_to_all(packed, 'gx', 0, 0, axis_index_groups=chips, tiled=True)]
  transfers between devices with their start and end apart: 7 -> 7, of which waited for: 4 -> 4; matrix products, arithmetic and copies ran while one was open for 0% -> 0% of each run, Pallas kernels for 8% -> 7%
where the time goes in v4:
time: 42.5 us; the launch traced here: 42.1 us
  waiting for transfers between devices  16.8 us (40%)
  starting transfers between devices  14.1 us (33%)
  Pallas kernels  10.4 us (24%)
  between operations  0.73 us (2%)
    pallas_call x4, Pallas kernels, kernel_call(): call(*[pltpu.with_memory_space_constraint(value, space) for space, value...  10.4 us
    all_to_all x1, waiting for transfers between devices, local(): lax.all_to_all(packed, 'gx', 0, 0, axis_index_groups=chips, tiled=True)  7.83 us
    all_to_all x1, starting transfers between devices, local(): lax.all_to_all(packed, 'gx', 0, 0, axis_index_groups=chips, tiled=True)  7.42 us
    all_to_all x1, waiting for transfers between devices, local(): gathered = lax.all_to_all(packed, 'gx', 0, 0, tiled=True)  6.2 us
    all_to_all x1, starting transfers between devices, local(): gathered = lax.all_to_all(packed, 'gx', 0, 0, tiled=True)  5.11 us
    ppermute x1, waiting for transfers between devices, local(): other = lax.ppermute(half, 'gx', near_pairs)  1.48 us
    ppermute x1, waiting for transfers between devices, local(): near_p = lax.ppermute(send_near, 'gx', near_pairs)  1.32 us
  transfers between devices with their start and end apart: 7, of which 4 were waited for; matrix products, arithmetic and copies ran while one was open for 0% of the time, Pallas kernels for 7%

profile of v4, /device:TPU:0, one launch (start us, length us, event | category | flops | bytes accessed | tf_op | source)
XLA Modules:
  0.0 42.1 jit_solution(10399032427906153432)
XLA Ops:
  0.6 2.7 %restrict_first.1 = (bf16[54,32,128]{2,1,0:T(8,128)(2,1)}, bf16[54,32,128]{2,1,0:T(8,128)(2,1)}, f32[8,56,128]{2,1,0:T(8,128)}, f32[16,32,128]{2,1,0:T(8,128)S(1...) custom-call(s32[256]{0:T(256)} %owned_hbm.1, ...), custom_call_target="tpu_custom_call" | custom-call | tf_op jit(solution)/shard_map/restrict_first/pallas_call | solution.py:554
  3.3 0.0 copy-start
  3.3 7.4 %all-to-all-start = ((f32[8,56,128]{2,1,0:T(8,128)}), f32[8,56,128]{2,1,0:T(8,128)S(1)}, u32[]{:S(2)}, u32[]{:S(2)}) async-start(f32[8,56,128]{2,1,0:T(8,128)} %get-tuple-element.27), calls=%async_computation | async-start | bytes 458752 | tf_op jit(solution)/shard_map/all_to_all | solution.py:602
  10.8 0.0 collective-permute-start.1
  10.8 0.0 copy-done
  10.8 0.7 %collective-permute-start.2 = (bf16[54,32,128]{2,1,0:T(8,128)(2,1)S(1)}, bf16[54,32,128]{2,1,0:T(8,128)(2,1)S(1)}, u32[]{:S(2)}, u32[]{:S(2)}) collective-permute-start(bf16[54,32,128]{2,1,0:T(8,128)(2,1)S(1)} %copy-done), channel_id=1, source_target_pairs={{1,2},{3,4},{5,6},{7,8},{9,10},{11,12},{13,14},{2,1},{4,3},{6,5},{... | collective-permute-start | bytes 1327112 | tf_op jit(solution)/shard_map/ppermute | solution.py:600
  11.5 7.8 %all-to-all-done.half_ref = f32[8,56,128]{2,1,0:T(8,128)S(1)} async-done(((f32[8,56,128]{2,1,0:T(8,128)}), f32[8,56,128]{2,1,0:T(8,128)S(1)}, u32[]{:S(2)}, u32[]{:S(2)}) %all-to-all-start) | async-done | bytes 229408 | tf_op jit(solution)/shard_map/all_to_all | solution.py:602
  19.3 0.0 collective-permute-start
  19.3 0.0 collective-permute-done.1.near_ref
  19.3 1.5 %collective-permute-done.other_ref = f32[8,56,128]{2,1,0:T(8,128)S(1)} collective-permute-done((f32[8,56,128]{2,1,0:T(8,128)S(1)}, f32[8,56,128]{2,1,0:T(8,128)S(1)}, u32[]{:S(2)}, u32[]{:S(2)}) %collective-permute-start) | collective-permute-done | bytes 229408 | tf_op jit(solution)/shard_map/ppermute | solution.py:604
  20.8 3.1 %iteration_first.1 = (f32[16,32,128]{2,1,0:T(8,128)S(1)}, f32[384,256]{1,0:T(8,128)S(1)}, f32[8,768]{1,0:T(8,128)S(1)}, f32[4,32,128]{2,1,0:T(8,128)S(1)}, f32[4...) custom-call(bf16[8,16,32,128]{3,2,1,0:T(8,128)(2,1)} %basis_hbm.5, ...), custom_call_target="tpu_custom_call", output_to_operand_aliasing={{0}: (11, {}), {1}: (12, {})} | custom-call | tf_op jit(solution)/shard_map/iteration_first/pallas_call | solution.py:554
  23.9 0.2 collective-permute-start.3
  24.1 0.0 collective-permute-done.2.far_ref
  24.1 1.3 %collective-permute-done.3.near_p_ref = f32[4,32,128]{2,1,0:T(8,128)S(1)} collective-permute-done((f32[4,32,128]{2,1,0:T(8,128)}, f32[4,32,128]{2,1,0:T(8,128)S(1)}, u32[]{:S(2)}, u32[]{:S(2)}) %collective-permute-start.3) | collective-permute-done | bytes 65568 | tf_op jit(solution)/shard_map/ppermute | solution.py:626
  25.5 1.5 %edge_first.1 = (f32[16,32,128]{2,1,0:T(8,128)S(1)}, f32[4,32,128]{2,1,0:T(8,128)}, f32[16,8,128]{2,1,0:T(8,128)}) custom-call(f32[8,768]{1,0:T(8,128)S(1)} %get-tuple-element.38.spread_ref, f32[4,32,128]{2,1,0:T(8,128)S(1)} %get-tuple-element.39.one_in, f32[4,32,128]{2,1,0:T(8,128)S(1)} %get-tuple-element.40.two_in, ...), custom_call_target="tpu_custom_call", output_to_operand_aliasing={{0}: (5, {})} | custom-call | tf_op jit(solution)/shard_map/edge_first/pallas_call | solution.py:554
  27.0 0.0 copy-start.1
  27.0 5.1 %all-to-all-start.1 = ((f32[16,8,128]{2,1,0:T(8,128)}), f32[16,8,128]{2,1,0:T(8,128)S(1)}, u32[]{:S(2)}, u32[]{:S(2)}) async-start(f32[16,8,128]{2,1,0:T(8,128)} %get-tuple-element.47), calls=%async_computation.1 | async-start | bytes 131072 | tf_op jit(solution)/shard_map/all_to_all | solution.py:645
  32.1 0.0 copy-done.1
  32.1 0.7 %collective-permute-start.4 = (f32[4,32,128]{2,1,0:T(8,128)S(1)}, f32[4,32,128]{2,1,0:T(8,128)S(1)}, u32[]{:S(2)}, u32[]{:S(2)}) collective-permute-start(f32[4,32,128]{2,1,0:T(8,128)S(1)} %copy-done.1), channel_id=1, source_target_pairs={{1,2},{3,4},{5,6},{7,8},{9,10},{11,12},{13,14},{2,1},{4,3},{6,5},{... | collective-permute-start | bytes 196616 | tf_op jit(solution)/shard_map/ppermute | solution.py:644
  32.8 0.0 collective-permute-done.4.far_p_ref
  32.8 6.2 %all-to-all-done.1.gathered_ref = f32[16,8,128]{2,1,0:T(8,128)S(1)} async-done(((f32[16,8,128]{2,1,0:T(8,128)}), f32[16,8,128]{2,1,0:T(8,128)S(1)}, u32[]{:S(2)}, u32[]{:S(2)}) %all-to-all-start.1) | async-done | bytes 65568 | tf_op jit(solution)/shard_map/all_to_all | solution.py:645
  39.0 3.1 %iteration_last.1 = (f32[16,32,128]{2,1,0:T(8,128)}, f32[16,32,128]{2,1,0:T(8,128)}) custom-call(bf16[8,16,32,128]{3,2,1,0:T(8,128)(2,1)} %basis_hbm.5, f32[16,8,128]{2,1,0:T(8,128)S(1)} %all-to-all-done.1.gathered_ref, f32[64,256]{1,0:T(8,128)S(1)} %get-tuple-element.28.inverse_ref, bf16[54,32,128]{2,1,0:T(8,128)(2,1)S(1)} %collective-permute-done.1.near_ref, ...), custom_call_target="tpu_custom_call" | custom-call | tf_op jit(solution)/shard_map/iteration_last/pallas_call | solution.py:554
Async XLA Ops:
  3.3 7.4 %copy-start = (bf16[54,32,128]{2,1,0:T(8,128)(2,1)S(1)}, bf16[54,32,128]{2,1,0:T(8,128)(2,1)}, u32[]{:S(2)}) copy-start(bf16[54,32,128]{2,1,0:T(8,128)(2,1)} %get-tuple-element.44) | copy-start | bytes 1327108
  3.3 16.0 %all-to-all-start = ((f32[8,56,128]{2,1,0:T(8,128)}), f32[8,56,128]{2,1,0:T(8,128)S(1)}, u32[]{:S(2)}, u32[]{:S(2)}) async-start(f32[8,56,128]{2,1,0:T(8,128)} %get-tuple-element.27), calls=%async_computation | async-start | bytes 458752 | tf_op jit(solution)/shard_map/all_to_all | solution.py:602
  10.8 8.5 %collective-permute-start.1 = (bf16[54,32,128]{2,1,0:T(8,128)(2,1)}, bf16[54,32,128]{2,1,0:T(8,128)(2,1)S(1)}, u32[]{:S(2)}, u32[]{:S(2)}) collective-permute-start(bf16[54,32,128]{2,1,0:T(8,128)(2,1)} %get-tuple-element.29), channel_id=1, source_target_pairs={{0,1},{1,0},{2,3},{3,2},{4,5},{5,4},{6,7},{7,6},{8,9},{9,8},{10,11... | collective-permute-start | bytes 1327112 | tf_op jit(solution)/shard_map/ppermute | solution.py:603
  10.8 13.4 %collective-permute-start.2 = (bf16[54,32,128]{2,1,0:T(8,128)(2,1)S(1)}, bf16[54,32,128]{2,1,0:T(8,128)(2,1)S(1)}, u32[]{:S(2)}, u32[]{:S(2)}) collective-permute-start(bf16[54,32,128]{2,1,0:T(8,128)(2,1)S(1)} %copy-done), channel_id=1, source_target_pairs={{1,2},{3,4},{5,6},{7,8},{9,10},{11,12},{13,14},{2,1},{4,3},{6,5},{... | collective-permute-start | bytes 1327112 | tf_op jit(solution)/shard_map/ppermute | solution.py:600
  19.3 1.5 %collective-permute-start = (f32[8,56,128]{2,1,0:T(8,128)S(1)}, f32[8,56,128]{2,1,0:T(8,128)S(1)}, u32[]{:S(2)}, u32[]{:S(2)}) collective-permute-start(f32[8,56,128]{2,1,0:T(8,128)S(1)} %all-to-all-done.half_ref), channel_id=1, source_target_pairs={{0,1},{1,0},{2,3},{3,2},{4,5},{5,4},{6,7},{7,6},{8,9},{9,8},{10,11... | collective-permute-start | bytes 688136 | tf_op jit(solution)/shard_map/ppermute | solution.py:604
  23.9 1.5 %collective-permute-start.3 = (f32[4,32,128]{2,1,0:T(8,128)}, f32[4,32,128]{2,1,0:T(8,128)S(1)}, u32[]{:S(2)}, u32[]{:S(2)}) collective-permute-start(f32[4,32,128]{2,1,0:T(8,128)} %get-tuple-element.45), channel_id=1, source_target_pairs={{0,1},{1,0},{2,3},{3,2},{4,5},{5,4},{6,7},{7,6},{8,9},{9,8},{10,11... | collective-permute-start | bytes 196616 | tf_op jit(solution)/shard_map/ppermute | solution.py:626
  27.0 5.1 %copy-start.1 = (f32[4,32,128]{2,1,0:T(8,128)S(1)}, f32[4,32,128]{2,1,0:T(8,128)}, u32[]{:S(2)}) copy-start(f32[4,32,128]{2,1,0:T(8,128)} %get-tuple-element.51) | copy-start | bytes 196612
  27.0 12.0 %all-to-all-start.1 = ((f32[16,8,128]{2,1,0:T(8,128)}), f32[16,8,128]{2,1,0:T(8,128)S(1)}, u32[]{:S(2)}, u32[]{:S(2)}) async-start(f32[16,8,128]{2,1,0:T(8,128)} %get-tuple-element.47), calls=%async_computation.1 | async-start | bytes 131072 | tf_op jit(solution)/shard_map/all_to_all | solution.py:645
  32.1 0.7 %collective-permute-start.4 = (f32[4,32,128]{2,1,0:T(8,128)S(1)}, f32[4,32,128]{2,1,0:T(8,128)S(1)}, u32[]{:S(2)}, u32[]{:S(2)}) collective-permute-start(f32[4,32,128]{2,1,0:T(8,128)S(1)} %copy-done.1), channel_id=1, source_target_pairs={{1,2},{3,4},{5,6},{7,8},{9,10},{11,12},{13,14},{2,1},{4,3},{6,5},{... | collective-permute-start | bytes 196616 | tf_op jit(solution)/shard_map/ppermute | solution.py:644

commit v5 on v4

--- a/solution.py
+++ b/solution.py
@@ -104,17 +104,22 @@
     return lax.rem(device, 128 // PER) * PER
 
 
+def tile_order(count):
+    order = list(range(count))
+    order[0], order[3] = order[3], order[0]
+    return order
+
+
 def window_of_tiles(gathered_ref, me):
-    count = gathered_ref.shape[0]
-    halves = []
-    for half in range(WIN // 128):
-        total = 0.0
-        for w in range(128 // PER):
-            device = me - LEAD + half * (128 // PER) + w
-            inside = (device >= 0) & (device < count)
-            total = total + jnp.where(inside, gathered_ref[jnp.clip(device, 0, count - 1)], 0.0)
-        halves.append(pltpu.roll(total, lax.rem(128 - lane_of(me + 128 // PER - LEAD), 128), 1))
-    return jnp.concatenate(halves, axis=1)
+    per = 128 // PER
+    halves = [0.0] * (WIN // 128)
+    for rank, device in enumerate(tile_order(gathered_ref.shape[0])):
+        place = device - me + LEAD
+        for half in range(WIN // 128):
+            inside = (place >= half * per) & (place < (half + 1) * per)
+            halves[half] = halves[half] + jnp.where(inside, gathered_ref[rank], 0.0)
+    turn = lax.rem(128 - lane_of(me + per - LEAD), 128)
+    return jnp.concatenate([pltpu.roll(half, turn, 1) for half in halves], axis=1)
 
 
 def started(pairs, sems, first=0):
@@ -529,8 +534,11 @@
     def step(u):
         residual_s[plane_at(u - HALO, planes)] = misfit(coef_ref, two_s, u)
 
-    planes_in_groups(HALO, top, planes, step)
-    stores += started(((residual_s, residual_out),), sems, 2)
+    half = planes // 2
+    for part in range(2):
+        planes_in_groups(HALO + part * half, HALO + (part + 1) * half, half, step)
+        span = pl.ds(plane_at(part * half, planes) - jnp.where(is_even(), 0, half - 1), half)
+        stores += started(((residual_s.at[span], residual_out.at[span]),), sems, 2 + part)
     for copy in stores:
         copy.wait()
 
@@ -642,7 +650,7 @@
     )
 
     far_p = lax.ppermute(send_far, "gx", far_pairs)
-    gathered = lax.all_to_all(packed, "gx", 0, 0, tiled=True)
+    gathered = lax.all_to_all(packed, "gx", 0, 0, axis_index_groups=[tile_order(count)], tiled=True)
     whole = (H, (planes,) + field, F32)
     return kernel_call(
         "iteration_last",
@@ -652,7 +660,7 @@
         [whole, whole],
         [
             whole_basis, factors, state, state, around, own, own,
-            pltpu.SemaphoreType.DMA((3,)),
+            pltpu.SemaphoreType.DMA((4,)),
         ],
     )
 

time: 42.5 us -> 42 us (0.988)
  waiting for transfers between devices: 16.8 us -> 15.3 us
  starting transfers between devices: 14.1 us -> 15.2 us
    all_to_all x1, waiting for transfers between devices: 6.2 us -> 4.7 us  [local(): lax.all_to_all(packed, 'gx', 0, 0, axis_index_groups=[tile_order(count)],...]
    all_to_all x1, starting transfers between devices: 5.11 us -> 6.23 us  [local(): lax.all_to_all(packed, 'gx', 0, 0, axis_index_groups=[tile_order(count)],...]
  transfers between devices with their start and end apart: 7 -> 7, of which waited for: 4 -> 4; matrix products, arithmetic and copies ran while one was open for 0% -> 0% of each run, Pallas kernels for 7% -> 8%
where the time goes in v5:
time: 42 us; the launch traced here: 41.6 us
  waiting for transfers between devices  15.3 us (36%)
  starting transfers between devices  15.2 us (36%)
  Pallas kernels  10.3 us (25%)
  between operations  0.72 us (2%)
    pallas_call x4, Pallas kernels, kernel_call(): call(*[pltpu.with_memory_space_constraint(value, space) for space, value...  10.3 us
    all_to_all x1, waiting for transfers between devices, local(): lax.all_to_all(packed, 'gx', 0, 0, axis_index_groups=chips, tiled=True)  7.83 us
    all_to_all x1, starting transfers between devices, local(): lax.all_to_all(packed, 'gx', 0, 0, axis_index_groups=chips, tiled=True)  7.42 us
    all_to_all x1, starting transfers between devices, local(): lax.all_to_all(packed, 'gx', 0, 0, axis_index_groups=[tile_order(count)],...  6.23 us
    all_to_all x1, waiting for transfers between devices, local(): lax.all_to_all(packed, 'gx', 0, 0, axis_index_groups=[tile_order(count)],...  4.7 us
    ppermute x1, waiting for transfers between devices, local(): other = lax.ppermute(half, 'gx', near_pairs)  1.48 us
    ppermute x1, waiting for transfers between devices, local(): near_p = lax.ppermute(send_near, 'gx', near_pairs)  1.32 us
  transfers between devices with their start and end apart: 7, of which 4 were waited for; matrix products, arithmetic and copies ran while one was open for 0% of the time, Pallas kernels for 8%

profile of v5, /device:TPU:0, one launch (start us, length us, event | category | flops | bytes accessed | tf_op | source)
XLA Modules:
  0.0 41.6 jit_solution(12707676021876917646)
XLA Ops:
  0.6 2.7 %restrict_first.1 = (bf16[54,32,128]{2,1,0:T(8,128)(2,1)}, bf16[54,32,128]{2,1,0:T(8,128)(2,1)}, f32[8,56,128]{2,1,0:T(8,128)}, f32[16,32,128]{2,1,0:T(8,128)S(1...) custom-call(s32[256]{0:T(256)} %owned_hbm.1, ...), custom_call_target="tpu_custom_call" | custom-call | tf_op jit(solution)/shard_map/restrict_first/pallas_call | solution.py:562
  3.3 0.0 copy-start
  3.3 7.4 %all-to-all-start = ((f32[8,56,128]{2,1,0:T(8,128)}), f32[8,56,128]{2,1,0:T(8,128)S(1)}, u32[]{:S(2)}, u32[]{:S(2)}) async-start(f32[8,56,128]{2,1,0:T(8,128)} %get-tuple-element.27), calls=%async_computation | async-start | bytes 458752 | tf_op jit(solution)/shard_map/all_to_all | solution.py:610
  10.8 0.0 collective-permute-start.1
  10.8 0.0 copy-done
  10.8 0.7 %collective-permute-start.2 = (bf16[54,32,128]{2,1,0:T(8,128)(2,1)S(1)}, bf16[54,32,128]{2,1,0:T(8,128)(2,1)S(1)}, u32[]{:S(2)}, u32[]{:S(2)}) collective-permute-start(bf16[54,32,128]{2,1,0:T(8,128)(2,1)S(1)} %copy-done), channel_id=1, source_target_pairs={{1,2},{3,4},{5,6},{7,8},{9,10},{11,12},{13,14},{2,1},{4,3},{6,5},{... | collective-permute-start | bytes 1327112 | tf_op jit(solution)/shard_map/ppermute | solution.py:608
  11.5 7.8 %all-to-all-done.half_ref = f32[8,56,128]{2,1,0:T(8,128)S(1)} async-done(((f32[8,56,128]{2,1,0:T(8,128)}), f32[8,56,128]{2,1,0:T(8,128)S(1)}, u32[]{:S(2)}, u32[]{:S(2)}) %all-to-all-start) | async-done | bytes 229408 | tf_op jit(solution)/shard_map/all_to_all | solution.py:610
  19.3 0.0 collective-permute-start
  19.3 0.0 collective-permute-done.1.near_ref
  19.3 1.5 %collective-permute-done.other_ref = f32[8,56,128]{2,1,0:T(8,128)S(1)} collective-permute-done((f32[8,56,128]{2,1,0:T(8,128)S(1)}, f32[8,56,128]{2,1,0:T(8,128)S(1)}, u32[]{:S(2)}, u32[]{:S(2)}) %collective-permute-start) | collective-permute-done | bytes 229408 | tf_op jit(solution)/shard_map/ppermute | solution.py:612
  20.8 3.1 %iteration_first.1 = (f32[16,32,128]{2,1,0:T(8,128)S(1)}, f32[384,256]{1,0:T(8,128)S(1)}, f32[8,768]{1,0:T(8,128)S(1)}, f32[4,32,128]{2,1,0:T(8,128)S(1)}, f32[4...) custom-call(bf16[8,16,32,128]{3,2,1,0:T(8,128)(2,1)} %basis_hbm.5, ...), custom_call_target="tpu_custom_call", output_to_operand_aliasing={{0}: (11, {}), {1}: (12, {})} | custom-call | tf_op jit(solution)/shard_map/iteration_first/pallas_call | solution.py:562
  23.9 0.2 collective-permute-start.3
  24.1 0.0 collective-permute-done.2.far_ref
  24.1 1.3 %collective-permute-done.3.near_p_ref = f32[4,32,128]{2,1,0:T(8,128)S(1)} collective-permute-done((f32[4,32,128]{2,1,0:T(8,128)}, f32[4,32,128]{2,1,0:T(8,128)S(1)}, u32[]{:S(2)}, u32[]{:S(2)}) %collective-permute-start.3) | collective-permute-done | bytes 65568 | tf_op jit(solution)/shard_map/ppermute | solution.py:634
  25.5 1.5 %edge_first.1 = (f32[16,32,128]{2,1,0:T(8,128)S(1)}, f32[4,32,128]{2,1,0:T(8,128)}, f32[16,8,128]{2,1,0:T(8,128)}) custom-call(f32[8,768]{1,0:T(8,128)S(1)} %get-tuple-element.38.spread_ref, f32[4,32,128]{2,1,0:T(8,128)S(1)} %get-tuple-element.39.one_in, f32[4,32,128]{2,1,0:T(8,128)S(1)} %get-tuple-element.40.two_in, ...), custom_call_target="tpu_custom_call", output_to_operand_aliasing={{0}: (5, {})} | custom-call | tf_op jit(solution)/shard_map/edge_first/pallas_call | solution.py:562
  27.0 0.0 copy-start.1
  27.0 6.2 %all-to-all-start.1 = ((f32[16,8,128]{2,1,0:T(8,128)}), f32[16,8,128]{2,1,0:T(8,128)S(1)}, u32[]{:S(2)}, u32[]{:S(2)}) async-start(f32[16,8,128]{2,1,0:T(8,128)} %get-tuple-element.47), calls=%async_computation.1 | async-start | bytes 131072 | tf_op jit(solution)/shard_map/all_to_all | solution.py:653
  33.2 0.0 copy-done.1
  33.2 0.7 %collective-permute-start.4 = (f32[4,32,128]{2,1,0:T(8,128)S(1)}, f32[4,32,128]{2,1,0:T(8,128)S(1)}, u32[]{:S(2)}, u32[]{:S(2)}) collective-permute-start(f32[4,32,128]{2,1,0:T(8,128)S(1)} %copy-done.1), channel_id=1, source_target_pairs={{1,2},{3,4},{5,6},{7,8},{9,10},{11,12},{13,14},{2,1},{4,3},{6,5},{... | collective-permute-start | bytes 196616 | tf_op jit(solution)/shard_map/ppermute | solution.py:652
  33.9 0.0 collective-permute-done.4.far_p_ref
  33.9 4.7 %all-to-all-done.1.gathered_ref = f32[16,8,128]{2,1,0:T(8,128)S(1)} async-done(((f32[16,8,128]{2,1,0:T(8,128)}), f32[16,8,128]{2,1,0:T(8,128)S(1)}, u32[]{:S(2)}, u32[]{:S(2)}) %all-to-all-start.1) | async-done | bytes 65568 | tf_op jit(solution)/shard_map/all_to_all | solution.py:653
  38.6 3.0 %iteration_last.1 = (f32[16,32,128]{2,1,0:T(8,128)}, f32[16,32,128]{2,1,0:T(8,128)}) custom-call(bf16[8,16,32,128]{3,2,1,0:T(8,128)(2,1)} %basis_hbm.5, f32[16,8,128]{2,1,0:T(8,128)S(1)} %all-to-all-done.1.gathered_ref, f32[64,256]{1,0:T(8,128)S(1)} %get-tuple-element.28.inverse_ref, bf16[54,32,128]{2,1,0:T(8,128)(2,1)S(1)} %collective-permute-done.1.near_ref, ...), custom_call_target="tpu_custom_call" | custom-call | tf_op jit(solution)/shard_map/iteration_last/pallas_call | solution.py:562
Async XLA Ops:
  3.3 7.4 %copy-start = (bf16[54,32,128]{2,1,0:T(8,128)(2,1)S(1)}, bf16[54,32,128]{2,1,0:T(8,128)(2,1)}, u32[]{:S(2)}) copy-start(bf16[54,32,128]{2,1,0:T(8,128)(2,1)} %get-tuple-element.44) | copy-start | bytes 1327108
  3.3 16.0 %all-to-all-start = ((f32[8,56,128]{2,1,0:T(8,128)}), f32[8,56,128]{2,1,0:T(8,128)S(1)}, u32[]{:S(2)}, u32[]{:S(2)}) async-start(f32[8,56,128]{2,1,0:T(8,128)} %get-tuple-element.27), calls=%async_computation | async-start | bytes 458752 | tf_op jit(solution)/shard_map/all_to_all | solution.py:610
  10.8 8.5 %collective-permute-start.1 = (bf16[54,32,128]{2,1,0:T(8,128)(2,1)}, bf16[54,32,128]{2,1,0:T(8,128)(2,1)S(1)}, u32[]{:S(2)}, u32[]{:S(2)}) collective-permute-start(bf16[54,32,128]{2,1,0:T(8,128)(2,1)} %get-tuple-element.29), channel_id=1, source_target_pairs={{0,1},{1,0},{2,3},{3,2},{4,5},{5,4},{6,7},{7,6},{8,9},{9,8},{10,11... | collective-permute-start | bytes 1327112 | tf_op jit(solution)/shard_map/ppermute | solution.py:611
  10.8 13.4 %collective-permute-start.2 = (bf16[54,32,128]{2,1,0:T(8,128)(2,1)S(1)}, bf16[54,32,128]{2,1,0:T(8,128)(2,1)S(1)}, u32[]{:S(2)}, u32[]{:S(2)}) collective-permute-start(bf16[54,32,128]{2,1,0:T(8,128)(2,1)S(1)} %copy-done), channel_id=1, source_target_pairs={{1,2},{3,4},{5,6},{7,8},{9,10},{11,12},{13,14},{2,1},{4,3},{6,5},{... | collective-permute-start | bytes 1327112 | tf_op jit(solution)/shard_map/ppermute | solution.py:608
  19.3 1.5 %collective-permute-start = (f32[8,56,128]{2,1,0:T(8,128)S(1)}, f32[8,56,128]{2,1,0:T(8,128)S(1)}, u32[]{:S(2)}, u32[]{:S(2)}) collective-permute-start(f32[8,56,128]{2,1,0:T(8,128)S(1)} %all-to-all-done.half_ref), channel_id=1, source_target_pairs={{0,1},{1,0},{2,3},{3,2},{4,5},{5,4},{6,7},{7,6},{8,9},{9,8},{10,11... | collective-permute-start | bytes 688136 | tf_op jit(solution)/shard_map/ppermute | solution.py:612
  23.9 1.5 %collective-permute-start.3 = (f32[4,32,128]{2,1,0:T(8,128)}, f32[4,32,128]{2,1,0:T(8,128)S(1)}, u32[]{:S(2)}, u32[]{:S(2)}) collective-permute-start(f32[4,32,128]{2,1,0:T(8,128)} %get-tuple-element.45), channel_id=1, source_target_pairs={{0,1},{1,0},{2,3},{3,2},{4,5},{5,4},{6,7},{7,6},{8,9},{9,8},{10,11... | collective-permute-start | bytes 196616 | tf_op jit(solution)/shard_map/ppermute | solution.py:634
  27.0 6.2 %copy-start.1 = (f32[4,32,128]{2,1,0:T(8,128)S(1)}, f32[4,32,128]{2,1,0:T(8,128)}, u32[]{:S(2)}) copy-start(f32[4,32,128]{2,1,0:T(8,128)} %get-tuple-element.51) | copy-start | bytes 196612
  27.0 11.6 %all-to-all-start.1 = ((f32[16,8,128]{2,1,0:T(8,128)}), f32[16,8,128]{2,1,0:T(8,128)S(1)}, u32[]{:S(2)}, u32[]{:S(2)}) async-start(f32[16,8,128]{2,1,0:T(8,128)} %get-tuple-element.47), calls=%async_computation.1 | async-start | bytes 131072 | tf_op jit(solution)/shard_map/all_to_all | solution.py:653
  33.2 0.7 %collective-permute-start.4 = (f32[4,32,128]{2,1,0:T(8,128)S(1)}, f32[4,32,128]{2,1,0:T(8,128)S(1)}, u32[]{:S(2)}, u32[]{:S(2)}) collective-permute-start(f32[4,32,128]{2,1,0:T(8,128)S(1)} %copy-done.1), channel_id=1, source_target_pairs={{1,2},{3,4},{5,6},{7,8},{9,10},{11,12},{13,14},{2,1},{4,3},{6,5},{... | collective-permute-start | bytes 196616 | tf_op jit(solution)/shard_map/ppermute | solution.py:652

commit v6 on v5

--- a/solution.py
+++ b/solution.py
@@ -106,7 +106,7 @@
 
 def tile_order(count):
     order = list(range(count))
-    order[0], order[3] = order[3], order[0]
+    order[:8] = order[4:8] + order[:4]
     return order
 
 
@@ -410,7 +410,8 @@
     chips = half_ref.shape[0]
 
     def unpack(chip, carry):
-        for ref, device in ((half_ref, 2 * chip + core), (other_ref, 2 * chip + 1 - core)):
+        first = 2 * jnp.where(chip < 4, jnp.bitwise_xor(chip, 2), chip)
+        for ref, device in ((half_ref, first + core), (other_ref, first + 1 - core)):
             at = device * PER
             for r in range(2):
                 rows = pl.ds(pl.multiple_of(at + r * 8, 8), 8)
@@ -606,7 +607,9 @@
         ],
     )
     far = lax.ppermute(far, "gx", far_pairs)
-    chips = [[core + 2 * chip for chip in range(count // 2)] for core in range(2)]
+    ranks = list(range(count // 2))
+    ranks[:4] = ranks[2:4] + ranks[:2]
+    chips = [[core + 2 * chip for chip in ranks] for core in range(2)]
     half = lax.all_to_all(packed, "gx", 0, 0, axis_index_groups=chips, tiled=True)
     near = lax.ppermute(near, "gx", near_pairs)
     other = lax.ppermute(half, "gx", near_pairs)

time: 42 us -> 40.6 us (0.967)
  waiting for transfers between devices: 15.3 us -> 13.9 us
    all_to_all x1, waiting for transfers between devices: 7.83 us -> 6.69 us  [local(): lax.all_to_all(packed, 'gx', 0, 0, axis_index_groups=chips, tiled=True)]
    all_to_all x1, starting transfers between devices: 6.23 us -> 5.5 us  [local(): lax.all_to_all(packed, 'gx', 0, 0, axis_index_groups=[tile_order(count)],...]
    all_to_all x1, starting transfers between devices: 7.42 us -> 7.98 us  [local(): lax.all_to_all(packed, 'gx', 0, 0, axis_index_groups=chips, tiled=True)]
where the time goes in v6:
time: 40.6 us; the launch traced here: 40 us
  starting transfers between devices  15 us (37%)
  waiting for transfers between devices  13.9 us (34%)
  Pallas kernels  10.3 us (25%)
  between operations  0.71 us (2%)
    pallas_call x4, Pallas kernels, kernel_call(): call(*[pltpu.with_memory_space_constraint(value, space) for space, value...  10.3 us
    all_to_all x1, starting transfers between devices, local(): lax.all_to_all(packed, 'gx', 0, 0, axis_index_groups=chips, tiled=True)  7.98 us
    all_to_all x1, waiting for transfers between devices, local(): lax.all_to_all(packed, 'gx', 0, 0, axis_index_groups=chips, tiled=True)  6.69 us
    all_to_all x1, starting transfers between devices, local(): lax.all_to_all(packed, 'gx', 0, 0, axis_index_groups=[tile_order(count)],...  5.5 us
    all_to_all x1, waiting for transfers between devices, local(): lax.all_to_all(packed, 'gx', 0, 0, axis_index_groups=[tile_order(count)],...  4.4 us
    ppermute x1, waiting for transfers between devices, local(): other = lax.ppermute(half, 'gx', near_pairs)  1.48 us
    ppermute x1, waiting for transfers between devices, local(): near_p = lax.ppermute(send_near, 'gx', near_pairs)  1.32 us
  transfers between devices with their start and end apart: 7, of which 4 were waited for; matrix products, arithmetic and copies ran while one was open for 0% of the time, Pallas kernels for 8%

profile of v6, /device:TPU:0, one launch (start us, length us, event | category | flops | bytes accessed | tf_op | source)
XLA Modules:
  0.0 40.0 jit_solution(13194385991929756996)
XLA Ops:
  0.6 2.7 %restrict_first.1 = (bf16[54,32,128]{2,1,0:T(8,128)(2,1)}, bf16[54,32,128]{2,1,0:T(8,128)(2,1)}, f32[8,56,128]{2,1,0:T(8,128)}, f32[16,32,128]{2,1,0:T(8,128)S(1...) custom-call(s32[256]{0:T(256)} %owned_hbm.1, ...), custom_call_target="tpu_custom_call" | custom-call | tf_op jit(solution)/shard_map/restrict_first/pallas_call | solution.py:563
  3.3 0.0 copy-start
  3.3 8.0 %all-to-all-start = ((f32[8,56,128]{2,1,0:T(8,128)}), f32[8,56,128]{2,1,0:T(8,128)S(1)}, u32[]{:S(2)}, u32[]{:S(2)}) async-start(f32[8,56,128]{2,1,0:T(8,128)} %get-tuple-element.27), calls=%async_computation | async-start | bytes 458752 | tf_op jit(solution)/shard_map/all_to_all | solution.py:613
  11.3 0.0 collective-permute-start.1
  11.3 0.0 copy-done
  11.3 0.7 %collective-permute-start.2 = (bf16[54,32,128]{2,1,0:T(8,128)(2,1)S(1)}, bf16[54,32,128]{2,1,0:T(8,128)(2,1)S(1)}, u32[]{:S(2)}, u32[]{:S(2)}) collective-permute-start(bf16[54,32,128]{2,1,0:T(8,128)(2,1)S(1)} %copy-done), channel_id=1, source_target_pairs={{1,2},{3,4},{5,6},{7,8},{9,10},{11,12},{13,14},{2,1},{4,3},{6,5},{... | collective-permute-start | bytes 1327112 | tf_op jit(solution)/shard_map/ppermute | solution.py:609
  12.0 6.7 %all-to-all-done.half_ref = f32[8,56,128]{2,1,0:T(8,128)S(1)} async-done(((f32[8,56,128]{2,1,0:T(8,128)}), f32[8,56,128]{2,1,0:T(8,128)S(1)}, u32[]{:S(2)}, u32[]{:S(2)}) %all-to-all-start) | async-done | bytes 229408 | tf_op jit(solution)/shard_map/all_to_all | solution.py:613
  18.7 0.0 collective-permute-start
  18.7 0.0 collective-permute-done.1.near_ref
  18.7 1.5 %collective-permute-done.other_ref = f32[8,56,128]{2,1,0:T(8,128)S(1)} collective-permute-done((f32[8,56,128]{2,1,0:T(8,128)S(1)}, f32[8,56,128]{2,1,0:T(8,128)S(1)}, u32[]{:S(2)}, u32[]{:S(2)}) %collective-permute-start) | collective-permute-done | bytes 229408 | tf_op jit(solution)/shard_map/ppermute | solution.py:615
  20.2 3.1 %iteration_first.1 = (f32[16,32,128]{2,1,0:T(8,128)S(1)}, f32[384,256]{1,0:T(8,128)S(1)}, f32[8,768]{1,0:T(8,128)S(1)}, f32[4,32,128]{2,1,0:T(8,128)S(1)}, f32[4...) custom-call(bf16[8,16,32,128]{3,2,1,0:T(8,128)(2,1)} %basis_hbm.5, ...), custom_call_target="tpu_custom_call", output_to_operand_aliasing={{0}: (11, {}), {1}: (12, {})} | custom-call | tf_op jit(solution)/shard_map/iteration_first/pallas_call | solution.py:563
  23.4 0.2 collective-permute-start.3
  23.6 0.0 collective-permute-done.2.far_ref
  23.6 1.3 %collective-permute-done.3.near_p_ref = f32[4,32,128]{2,1,0:T(8,128)S(1)} collective-permute-done((f32[4,32,128]{2,1,0:T(8,128)}, f32[4,32,128]{2,1,0:T(8,128)S(1)}, u32[]{:S(2)}, u32[]{:S(2)}) %collective-permute-start.3) | collective-permute-done | bytes 65568 | tf_op jit(solution)/shard_map/ppermute | solution.py:637
  24.9 1.5 %edge_first.1 = (f32[16,32,128]{2,1,0:T(8,128)S(1)}, f32[4,32,128]{2,1,0:T(8,128)}, f32[16,8,128]{2,1,0:T(8,128)}) custom-call(f32[8,768]{1,0:T(8,128)S(1)} %get-tuple-element.38.spread_ref, f32[4,32,128]{2,1,0:T(8,128)S(1)} %get-tuple-element.39.one_in, f32[4,32,128]{2,1,0:T(8,128)S(1)} %get-tuple-element.40.two_in, ...), custom_call_target="tpu_custom_call", output_to_operand_aliasing={{0}: (5, {})} | custom-call | tf_op jit(solution)/shard_map/edge_first/pallas_call | solution.py:563
  26.4 0.0 copy-start.1
  26.4 5.5 %all-to-all-start.1 = ((f32[16,8,128]{2,1,0:T(8,128)}), f32[16,8,128]{2,1,0:T(8,128)S(1)}, u32[]{:S(2)}, u32[]{:S(2)}) async-start(f32[16,8,128]{2,1,0:T(8,128)} %get-tuple-element.47), calls=%async_computation.1 | async-start | bytes 131072 | tf_op jit(solution)/shard_map/all_to_all | solution.py:656
  31.9 0.0 copy-done.1
  31.9 0.7 %collective-permute-start.4 = (f32[4,32,128]{2,1,0:T(8,128)S(1)}, f32[4,32,128]{2,1,0:T(8,128)S(1)}, u32[]{:S(2)}, u32[]{:S(2)}) collective-permute-start(f32[4,32,128]{2,1,0:T(8,128)S(1)} %copy-done.1), channel_id=1, source_target_pairs={{1,2},{3,4},{5,6},{7,8},{9,10},{11,12},{13,14},{2,1},{4,3},{6,5},{... | collective-permute-start | bytes 196616 | tf_op jit(solution)/shard_map/ppermute | solution.py:655
  32.6 0.0 collective-permute-done.4.far_p_ref
  32.6 4.4 %all-to-all-done.1.gathered_ref = f32[16,8,128]{2,1,0:T(8,128)S(1)} async-done(((f32[16,8,128]{2,1,0:T(8,128)}), f32[16,8,128]{2,1,0:T(8,128)S(1)}, u32[]{:S(2)}, u32[]{:S(2)}) %all-to-all-start.1) | async-done | bytes 65568 | tf_op jit(solution)/shard_map/all_to_all | solution.py:656
  37.0 3.0 %iteration_last.1 = (f32[16,32,128]{2,1,0:T(8,128)}, f32[16,32,128]{2,1,0:T(8,128)}) custom-call(bf16[8,16,32,128]{3,2,1,0:T(8,128)(2,1)} %basis_hbm.5, f32[16,8,128]{2,1,0:T(8,128)S(1)} %all-to-all-done.1.gathered_ref, f32[64,256]{1,0:T(8,128)S(1)} %get-tuple-element.28.inverse_ref, bf16[54,32,128]{2,1,0:T(8,128)(2,1)S(1)} %collective-permute-done.1.near_ref, ...), custom_call_target="tpu_custom_call" | custom-call | tf_op jit(solution)/shard_map/iteration_last/pallas_call | solution.py:563
Async XLA Ops:
  3.3 8.0 %copy-start = (bf16[54,32,128]{2,1,0:T(8,128)(2,1)S(1)}, bf16[54,32,128]{2,1,0:T(8,128)(2,1)}, u32[]{:S(2)}) copy-start(bf16[54,32,128]{2,1,0:T(8,128)(2,1)} %get-tuple-element.44) | copy-start | bytes 1327108
  3.3 15.4 %all-to-all-start = ((f32[8,56,128]{2,1,0:T(8,128)}), f32[8,56,128]{2,1,0:T(8,128)S(1)}, u32[]{:S(2)}, u32[]{:S(2)}) async-start(f32[8,56,128]{2,1,0:T(8,128)} %get-tuple-element.27), calls=%async_computation | async-start | bytes 458752 | tf_op jit(solution)/shard_map/all_to_all | solution.py:613
  11.3 7.4 %collective-permute-start.1 = (bf16[54,32,128]{2,1,0:T(8,128)(2,1)}, bf16[54,32,128]{2,1,0:T(8,128)(2,1)S(1)}, u32[]{:S(2)}, u32[]{:S(2)}) collective-permute-start(bf16[54,32,128]{2,1,0:T(8,128)(2,1)} %get-tuple-element.29), channel_id=1, source_target_pairs={{0,1},{1,0},{2,3},{3,2},{4,5},{5,4},{6,7},{7,6},{8,9},{9,8},{10,11... | collective-permute-start | bytes 1327112 | tf_op jit(solution)/shard_map/ppermute | solution.py:614
  11.3 12.2 %collective-permute-start.2 = (bf16[54,32,128]{2,1,0:T(8,128)(2,1)S(1)}, bf16[54,32,128]{2,1,0:T(8,128)(2,1)S(1)}, u32[]{:S(2)}, u32[]{:S(2)}) collective-permute-start(bf16[54,32,128]{2,1,0:T(8,128)(2,1)S(1)} %copy-done), channel_id=1, source_target_pairs={{1,2},{3,4},{5,6},{7,8},{9,10},{11,12},{13,14},{2,1},{4,3},{6,5},{... | collective-permute-start | bytes 1327112 | tf_op jit(solution)/shard_map/ppermute | solution.py:609
  18.7 1.5 %collective-permute-start = (f32[8,56,128]{2,1,0:T(8,128)S(1)}, f32[8,56,128]{2,1,0:T(8,128)S(1)}, u32[]{:S(2)}, u32[]{:S(2)}) collective-permute-start(f32[8,56,128]{2,1,0:T(8,128)S(1)} %all-to-all-done.half_ref), channel_id=1, source_target_pairs={{0,1},{1,0},{2,3},{3,2},{4,5},{5,4},{6,7},{7,6},{8,9},{9,8},{10,11... | collective-permute-start | bytes 688136 | tf_op jit(solution)/shard_map/ppermute | solution.py:615
  23.4 1.5 %collective-permute-start.3 = (f32[4,32,128]{2,1,0:T(8,128)}, f32[4,32,128]{2,1,0:T(8,128)S(1)}, u32[]{:S(2)}, u32[]{:S(2)}) collective-permute-start(f32[4,32,128]{2,1,0:T(8,128)} %get-tuple-element.45), channel_id=1, source_target_pairs={{0,1},{1,0},{2,3},{3,2},{4,5},{5,4},{6,7},{7,6},{8,9},{9,8},{10,11... | collective-permute-start | bytes 196616 | tf_op jit(solution)/shard_map/ppermute | solution.py:637
  26.4 5.5 %copy-start.1 = (f32[4,32,128]{2,1,0:T(8,128)S(1)}, f32[4,32,128]{2,1,0:T(8,128)}, u32[]{:S(2)}) copy-start(f32[4,32,128]{2,1,0:T(8,128)} %get-tuple-element.51) | copy-start | bytes 196612
  26.4 10.6 %all-to-all-start.1 = ((f32[16,8,128]{2,1,0:T(8,128)}), f32[16,8,128]{2,1,0:T(8,128)S(1)}, u32[]{:S(2)}, u32[]{:S(2)}) async-start(f32[16,8,128]{2,1,0:T(8,128)} %get-tuple-element.47), calls=%async_computation.1 | async-start | bytes 131072 | tf_op jit(solution)/shard_map/all_to_all | solution.py:656
  31.9 0.7 %collective-permute-start.4 = (f32[4,32,128]{2,1,0:T(8,128)S(1)}, f32[4,32,128]{2,1,0:T(8,128)S(1)}, u32[]{:S(2)}, u32[]{:S(2)}) collective-permute-start(f32[4,32,128]{2,1,0:T(8,128)S(1)} %copy-done.1), channel_id=1, source_target_pairs={{1,2},{3,4},{5,6},{7,8},{9,10},{11,12},{13,14},{2,1},{4,3},{6,5},{... | collective-permute-start | bytes 196616 | tf_op jit(solution)/shard_map/ppermute | solution.py:655

commit v7 on v6

--- a/solution.py
+++ b/solution.py
@@ -410,7 +410,7 @@
     chips = half_ref.shape[0]
 
     def unpack(chip, carry):
-        first = 2 * jnp.where(chip < 4, jnp.bitwise_xor(chip, 2), chip)
+        first = 2 * jnp.bitwise_xor(chip, 4)
         for ref, device in ((half_ref, first + core), (other_ref, first + 1 - core)):
             at = device * PER
             for r in range(2):
@@ -608,7 +608,7 @@
     )
     far = lax.ppermute(far, "gx", far_pairs)
     ranks = list(range(count // 2))
-    ranks[:4] = ranks[2:4] + ranks[:2]
+    ranks = [rank ^ 4 for rank in ranks]
     chips = [[core + 2 * chip for chip in ranks] for core in range(2)]
     half = lax.all_to_all(packed, "gx", 0, 0, axis_index_groups=chips, tiled=True)
     near = lax.ppermute(near, "gx", near_pairs)

time: 40.6 us -> 40.3 us (level)
  waiting for transfers between devices: 13.9 us -> 12.7 us
  starting transfers between devices: 15 us -> 15.9 us
    all_to_all x1, waiting for transfers between devices: 6.69 us -> 5.48 us  [local(): lax.all_to_all(packed, 'gx', 0, 0, axis_index_groups=chips, tiled=True)]
    all_to_all x1, starting transfers between devices: 5.5 us -> 6.39 us  [local(): lax.all_to_all(packed, 'gx', 0, 0, axis_index_groups=[tile_order(count)],...]
where the time goes in v7:
time: 40.3 us; the launch traced here: 39.7 us
  starting transfers between devices  15.9 us (39%)
  waiting for transfers between devices  12.7 us (32%)
  Pallas kernels  10.3 us (26%)
  between operations  0.71 us (2%)
    pallas_call x4, Pallas kernels, kernel_call(): call(*[pltpu.with_memory_space_constraint(value, space) for space, value...  10.3 us
    all_to_all x1, starting transfers between devices, local(): lax.all_to_all(packed, 'gx', 0, 0, axis_index_groups=chips, tiled=True)  7.99 us
    all_to_all x1, starting transfers between devices, local(): lax.all_to_all(packed, 'gx', 0, 0, axis_index_groups=[tile_order(count)],...  6.39 us
    all_to_all x1, waiting for transfers between devices, local(): lax.all_to_all(packed, 'gx', 0, 0, axis_index_groups=chips, tiled=True)  5.48 us
    all_to_all x1, waiting for transfers between devices, local(): lax.all_to_all(packed, 'gx', 0, 0, axis_index_groups=[tile_order(count)],...  4.4 us
    ppermute x1, waiting for transfers between devices, local(): other = lax.ppermute(half, 'gx', near_pairs)  1.48 us
    ppermute x1, waiting for transfers between devices, local(): near_p = lax.ppermute(send_near, 'gx', near_pairs)  1.32 us
  transfers between devices with their start and end apart: 7, of which 4 were waited for; matrix products, arithmetic and copies ran while one was open for 0% of the time, Pallas kernels for 8%

profile of v7, /device:TPU:0, one launch (start us, length us, event | category | flops | bytes accessed | tf_op | source)
XLA Modules:
  0.0 39.7 jit_solution(6950156612571980403)
XLA Ops:
  0.6 2.7 %restrict_first.1 = (bf16[54,32,128]{2,1,0:T(8,128)(2,1)}, bf16[54,32,128]{2,1,0:T(8,128)(2,1)}, f32[8,56,128]{2,1,0:T(8,128)}, f32[16,32,128]{2,1,0:T(8,128)S(1...) custom-call(s32[256]{0:T(256)} %owned_hbm.1, ...), custom_call_target="tpu_custom_call" | custom-call | tf_op jit(solution)/shard_map/restrict_first/pallas_call | solution.py:563
  3.3 0.0 copy-start
  3.3 8.0 %all-to-all-start = ((f32[8,56,128]{2,1,0:T(8,128)}), f32[8,56,128]{2,1,0:T(8,128)S(1)}, u32[]{:S(2)}, u32[]{:S(2)}) async-start(f32[8,56,128]{2,1,0:T(8,128)} %get-tuple-element.27), calls=%async_computation | async-start | bytes 458752 | tf_op jit(solution)/shard_map/all_to_all | solution.py:613
  11.3 0.0 collective-permute-start.1
  11.3 0.0 copy-done
  11.3 0.7 %collective-permute-start.2 = (bf16[54,32,128]{2,1,0:T(8,128)(2,1)S(1)}, bf16[54,32,128]{2,1,0:T(8,128)(2,1)S(1)}, u32[]{:S(2)}, u32[]{:S(2)}) collective-permute-start(bf16[54,32,128]{2,1,0:T(8,128)(2,1)S(1)} %copy-done), channel_id=1, source_target_pairs={{1,2},{3,4},{5,6},{7,8},{9,10},{11,12},{13,14},{2,1},{4,3},{6,5},{... | collective-permute-start | bytes 1327112 | tf_op jit(solution)/shard_map/ppermute | solution.py:609
  12.0 5.5 %all-to-all-done.half_ref = f32[8,56,128]{2,1,0:T(8,128)S(1)} async-done(((f32[8,56,128]{2,1,0:T(8,128)}), f32[8,56,128]{2,1,0:T(8,128)S(1)}, u32[]{:S(2)}, u32[]{:S(2)}) %all-to-all-start) | async-done | bytes 229408 | tf_op jit(solution)/shard_map/all_to_all | solution.py:613
  17.5 0.0 collective-permute-start
  17.5 0.0 collective-permute-done.1.near_ref
  17.5 1.5 %collective-permute-done.other_ref = f32[8,56,128]{2,1,0:T(8,128)S(1)} collective-permute-done((f32[8,56,128]{2,1,0:T(8,128)S(1)}, f32[8,56,128]{2,1,0:T(8,128)S(1)}, u32[]{:S(2)}, u32[]{:S(2)}) %collective-permute-start) | collective-permute-done | bytes 229408 | tf_op jit(solution)/shard_map/ppermute | solution.py:615
  19.0 3.1 %iteration_first.1 = (f32[16,32,128]{2,1,0:T(8,128)S(1)}, f32[384,256]{1,0:T(8,128)S(1)}, f32[8,768]{1,0:T(8,128)S(1)}, f32[4,32,128]{2,1,0:T(8,128)S(1)}, f32[4...) custom-call(bf16[8,16,32,128]{3,2,1,0:T(8,128)(2,1)} %basis_hbm.5, ...), custom_call_target="tpu_custom_call", output_to_operand_aliasing={{0}: (11, {}), {1}: (12, {})} | custom-call | tf_op jit(solution)/shard_map/iteration_first/pallas_call | solution.py:563
  22.1 0.2 collective-permute-start.3
  22.3 0.0 collective-permute-done.2.far_ref
  22.3 1.3 %collective-permute-done.3.near_p_ref = f32[4,32,128]{2,1,0:T(8,128)S(1)} collective-permute-done((f32[4,32,128]{2,1,0:T(8,128)}, f32[4,32,128]{2,1,0:T(8,128)S(1)}, u32[]{:S(2)}, u32[]{:S(2)}) %collective-permute-start.3) | collective-permute-done | bytes 65568 | tf_op jit(solution)/shard_map/ppermute | solution.py:637
  23.7 1.5 %edge_first.1 = (f32[16,32,128]{2,1,0:T(8,128)S(1)}, f32[4,32,128]{2,1,0:T(8,128)}, f32[16,8,128]{2,1,0:T(8,128)}) custom-call(f32[8,768]{1,0:T(8,128)S(1)} %get-tuple-element.38.spread_ref, f32[4,32,128]{2,1,0:T(8,128)S(1)} %get-tuple-element.39.one_in, f32[4,32,128]{2,1,0:T(8,128)S(1)} %get-tuple-element.40.two_in, ...), custom_call_target="tpu_custom_call", output_to_operand_aliasing={{0}: (5, {})} | custom-call | tf_op jit(solution)/shard_map/edge_first/pallas_call | solution.py:563
  25.2 0.0 copy-start.1
  25.2 6.4 %all-to-all-start.1 = ((f32[16,8,128]{2,1,0:T(8,128)}), f32[16,8,128]{2,1,0:T(8,128)S(1)}, u32[]{:S(2)}, u32[]{:S(2)}) async-start(f32[16,8,128]{2,1,0:T(8,128)} %get-tuple-element.47), calls=%async_computation.1 | async-start | bytes 131072 | tf_op jit(solution)/shard_map/all_to_all | solution.py:656
  31.6 0.0 copy-done.1
  31.6 0.7 %collective-permute-start.4 = (f32[4,32,128]{2,1,0:T(8,128)S(1)}, f32[4,32,128]{2,1,0:T(8,128)S(1)}, u32[]{:S(2)}, u32[]{:S(2)}) collective-permute-start(f32[4,32,128]{2,1,0:T(8,128)S(1)} %copy-done.1), channel_id=1, source_target_pairs={{1,2},{3,4},{5,6},{7,8},{9,10},{11,12},{13,14},{2,1},{4,3},{6,5},{... | collective-permute-start | bytes 196616 | tf_op jit(solution)/shard_map/ppermute | solution.py:655
  32.2 0.0 collective-permute-done.4.far_p_ref
  32.3 4.4 %all-to-all-done.1.gathered_ref = f32[16,8,128]{2,1,0:T(8,128)S(1)} async-done(((f32[16,8,128]{2,1,0:T(8,128)}), f32[16,8,128]{2,1,0:T(8,128)S(1)}, u32[]{:S(2)}, u32[]{:S(2)}) %all-to-all-start.1) | async-done | bytes 65568 | tf_op jit(solution)/shard_map/all_to_all | solution.py:656
  36.7 3.0 %iteration_last.1 = (f32[16,32,128]{2,1,0:T(8,128)}, f32[16,32,128]{2,1,0:T(8,128)}) custom-call(bf16[8,16,32,128]{3,2,1,0:T(8,128)(2,1)} %basis_hbm.5, f32[16,8,128]{2,1,0:T(8,128)S(1)} %all-to-all-done.1.gathered_ref, f32[64,256]{1,0:T(8,128)S(1)} %get-tuple-element.28.inverse_ref, bf16[54,32,128]{2,1,0:T(8,128)(2,1)S(1)} %collective-permute-done.1.near_ref, ...), custom_call_target="tpu_custom_call" | custom-call | tf_op jit(solution)/shard_map/iteration_last/pallas_call | solution.py:563
Async XLA Ops:
  3.3 8.0 %copy-start = (bf16[54,32,128]{2,1,0:T(8,128)(2,1)S(1)}, bf16[54,32,128]{2,1,0:T(8,128)(2,1)}, u32[]{:S(2)}) copy-start(bf16[54,32,128]{2,1,0:T(8,128)(2,1)} %get-tuple-element.44) | copy-start | bytes 1327108
  3.3 14.2 %all-to-all-start = ((f32[8,56,128]{2,1,0:T(8,128)}), f32[8,56,128]{2,1,0:T(8,128)S(1)}, u32[]{:S(2)}, u32[]{:S(2)}) async-start(f32[8,56,128]{2,1,0:T(8,128)} %get-tuple-element.27), calls=%async_computation | async-start | bytes 458752 | tf_op jit(solution)/shard_map/all_to_all | solution.py:613
  11.3 6.2 %collective-permute-start.1 = (bf16[54,32,128]{2,1,0:T(8,128)(2,1)}, bf16[54,32,128]{2,1,0:T(8,128)(2,1)S(1)}, u32[]{:S(2)}, u32[]{:S(2)}) collective-permute-start(bf16[54,32,128]{2,1,0:T(8,128)(2,1)} %get-tuple-element.29), channel_id=1, source_target_pairs={{0,1},{1,0},{2,3},{3,2},{4,5},{5,4},{6,7},{7,6},{8,9},{9,8},{10,11... | collective-permute-start | bytes 1327112 | tf_op jit(solution)/shard_map/ppermute | solution.py:614
  11.3 11.0 %collective-permute-start.2 = (bf16[54,32,128]{2,1,0:T(8,128)(2,1)S(1)}, bf16[54,32,128]{2,1,0:T(8,128)(2,1)S(1)}, u32[]{:S(2)}, u32[]{:S(2)}) collective-permute-start(bf16[54,32,128]{2,1,0:T(8,128)(2,1)S(1)} %copy-done), channel_id=1, source_target_pairs={{1,2},{3,4},{5,6},{7,8},{9,10},{11,12},{13,14},{2,1},{4,3},{6,5},{... | collective-permute-start | bytes 1327112 | tf_op jit(solution)/shard_map/ppermute | solution.py:609
  17.5 1.5 %collective-permute-start = (f32[8,56,128]{2,1,0:T(8,128)S(1)}, f32[8,56,128]{2,1,0:T(8,128)S(1)}, u32[]{:S(2)}, u32[]{:S(2)}) collective-permute-start(f32[8,56,128]{2,1,0:T(8,128)S(1)} %all-to-all-done.half_ref), channel_id=1, source_target_pairs={{0,1},{1,0},{2,3},{3,2},{4,5},{5,4},{6,7},{7,6},{8,9},{9,8},{10,11... | collective-permute-start | bytes 688136 | tf_op jit(solution)/shard_map/ppermute | solution.py:615
  22.1 1.5 %collective-permute-start.3 = (f32[4,32,128]{2,1,0:T(8,128)}, f32[4,32,128]{2,1,0:T(8,128)S(1)}, u32[]{:S(2)}, u32[]{:S(2)}) collective-permute-start(f32[4,32,128]{2,1,0:T(8,128)} %get-tuple-element.45), channel_id=1, source_target_pairs={{0,1},{1,0},{2,3},{3,2},{4,5},{5,4},{6,7},{7,6},{8,9},{9,8},{10,11... | collective-permute-start | bytes 196616 | tf_op jit(solution)/shard_map/ppermute | solution.py:637
  25.2 6.4 %copy-start.1 = (f32[4,32,128]{2,1,0:T(8,128)S(1)}, f32[4,32,128]{2,1,0:T(8,128)}, u32[]{:S(2)}) copy-start(f32[4,32,128]{2,1,0:T(8,128)} %get-tuple-element.51) | copy-start | bytes 196612
  25.2 11.5 %all-to-all-start.1 = ((f32[16,8,128]{2,1,0:T(8,128)}), f32[16,8,128]{2,1,0:T(8,128)S(1)}, u32[]{:S(2)}, u32[]{:S(2)}) async-start(f32[16,8,128]{2,1,0:T(8,128)} %get-tuple-element.47), calls=%async_computation.1 | async-start | bytes 131072 | tf_op jit(solution)/shard_map/all_to_all | solution.py:656
  31.6 0.7 %collective-permute-start.4 = (f32[4,32,128]{2,1,0:T(8,128)S(1)}, f32[4,32,128]{2,1,0:T(8,128)S(1)}, u32[]{:S(2)}, u32[]{:S(2)}) collective-permute-start(f32[4,32,128]{2,1,0:T(8,128)S(1)} %copy-done.1), channel_id=1, source_target_pairs={{1,2},{3,4},{5,6},{7,8},{9,10},{11,12},{13,14},{2,1},{4,3},{6,5},{... | collective-permute-start | bytes 196616 | tf_op jit(solution)/shard_map/ppermute | solution.py:655

commit v8 on v7

--- a/solution.py
+++ b/solution.py
@@ -69,7 +69,7 @@
 
     if totals is None:
         totals = (jnp.zeros((8, 128), F32),) * (NBF * NYB)
-    return lax.fori_loop(low, high, step, tuple(totals))
+    return lax.fori_loop(low, high, step, tuple(totals), unroll=high - low <= 4)
 
 
 def restricted(totals):

time: 40.3 us -> 40.2 us (level)
  no operation moved by 1% of the time
where the time goes in v8:
time: 40.2 us; the launch traced here: 39.6 us
  starting transfers between devices  15.9 us (40%)
  waiting for transfers between devices  12.7 us (32%)
  Pallas kernels  10.2 us (25%)
  between operations  0.71 us (2%)
    pallas_call x4, Pallas kernels, kernel_call(): call(*[pltpu.with_memory_space_constraint(value, space) for space, value...  10.2 us
    all_to_all x1, starting transfers between devices, local(): lax.all_to_all(packed, 'gx', 0, 0, axis_index_groups=chips, tiled=True)  7.99 us
    all_to_all x1, starting transfers between devices, local(): lax.all_to_all(packed, 'gx', 0, 0, axis_index_groups=[tile_order(count)],...  6.39 us
    all_to_all x1, waiting for transfers between devices, local(): lax.all_to_all(packed, 'gx', 0, 0, axis_index_groups=chips, tiled=True)  5.48 us
    all_to_all x1, waiting for transfers between devices, local(): lax.all_to_all(packed, 'gx', 0, 0, axis_index_groups=[tile_order(count)],...  4.4 us
    ppermute x1, waiting for transfers between devices, local(): other = lax.ppermute(half, 'gx', near_pairs)  1.48 us
    ppermute x1, waiting for transfers between devices, local(): near_p = lax.ppermute(send_near, 'gx', near_pairs)  1.32 us
  transfers between devices with their start and end apart: 7, of which 4 were waited for; matrix products, arithmetic and copies ran while one was open for 0% of the time, Pallas kernels for 8%

profile of v8, /device:TPU:0, one launch (start us, length us, event | category | flops | bytes accessed | tf_op | source)
XLA Modules:
  0.0 39.6 jit_solution(14673546011104320543)
XLA Ops:
  0.6 2.7 %restrict_first.1 = (bf16[54,32,128]{2,1,0:T(8,128)(2,1)}, bf16[54,32,128]{2,1,0:T(8,128)(2,1)}, f32[8,56,128]{2,1,0:T(8,128)}, f32[16,32,128]{2,1,0:T(8,128)S(1...) custom-call(s32[256]{0:T(256)} %owned_hbm.1, ...), custom_call_target="tpu_custom_call" | custom-call | tf_op jit(solution)/shard_map/restrict_first/pallas_call | solution.py:563
  3.3 0.0 copy-start
  3.3 8.0 %all-to-all-start = ((f32[8,56,128]{2,1,0:T(8,128)}), f32[8,56,128]{2,1,0:T(8,128)S(1)}, u32[]{:S(2)}, u32[]{:S(2)}) async-start(f32[8,56,128]{2,1,0:T(8,128)} %get-tuple-element.27), calls=%async_computation | async-start | bytes 458752 | tf_op jit(solution)/shard_map/all_to_all | solution.py:613
  11.3 0.0 collective-permute-start.1
  11.3 0.0 copy-done
  11.3 0.7 %collective-permute-start.2 = (bf16[54,32,128]{2,1,0:T(8,128)(2,1)S(1)}, bf16[54,32,128]{2,1,0:T(8,128)(2,1)S(1)}, u32[]{:S(2)}, u32[]{:S(2)}) collective-permute-start(bf16[54,32,128]{2,1,0:T(8,128)(2,1)S(1)} %copy-done), channel_id=1, source_target_pairs={{1,2},{3,4},{5,6},{7,8},{9,10},{11,12},{13,14},{2,1},{4,3},{6,5},{... | collective-permute-start | bytes 1327112 | tf_op jit(solution)/shard_map/ppermute | solution.py:609
  12.0 5.5 %all-to-all-done.half_ref = f32[8,56,128]{2,1,0:T(8,128)S(1)} async-done(((f32[8,56,128]{2,1,0:T(8,128)}), f32[8,56,128]{2,1,0:T(8,128)S(1)}, u32[]{:S(2)}, u32[]{:S(2)}) %all-to-all-start) | async-done | bytes 229408 | tf_op jit(solution)/shard_map/all_to_all | solution.py:613
  17.5 0.0 collective-permute-start
  17.5 0.0 collective-permute-done.1.near_ref
  17.5 1.5 %collective-permute-done.other_ref = f32[8,56,128]{2,1,0:T(8,128)S(1)} collective-permute-done((f32[8,56,128]{2,1,0:T(8,128)S(1)}, f32[8,56,128]{2,1,0:T(8,128)S(1)}, u32[]{:S(2)}, u32[]{:S(2)}) %collective-permute-start) | collective-permute-done | bytes 229408 | tf_op jit(solution)/shard_map/ppermute | solution.py:615
  19.0 3.1 %iteration_first.1 = (f32[16,32,128]{2,1,0:T(8,128)S(1)}, f32[384,256]{1,0:T(8,128)S(1)}, f32[8,768]{1,0:T(8,128)S(1)}, f32[4,32,128]{2,1,0:T(8,128)S(1)}, f32[4...) custom-call(bf16[8,16,32,128]{3,2,1,0:T(8,128)(2,1)} %basis_hbm.5, ...), custom_call_target="tpu_custom_call", output_to_operand_aliasing={{0}: (11, {}), {1}: (12, {})} | custom-call | tf_op jit(solution)/shard_map/iteration_first/pallas_call | solution.py:563
  22.1 0.2 collective-permute-start.3
  22.3 0.0 collective-permute-done.2.far_ref
  22.3 1.3 %collective-permute-done.3.near_p_ref = f32[4,32,128]{2,1,0:T(8,128)S(1)} collective-permute-done((f32[4,32,128]{2,1,0:T(8,128)}, f32[4,32,128]{2,1,0:T(8,128)S(1)}, u32[]{:S(2)}, u32[]{:S(2)}) %collective-permute-start.3) | collective-permute-done | bytes 65568 | tf_op jit(solution)/shard_map/ppermute | solution.py:637
  23.6 1.4 %edge_first.1 = (f32[16,32,128]{2,1,0:T(8,128)S(1)}, f32[4,32,128]{2,1,0:T(8,128)}, f32[16,8,128]{2,1,0:T(8,128)}) custom-call(f32[8,768]{1,0:T(8,128)S(1)} %get-tuple-element.38.spread_ref, f32[4,32,128]{2,1,0:T(8,128)S(1)} %get-tuple-element.39.one_in, f32[4,32,128]{2,1,0:T(8,128)S(1)} %get-tuple-element.40.two_in, ...), custom_call_target="tpu_custom_call", output_to_operand_aliasing={{0}: (5, {})} | custom-call | tf_op jit(solution)/shard_map/edge_first/pallas_call | solution.py:563
  25.1 0.0 copy-start.1
  25.1 6.4 %all-to-all-start.1 = ((f32[16,8,128]{2,1,0:T(8,128)}), f32[16,8,128]{2,1,0:T(8,128)S(1)}, u32[]{:S(2)}, u32[]{:S(2)}) async-start(f32[16,8,128]{2,1,0:T(8,128)} %get-tuple-element.47), calls=%async_computation.1 | async-start | bytes 131072 | tf_op jit(solution)/shard_map/all_to_all | solution.py:656
  31.5 0.0 copy-done.1
  31.5 0.7 %collective-permute-start.4 = (f32[4,32,128]{2,1,0:T(8,128)S(1)}, f32[4,32,128]{2,1,0:T(8,128)S(1)}, u32[]{:S(2)}, u32[]{:S(2)}) collective-permute-start(f32[4,32,128]{2,1,0:T(8,128)S(1)} %copy-done.1), channel_id=1, source_target_pairs={{1,2},{3,4},{5,6},{7,8},{9,10},{11,12},{13,14},{2,1},{4,3},{6,5},{... | collective-permute-start | bytes 196616 | tf_op jit(solution)/shard_map/ppermute | solution.py:655
  32.2 0.0 collective-permute-done.4.far_p_ref
  32.2 4.4 %all-to-all-done.1.gathered_ref = f32[16,8,128]{2,1,0:T(8,128)S(1)} async-done(((f32[16,8,128]{2,1,0:T(8,128)}), f32[16,8,128]{2,1,0:T(8,128)S(1)}, u32[]{:S(2)}, u32[]{:S(2)}) %all-to-all-start.1) | async-done | bytes 65568 | tf_op jit(solution)/shard_map/all_to_all | solution.py:656
  36.6 3.0 %iteration_last.1 = (f32[16,32,128]{2,1,0:T(8,128)}, f32[16,32,128]{2,1,0:T(8,128)}) custom-call(bf16[8,16,32,128]{3,2,1,0:T(8,128)(2,1)} %basis_hbm.5, f32[16,8,128]{2,1,0:T(8,128)S(1)} %all-to-all-done.1.gathered_ref, f32[64,256]{1,0:T(8,128)S(1)} %get-tuple-element.28.inverse_ref, bf16[54,32,128]{2,1,0:T(8,128)(2,1)S(1)} %collective-permute-done.1.near_ref, ...), custom_call_target="tpu_custom_call" | custom-call | tf_op jit(solution)/shard_map/iteration_last/pallas_call | solution.py:563
Async XLA Ops:
  3.3 8.0 %copy-start = (bf16[54,32,128]{2,1,0:T(8,128)(2,1)S(1)}, bf16[54,32,128]{2,1,0:T(8,128)(2,1)}, u32[]{:S(2)}) copy-start(bf16[54,32,128]{2,1,0:T(8,128)(2,1)} %get-tuple-element.44) | copy-start | bytes 1327108
  3.3 14.2 %all-to-all-start = ((f32[8,56,128]{2,1,0:T(8,128)}), f32[8,56,128]{2,1,0:T(8,128)S(1)}, u32[]{:S(2)}, u32[]{:S(2)}) async-start(f32[8,56,128]{2,1,0:T(8,128)} %get-tuple-element.27), calls=%async_computation | async-start | bytes 458752 | tf_op jit(solution)/shard_map/all_to_all | solution.py:613
  11.3 6.2 %collective-permute-start.1 = (bf16[54,32,128]{2,1,0:T(8,128)(2,1)}, bf16[54,32,128]{2,1,0:T(8,128)(2,1)S(1)}, u32[]{:S(2)}, u32[]{:S(2)}) collective-permute-start(bf16[54,32,128]{2,1,0:T(8,128)(2,1)} %get-tuple-element.29), channel_id=1, source_target_pairs={{0,1},{1,0},{2,3},{3,2},{4,5},{5,4},{6,7},{7,6},{8,9},{9,8},{10,11... | collective-permute-start | bytes 1327112 | tf_op jit(solution)/shard_map/ppermute | solution.py:614
  11.3 11.0 %collective-permute-start.2 = (bf16[54,32,128]{2,1,0:T(8,128)(2,1)S(1)}, bf16[54,32,128]{2,1,0:T(8,128)(2,1)S(1)}, u32[]{:S(2)}, u32[]{:S(2)}) collective-permute-start(bf16[54,32,128]{2,1,0:T(8,128)(2,1)S(1)} %copy-done), channel_id=1, source_target_pairs={{1,2},{3,4},{5,6},{7,8},{9,10},{11,12},{13,14},{2,1},{4,3},{6,5},{... | collective-permute-start | bytes 1327112 | tf_op jit(solution)/shard_map/ppermute | solution.py:609
  17.5 1.5 %collective-permute-start = (f32[8,56,128]{2,1,0:T(8,128)S(1)}, f32[8,56,128]{2,1,0:T(8,128)S(1)}, u32[]{:S(2)}, u32[]{:S(2)}) collective-permute-start(f32[8,56,128]{2,1,0:T(8,128)S(1)} %all-to-all-done.half_ref), channel_id=1, source_target_pairs={{0,1},{1,0},{2,3},{3,2},{4,5},{5,4},{6,7},{7,6},{8,9},{9,8},{10,11... | collective-permute-start | bytes 688136 | tf_op jit(solution)/shard_map/ppermute | solution.py:615
  22.1 1.5 %collective-permute-start.3 = (f32[4,32,128]{2,1,0:T(8,128)}, f32[4,32,128]{2,1,0:T(8,128)S(1)}, u32[]{:S(2)}, u32[]{:S(2)}) collective-permute-start(f32[4,32,128]{2,1,0:T(8,128)} %get-tuple-element.45), channel_id=1, source_target_pairs={{0,1},{1,0},{2,3},{3,2},{4,5},{5,4},{6,7},{7,6},{8,9},{9,8},{10,11... | collective-permute-start | bytes 196616 | tf_op jit(solution)/shard_map/ppermute | solution.py:637
  25.1 6.4 %copy-start.1 = (f32[4,32,128]{2,1,0:T(8,128)S(1)}, f32[4,32,128]{2,1,0:T(8,128)}, u32[]{:S(2)}) copy-start(f32[4,32,128]{2,1,0:T(8,128)} %get-tuple-element.51) | copy-start | bytes 196612
  25.1 11.5 %all-to-all-start.1 = ((f32[16,8,128]{2,1,0:T(8,128)}), f32[16,8,128]{2,1,0:T(8,128)S(1)}, u32[]{:S(2)}, u32[]{:S(2)}) async-start(f32[16,8,128]{2,1,0:T(8,128)} %get-tuple-element.47), calls=%async_computation.1 | async-start | bytes 131072 | tf_op jit(solution)/shard_map/all_to_all | solution.py:656
  31.5 0.7 %collective-permute-start.4 = (f32[4,32,128]{2,1,0:T(8,128)S(1)}, f32[4,32,128]{2,1,0:T(8,128)S(1)}, u32[]{:S(2)}, u32[]{:S(2)}) collective-permute-start(f32[4,32,128]{2,1,0:T(8,128)S(1)} %copy-done.1), channel_id=1, source_target_pairs={{1,2},{3,4},{5,6},{7,8},{9,10},{11,12},{13,14},{2,1},{4,3},{6,5},{... | collective-permute-start | bytes 196616 | tf_op jit(solution)/shard_map/ppermute | solution.py:655
